TPU v7x, 32 devices: a whole 2x2x4 slice. The times are simulated.
32 devices in a mesh: rows: 8 (over y, x, core), seq: 4 (over z).
Axes of the slice: x: 2, y: 2, z: 4, core: 2. Of those that a mesh axis runs over, the one named last changes fastest.
Arguments:
- tokens: bfloat16 [16, 2048, 768], P('rows', 'seq'), may hold values from -6 to 6
- segment_ids: int32 [16, 2048], P('rows'), may hold values from 0 to 3, as said below
- cotangent: bfloat16 [16, 2048, 768], P('rows', 'seq'), may hold values from -6 to 6
- query_key_value: bfloat16 [768, 2304], replicated, may hold values from -0.21875 to 0.21875
- out_weight: bfloat16 [768, 768], replicated, may hold values from -0.21875 to 0.21875
- up_weight: bfloat16 [768, 3072], replicated, may hold values from -0.21875 to 0.21875
- down_weight: bfloat16 [3072, 768], replicated, may hold values from -0.109375 to 0.109375
- attend_gain: float32 [768], replicated, may hold values from 0.25 to 1.75
- inner_gain: float32 [768], replicated, may hold values from 0.25 to 1.75
- feed_gain: float32 [768], replicated, may hold values from 0.25 to 1.75
- hidden_gain: float32 [3072], replicated, may hold values from 0.25 to 1.75
Outputs:
- output: bfloat16 [16, 2048, 768], P('rows', 'seq')
- tokens_grad: bfloat16 [16, 2048, 768], P('rows', 'seq')
- query_key_value_grad: float32 [768, 2304], replicated
- out_weight_grad: float32 [768, 768], replicated
- up_weight_grad: float32 [768, 3072], replicated
- down_weight_grad: float32 [3072, 768], replicated
- attend_gain_grad: float32 [768], replicated
- inner_gain_grad: float32 [768], replicated
- feed_gain_grad: float32 [768], replicated
- hidden_gain_grad: float32 [3072], replicated
Inputs may be any that keep to these rules, and one draw needn't show every extreme that they name: `segment_ids`: within each row the ids are 0 everywhere (one document of 2048 tokens) or 0, 1, 2, 3 on four equal runs of 512 tokens; of the 2 rows at one index of rows at least one is of each kind.
All inputs are finite; a program needn't handle non-finite values.
Results may differ from a plain program's by a relative error of at most 0.02.
Values may be sent and summed in bfloat16 or wider, within the bound.
A program may use at most 256 MiB of HBM per device.

v0:
```python
import math

import jax
import jax.numpy as jnp
from jax import lax
from jax.sharding import PartitionSpec as P

D = 768
HEADS = 12
HEAD_DIM = 64


EPSILON = 1e-05
MASKED = -1e30


def passed_along(value, axis, steps):
    count = lax.axis_size(axis)
    initial, last = (max(0, -steps), min(count, count - steps))
    return lax.ppermute(value, axis, [(source, source + steps) for source in range(initial, last)])


def from_behind(value, axis, steps):
    count = lax.axis_size(axis)
    pairs = [(source, (source + steps) % count) for source in range(count)]
    return lax.ppermute(value, axis, pairs)


def layer_norm(values, gain):
    average = jnp.mean(values, axis=-1, keepdims=True)
    centred = values - average
    inverse = lax.rsqrt(jnp.mean(centred * centred, axis=-1, keepdims=True) + EPSILON)
    normed = centred * inverse
    return (normed * gain, normed, inverse)


def norm_back(upstream, normed, inverse, gain):
    scaled = upstream * gain
    spread = (
        scaled
        - jnp.mean(scaled, axis=-1, keepdims=True)
        - normed * jnp.mean(scaled * normed, axis=-1, keepdims=True)
    )
    return (spread * inverse, jnp.sum(upstream * normed, axis=0))


def gelu_exact(values):
    return jax.nn.gelu(values, approximate=False)


def matmul(left, right):
    return jnp.dot(left, right, preferred_element_type=jnp.float32)


def left_t(left, right):
    return lax.dot_general(
        left, right, (((0,), (0,)), ((), ())), preferred_element_type=jnp.float32
    )


def right_t(left, right):
    return lax.dot_general(
        left, right, (((1,), (1,)), ((), ())), preferred_element_type=jnp.float32
    )


def split_heads(values):
    return values.reshape(values.shape[0], values.shape[1], HEADS, HEAD_DIM)


def allowed_pairs(query_pos, query_seg, key_pos, key_seg):
    causal = key_pos[None, None, None, :] <= query_pos[None, None, :, None]
    same_doc = key_seg[:, None, None, :] == query_seg[:, None, :, None]
    return causal & same_doc


def scores(queries, key_rows):
    return jnp.einsum(
        "rqhd,rkhd->rhqk",
        split_heads(queries),
        split_heads(key_rows),
        preferred_element_type=jnp.float32,
    ) * HEAD_DIM ** (-0.5)


def fold_keys(carry, piece, queries, query_pos, query_seg, segment_ids):
    key_rows, value_rows = piece
    row_count = key_rows.shape[0]
    key_count = key_rows.shape[1]
    block_width = math.gcd(key_count, queries.shape[1])
    block_count = key_count // block_width
    key_blocks = key_rows.reshape(row_count, block_count, block_width, D).transpose(1, 0, 2, 3)
    value_blocks = value_rows.reshape(row_count, block_count, block_width, D).transpose(1, 0, 2, 3)

    def one_block(state, block_item):
        accum, running, softmax_total = state
        key_block, value_block, offset = block_item
        key_start = offset * block_width
        key_pos = key_start + jnp.arange(block_width, dtype=jnp.int32)
        key_seg = lax.dynamic_slice_in_dim(segment_ids, key_start, block_width, 1)
        allowed = allowed_pairs(query_pos, query_seg, key_pos, key_seg)
        logits = jnp.where(allowed, scores(queries, key_block), MASKED)
        new_peak = jnp.maximum(running, jnp.max(logits, axis=-1))
        weights = jnp.where(allowed, jnp.exp(logits - new_peak[..., None]), 0.0)
        factor = jnp.exp(running - new_peak)
        softmax_total = softmax_total * factor + jnp.sum(weights, axis=-1)
        accum = accum * factor[..., None] + jnp.einsum(
            "rhqk,rkhd->rhqd",
            weights.astype(jnp.bfloat16),
            split_heads(value_block),
            preferred_element_type=jnp.float32,
        )
        return ((accum, new_peak, softmax_total), None)

    carry, unused = lax.scan(
        one_block, carry, (key_blocks, value_blocks, jnp.arange(block_count, dtype=jnp.int32))
    )
    return carry


def back_block(queries, grad_rows, log_total, delta, key_rows, value_rows, allowed):
    logits = jnp.where(allowed, scores(queries, key_rows), MASKED)
    probs = jnp.where(allowed, jnp.exp(logits - log_total[..., None]), 0.0)
    dprobs = jnp.einsum(
        "rqhd,rkhd->rhqk",
        split_heads(grad_rows),
        split_heads(value_rows),
        preferred_element_type=jnp.float32,
    )
    dlogits = (probs * (dprobs - delta[..., None])).astype(jnp.bfloat16)
    factor = HEAD_DIM ** (-0.5)
    query_part = (
        jnp.einsum(
            "rhqk,rkhd->rqhd", dlogits, split_heads(key_rows), preferred_element_type=jnp.float32
        )
        * factor
    )
    key_part = (
        jnp.einsum(
            "rhqk,rqhd->rkhd", dlogits, split_heads(queries), preferred_element_type=jnp.float32
        )
        * factor
    )
    value_part = jnp.einsum(
        "rhqk,rqhd->rkhd",
        probs.astype(jnp.bfloat16),
        split_heads(grad_rows),
        preferred_element_type=jnp.float32,
    )
    return (
        query_part.reshape(queries.shape),
        key_part.reshape(key_rows.shape),
        value_part.reshape(value_rows.shape),
    )


def per_device(
    tokens,
    segment_ids,
    cotangent,
    query_key_value,
    out_weight,
    up_weight,
    down_weight,
    attend_gain,
    inner_gain,
    feed_gain,
    hidden_gain,
):
    row_count = tokens.shape[0]
    width_q = tokens.shape[1]
    model_width = tokens.shape[2]
    token_count = row_count * width_q
    seq_index = lax.axis_index("seq")
    seq_size = lax.axis_size("seq")
    local_pos = seq_index * width_q + jnp.arange(width_q, dtype=jnp.int32)
    local_seg = lax.dynamic_slice_in_dim(segment_ids, seq_index * width_q, width_q, 1)
    residual = tokens.reshape(token_count, model_width).astype(jnp.float32)
    attend_out, attend_normed, attend_inverse = layer_norm(residual, attend_gain)
    attend_low = attend_out.astype(jnp.bfloat16)
    projected = matmul(attend_low, query_key_value).astype(jnp.bfloat16)
    queries = projected[:, :model_width].reshape(row_count, width_q, model_width)
    key_rows = projected[:, model_width : 2 * model_width].reshape(row_count, width_q, model_width)
    value_rows = projected[:, 2 * model_width :].reshape(row_count, width_q, model_width)
    start_state = (
        jnp.zeros((row_count, HEADS, width_q, HEAD_DIM), jnp.float32),
        jnp.full((row_count, HEADS, width_q), MASKED, jnp.float32),
        jnp.zeros((row_count, HEADS, width_q), jnp.float32),
    )
    accum, running, softmax_total = fold_keys(
        start_state,
        (
            lax.all_gather(key_rows, "seq", axis=1, tiled=True),
            lax.all_gather(value_rows, "seq", axis=1, tiled=True),
        ),
        queries,
        local_pos,
        local_seg,
        segment_ids,
    )
    log_total = running + jnp.log(softmax_total)
    attended = (accum / softmax_total[..., None]).transpose(0, 2, 1, 3)
    attended_flat = attended.reshape(token_count, model_width)
    inner_out, inner_normed, inner_inverse = layer_norm(attended_flat, inner_gain)
    inner_low = inner_out.astype(jnp.bfloat16)
    state = residual + matmul(inner_low, out_weight)
    feed_out, feed_normed, feed_inverse = layer_norm(state, feed_gain)
    feed_low = feed_out.astype(jnp.bfloat16)
    pre_act = matmul(feed_low, up_weight)
    hidden, gelu_back = jax.vjp(gelu_exact, pre_act)
    hidden_out, hidden_normed, hidden_inverse = layer_norm(hidden, hidden_gain)
    hidden_low = hidden_out.astype(jnp.bfloat16)
    result = state + matmul(hidden_low, down_weight)
    output = result.astype(jnp.bfloat16).reshape(tokens.shape)
    upstream_low = cotangent.reshape(token_count, model_width)
    upstream = upstream_low.astype(jnp.float32)
    down_term = left_t(hidden_low, upstream_low)
    hidden_grad, hidden_gain_term = norm_back(
        right_t(upstream_low, down_weight), hidden_normed, hidden_inverse, hidden_gain
    )
    pre_grad = gelu_back(hidden_grad)[0]
    pre_low = pre_grad.astype(jnp.bfloat16)
    up_term = left_t(feed_low, pre_low)
    feed_grad, feed_gain_term = norm_back(
        right_t(pre_low, up_weight), feed_normed, feed_inverse, feed_gain
    )
    state_grad = upstream + feed_grad
    state_low = state_grad.astype(jnp.bfloat16)
    out_term = left_t(inner_low, state_low)
    inner_grad, inner_gain_term = norm_back(
        right_t(state_low, out_weight), inner_normed, inner_inverse, inner_gain
    )
    attend_grad_low = inner_grad.astype(jnp.bfloat16).reshape(row_count, width_q, model_width)
    delta = jnp.sum(split_heads(attend_grad_low).astype(jnp.float32) * attended, axis=-1).transpose(
        0, 2, 1
    )
    zero_rows = jnp.zeros((row_count, width_q, model_width), jnp.float32)

    def key_step(step_count, cycle_state):
        moving_keys, moving_values, moving_dkeys, moving_dvalues, query_acc = cycle_state
        source = jnp.remainder(seq_index - step_count, seq_size)
        key_start = source * width_q
        key_pos = key_start + jnp.arange(width_q, dtype=jnp.int32)
        key_seg = lax.dynamic_slice_in_dim(segment_ids, key_start, width_q, 1)
        allowed = allowed_pairs(local_pos, local_seg, key_pos, key_seg)
        query_part, key_part, value_part = back_block(
            queries, attend_grad_low, log_total, delta, moving_keys, moving_values, allowed
        )
        moving_keys, moving_values = passed_along((moving_keys, moving_values), "seq", 1)
        moving_dkeys, moving_dvalues = (
            from_behind((moving_dkeys + key_part).astype(jnp.bfloat16), "seq", 1).astype(
                jnp.float32
            ),
            from_behind((moving_dvalues + value_part).astype(jnp.bfloat16), "seq", 1).astype(
                jnp.float32
            ),
        )
        return (moving_keys, moving_values, moving_dkeys, moving_dvalues, query_acc + query_part)

    cycle_out = lax.fori_loop(
        0, seq_size, key_step, (key_rows, value_rows, zero_rows, zero_rows, zero_rows)
    )
    key_grad, value_grad, query_grad = (cycle_out[2], cycle_out[3], cycle_out[4])
    joined_grad = jnp.concatenate(
        [
            query_grad.astype(jnp.bfloat16),
            key_grad.astype(jnp.bfloat16),
            value_grad.astype(jnp.bfloat16),
        ],
        axis=-1,
    ).reshape(token_count, 3 * model_width)
    qkv_term = left_t(attend_low, joined_grad)
    attend_back, attend_gain_term = norm_back(
        right_t(joined_grad, query_key_value), attend_normed, attend_inverse, attend_gain
    )
    tokens_grad = (state_grad + attend_back).astype(jnp.bfloat16).reshape(tokens.shape)
    all_sectioned = (
        lax.psum_scatter(
            qkv_term.astype(jnp.bfloat16), "rows", scatter_dimension=0, tiled=True
        ).astype(jnp.float32),
        lax.psum_scatter(
            out_term.astype(jnp.bfloat16), "rows", scatter_dimension=0, tiled=True
        ).astype(jnp.float32),
        lax.psum_scatter(
            up_term.astype(jnp.bfloat16), "rows", scatter_dimension=0, tiled=True
        ).astype(jnp.float32),
        lax.psum_scatter(
            down_term.astype(jnp.bfloat16), "rows", scatter_dimension=0, tiled=True
        ).astype(jnp.float32),
    )
    seq_sectioned = (
        lax.psum_scatter(
            all_sectioned[0].astype(jnp.bfloat16), "seq", scatter_dimension=1, tiled=True
        ).astype(jnp.float32),
        lax.psum_scatter(
            all_sectioned[1].astype(jnp.bfloat16), "seq", scatter_dimension=1, tiled=True
        ).astype(jnp.float32),
        lax.psum_scatter(
            all_sectioned[2].astype(jnp.bfloat16), "seq", scatter_dimension=1, tiled=True
        ).astype(jnp.float32),
        lax.psum_scatter(
            all_sectioned[3].astype(jnp.bfloat16), "seq", scatter_dimension=1, tiled=True
        ).astype(jnp.float32),
    )
    seq_whole = (
        lax.all_gather(seq_sectioned[0].astype(jnp.bfloat16), "seq", axis=1, tiled=True).astype(
            jnp.float32
        ),
        lax.all_gather(seq_sectioned[1].astype(jnp.bfloat16), "seq", axis=1, tiled=True).astype(
            jnp.float32
        ),
        lax.all_gather(seq_sectioned[2].astype(jnp.bfloat16), "seq", axis=1, tiled=True).astype(
            jnp.float32
        ),
        lax.all_gather(seq_sectioned[3].astype(jnp.bfloat16), "seq", axis=1, tiled=True).astype(
            jnp.float32
        ),
    )
    qkv_grad, out_grad, up_grad, down_grad = (
        lax.all_gather(seq_whole[0].astype(jnp.bfloat16), "rows", axis=0, tiled=True).astype(
            jnp.float32
        ),
        lax.all_gather(seq_whole[1].astype(jnp.bfloat16), "rows", axis=0, tiled=True).astype(
            jnp.float32
        ),
        lax.all_gather(seq_whole[2].astype(jnp.bfloat16), "rows", axis=0, tiled=True).astype(
            jnp.float32
        ),
        lax.all_gather(seq_whole[3].astype(jnp.bfloat16), "rows", axis=0, tiled=True).astype(
            jnp.float32
        ),
    )
    attend_total, inner_total, feed_total, hidden_total = lax.psum(
        (attend_gain_term, inner_gain_term, feed_gain_term, hidden_gain_term), ("rows", "seq")
    )
    return (
        output,
        tokens_grad,
        qkv_grad,
        out_grad,
        up_grad,
        down_grad,
        attend_total,
        inner_total,
        feed_total,
        hidden_total,
    )


def solution(mesh):
    return jax.shard_map(
        per_device,
        mesh=mesh,
        in_specs=(
            P("rows", "seq", None),
            P("rows", None),
            P("rows", "seq", None),
            P(),
            P(),
            P(),
            P(),
            P(),
            P(),
            P(),
            P(),
        ),
        out_specs=(
            P("rows", "seq", None),
            P("rows", "seq", None),
            P(),
            P(),
            P(),
            P(),
            P(),
            P(),
            P(),
            P(),
        ),
        check_vma=False,
    )
```

profile of v0, /device:TPU:9, one launch (start us, length us, event | category | flops | bytes accessed | tf_op | source)
XLA Modules:
  0.0 1747.7 jit_solution(13753279184504052106)
XLA Ops:
  36.7 96.5 %all-gather.8.cloned.1.call-done = bf16[2,2048,768]{2,1,0:T(8,128)(2,1)} async-done(((bf16[2,512,768]{2,1,0:T(8,128)(2,1)}), bf16[2,2048,768]{2,1,0:T(8,128)(2,1)}) %all-gather.8.cloned.1.call-update) | async-done | bytes 6291472 | tf_op jit(solution)/shard_map/all_gather | solution.py:193
  133.2 115.7 %all-gather.10.cloned.1.call-done = bf16[2,2048,768]{2,1,0:T(8,128)(2,1)} async-done(((bf16[2,512,768]{2,1,0:T(8,128)(2,1)}), bf16[2,2048,768]{2,1,0:T(8,128)(2,1)}) %all-gather.10.cloned.1.call-update) | async-done | bytes 6291472 | tf_op jit(solution)/shard_map/all_gather | solution.py:194
  248.9 222.4 %while.41 = (s32[]{:T(128)}, f32[2,12,512,64]{2,3,1,0:T(8,128)}, f32[2,12,512]{2,1,0:T(8,128)}, f32[2,12,512]{2,1,0:T(8,128)}, s32[4]{0:T(128)S(1)}, /*index=5*/...) while((s32[]{:T(128)}, f32[2,12,512,64]{2,3,1,0:T(8,128)}, ...), condition=%wide.wide.region_5.6_spmd.clone, body=%wide.wide.region_2.5_spmd.clone.sunk | while | flops 1696134144 | bytes 103506304 | solution.py:115
  481.2 35.5 %fusion.68 = (f32[1024]{0:T(1024)S(1)}, f32[1024,3072]{1,0:T(8,128)S(1)}, f32[1024,3072]{1,0:T(8,128)}, f32[1024,3072]{1,0:T(8,128)}) fusion(bf16[768,3072]{1,0:T(8,128)(2,1)S(1)} %bitcast.235, f32[1024,768]{1,0:T(8,128)S(1)} %get-tuple-element.695, f32[768]{0:T(1024)S(1)} %copy-done.45, f32[1024]{0:T(1024)S(1)} %add_rsqrt_fusion.1, ...), kind=kOutput, calls=%fused_computation.149 | convolution fusion | flops 5039455232 | bytes 45628416 | tf_op jit(solution)/shard_map/dot_general | solution.py:52
  535.6 21.1 %add_convert_fusion = (bf16[1024,3072]{1,0:T(8,128)(2,1)S(1)}, bf16[1024,3072]{1,0:T(8,128)(2,1)}) fusion(f32[1024,3072]{1,0:T(8,128)} %get-tuple-element.674, f32[1024,3072]{1,0:T(8,128)} %get-tuple-element.696, f32[1024,3072]{1,0:T(8,128)} %get-tuple-element.697, f32[1024,3072]{1,0:T(8,128)} %copy-done.6, f32[1024]{0:T(1024)S(1)} %get-tuple-element.701, ...), kind=kLoop, calls=%fused_computation.55 | loop fusion | flops 72351744 | bytes 62943232 | tf_op jit(solution)/shard_map/convert_element_type | solution.py:222
  589.3 720.0 %while.42 = (s32[]{:T(128)}, bf16[2,512,768]{1,2,0:T(8,128)(2,1)}, bf16[2,512,768]{1,2,0:T(8,128)(2,1)}, f32[2,512,768]{1,2,0:T(8,128)}, f32[2,512,768]{1,2,0:T(...) while((s32[]{:T(128)}, bf16[2,512,768]{1,2,0:T(8,128)(2,1)}, ...), condition=%wide.wide.region_20.21_spmd.clone, body=%wide.wide.region_19.20_spmd.clone.sunk | while | flops 4112778240 | bytes 291545856 | solution.py:260
  675.7 29.7 %collective-permute-done.3 = bf16[2,512,768]{1,2,0:T(8,128)(2,1)} collective-permute-done((bf16[2,512,768]{1,2,0:T(8,128)(2,1)}, bf16[2,512,768]{1,2,0:T(8,128)(2,1)}, u32[]{:S(2)}, u32[]{:S(2)}) %collective-permute-start.3) | collective-permute-done | bytes 1572896 | tf_op jit(solution)/shard_map/while/body/eval_jaxpr/ppermute | solution.py:26
  708.9 30.2 %collective-permute-done = bf16[2,512,768]{1,2,0:T(8,128)(2,1)} collective-permute-done((bf16[2,512,768]{1,2,0:T(8,128)(2,1)}, bf16[2,512,768]{1,2,0:T(8,128)(2,1)}, u32[]{:S(2)}, u32[]{:S(2)}) %collective-permute-start) | collective-permute-done | bytes 1572896 | tf_op jit(solution)/shard_map/while/body/eval_jaxpr/ppermute | solution.py:20
  739.1 33.7 %collective-permute-done.1 = bf16[2,512,768]{1,2,0:T(8,128)(2,1)} collective-permute-done((bf16[2,512,768]{1,2,0:T(8,128)(2,1)}, bf16[2,512,768]{1,2,0:T(8,128)(2,1)}, u32[]{:S(2)}, u32[]{:S(2)}) %collective-permute-start.1) | collective-permute-done | bytes 1572896 | tf_op jit(solution)/shard_map/while/body/eval_jaxpr/ppermute | solution.py:20
  857.2 28.0 %collective-permute-done.3 = bf16[2,512,768]{1,2,0:T(8,128)(2,1)} collective-permute-done((bf16[2,512,768]{1,2,0:T(8,128)(2,1)}, bf16[2,512,768]{1,2,0:T(8,128)(2,1)}, u32[]{:S(2)}, u32[]{:S(2)}) %collective-permute-start.3) | collective-permute-done | bytes 1572896 | tf_op jit(solution)/shard_map/while/body/eval_jaxpr/ppermute | solution.py:26
  888.6 30.2 %collective-permute-done = bf16[2,512,768]{1,2,0:T(8,128)(2,1)} collective-permute-done((bf16[2,512,768]{1,2,0:T(8,128)(2,1)}, bf16[2,512,768]{1,2,0:T(8,128)(2,1)}, u32[]{:S(2)}, u32[]{:S(2)}) %collective-permute-start) | collective-permute-done | bytes 1572896 | tf_op jit(solution)/shard_map/while/body/eval_jaxpr/ppermute | solution.py:20
  918.8 33.7 %collective-permute-done.1 = bf16[2,512,768]{1,2,0:T(8,128)(2,1)} collective-permute-done((bf16[2,512,768]{1,2,0:T(8,128)(2,1)}, bf16[2,512,768]{1,2,0:T(8,128)(2,1)}, u32[]{:S(2)}, u32[]{:S(2)}) %collective-permute-start.1) | collective-permute-done | bytes 1572896 | tf_op jit(solution)/shard_map/while/body/eval_jaxpr/ppermute | solution.py:20
  1036.9 27.0 %collective-permute-done.3 = bf16[2,512,768]{1,2,0:T(8,128)(2,1)} collective-permute-done((bf16[2,512,768]{1,2,0:T(8,128)(2,1)}, bf16[2,512,768]{1,2,0:T(8,128)(2,1)}, u32[]{:S(2)}, u32[]{:S(2)}) %collective-permute-start.3) | collective-permute-done | bytes 1572896 | tf_op jit(solution)/shard_map/while/body/eval_jaxpr/ppermute | solution.py:26
  1067.4 30.2 %collective-permute-done = bf16[2,512,768]{1,2,0:T(8,128)(2,1)} collective-permute-done((bf16[2,512,768]{1,2,0:T(8,128)(2,1)}, bf16[2,512,768]{1,2,0:T(8,128)(2,1)}, u32[]{:S(2)}, u32[]{:S(2)}) %collective-permute-start) | collective-permute-done | bytes 1572896 | tf_op jit(solution)/shard_map/while/body/eval_jaxpr/ppermute | solution.py:20
  1097.6 33.7 %collective-permute-done.1 = bf16[2,512,768]{1,2,0:T(8,128)(2,1)} collective-permute-done((bf16[2,512,768]{1,2,0:T(8,128)(2,1)}, bf16[2,512,768]{1,2,0:T(8,128)(2,1)}, u32[]{:S(2)}, u32[]{:S(2)}) %collective-permute-start.1) | collective-permute-done | bytes 1572896 | tf_op jit(solution)/shard_map/while/body/eval_jaxpr/ppermute | solution.py:20
  1215.7 26.1 %collective-permute-done.3 = bf16[2,512,768]{1,2,0:T(8,128)(2,1)} collective-permute-done((bf16[2,512,768]{1,2,0:T(8,128)(2,1)}, bf16[2,512,768]{1,2,0:T(8,128)(2,1)}, u32[]{:S(2)}, u32[]{:S(2)}) %collective-permute-start.3) | collective-permute-done | bytes 1572896 | tf_op jit(solution)/shard_map/while/body/eval_jaxpr/ppermute | solution.py:26
  1245.3 30.2 %collective-permute-done = bf16[2,512,768]{1,2,0:T(8,128)(2,1)} collective-permute-done((bf16[2,512,768]{1,2,0:T(8,128)(2,1)}, bf16[2,512,768]{1,2,0:T(8,128)(2,1)}, u32[]{:S(2)}, u32[]{:S(2)}) %collective-permute-start) | collective-permute-done | bytes 1572896 | tf_op jit(solution)/shard_map/while/body/eval_jaxpr/ppermute | solution.py:20
  1275.5 33.7 %collective-permute-done.1 = bf16[2,512,768]{1,2,0:T(8,128)(2,1)} collective-permute-done((bf16[2,512,768]{1,2,0:T(8,128)(2,1)}, bf16[2,512,768]{1,2,0:T(8,128)(2,1)}, u32[]{:S(2)}, u32[]{:S(2)}) %collective-permute-start.1) | collective-permute-done | bytes 1572896 | tf_op jit(solution)/shard_map/while/body/eval_jaxpr/ppermute | solution.py:20
  1349.4 27.6 %reduce-scatter.15.cloned.1.call-done = bf16[96,2304]{1,0:T(8,128)(2,1)} async-done(((bf16[768,2304]{1,0:T(8,128)(2,1)}), bf16[96,2304]{1,0:T(8,128)(2,1)}) %reduce-scatter.15.cloned.1.call-update) | async-done | bytes 442384 | tf_op jit(solution)/shard_map/reduce_scatter | solution.py:278
  1379.2 56.0 %reduce-scatter.19.cloned.1.call-done = bf16[96,3072]{1,0:T(8,128)(2,1)} async-done(((bf16[768,3072]{1,0:T(8,128)(2,1)}), bf16[96,3072]{1,0:T(8,128)(2,1)}) %reduce-scatter.19.cloned.1.call-update) | async-done | bytes 589840 | tf_op jit(solution)/shard_map/reduce_scatter | solution.py:284
  1435.3 57.7 %reduce-scatter.23.cloned.1.call-done = bf16[384,768]{1,0:T(8,128)(2,1)} async-done(((bf16[3072,768]{1,0:T(8,128)(2,1)}), bf16[384,768]{1,0:T(8,128)(2,1)}) %reduce-scatter.23.cloned.1.call-update) | async-done | bytes 589840 | tf_op jit(solution)/shard_map/reduce_scatter | solution.py:287
  1560.9 17.3 all_gather.36
  1610.5 44.7 %all-reduce = (f32[768]{0:T(1024)}, f32[768]{0:T(1024)}, f32[768]{0:T(1024)}, f32[3072]{0:T(1024)}) all-reduce(f32[768]{0:T(1024)} %get-tuple-element.611, f32[768]{0:T(1024)} %get-tuple-element.609, f32[768]{0:T(1024)} %get-tuple-element.607, f32[3072]{0:T(1024)} %get-tuple-element.604), channel_id=1, replica_groups=mesh['rows'=8,'seq'=4] {'rows','seq'}, use_global_device_ids=true, to_apply=%region_32.33 | all-reduce | flops 5376 | bytes 43008 | tf_op jit(solution)/shard_map/psum | solution.py:333
  1699.4 34.1 %all-gather.18.cloned.1.call-done = bf16[3072,768]{0,1:T(8,128)(2,1)} async-done(((bf16[384,768]{0,1:T(8,128)(2,1)}), bf16[3072,768]{0,1:T(8,128)(2,1)}) %all-gather.18.cloned.1.call-update) | async-done | bytes 4718608 | tf_op jit(solution)/shard_map/all_gather | solution.py:329
  (446 shorter events, 856.0 us)
Async XLA Ops:
  7.2 126.0 %all-gather.8.cloned.1.call-start = ((), (), s32[]{:S(2)}) async-start(), calls=%async_computation.8 | async-start | bytes 7864320 | tf_op jit(solution)/shard_map/all_gather | solution.py:193
  19.3 229.6 %all-gather.10.cloned.1.call-start = ((), (), s32[]{:S(2)}) async-start(), calls=%async_computation.9 | async-start | bytes 7864320 | tf_op jit(solution)/shard_map/all_gather | solution.py:194
  20.1 1327.5 %reduce-scatter.17.cloned.1.call-start = ((), (), s32[]{:S(2)}) async-start(), calls=%async_computation.12 | async-start | bytes 1327104 | tf_op jit(solution)/shard_map/reduce_scatter | solution.py:281
  589.3 787.8 %reduce-scatter.15.cloned.1.call-start = ((), (), s32[]{:S(2)}) async-start(), calls=%async_computation.10 | async-start | bytes 3981312 | tf_op jit(solution)/shard_map/reduce_scatter | solution.py:278
  649.8 55.6 %collective-permute-start.3 = (bf16[2,512,768]{1,2,0:T(8,128)(2,1)}, bf16[2,512,768]{1,2,0:T(8,128)(2,1)}, u32[]{:S(2)}, u32[]{:S(2)}) collective-permute-start(bf16[2,512,768]{1,2,0:T(8,128)(2,1)} %fusion.158), channel_id=1, source_target_pairs={{0,1},{1,2},{2,3},{3,0},{4,5},{5,6},{6,7},{7,4},{8,9},{9,10},{10,1... | collective-permute-start | bytes 4718600 | tf_op jit(solution)/shard_map/while/body/eval_jaxpr/ppermute | solution.py:26
  650.0 89.1 %collective-permute-start = (bf16[2,512,768]{1,2,0:T(8,128)(2,1)}, bf16[2,512,768]{1,2,0:T(8,128)(2,1)}, u32[]{:S(2)}, u32[]{:S(2)}) collective-permute-start(bf16[2,512,768]{1,2,0:T(8,128)(2,1)} %copy.171), channel_id=1, source_target_pairs={{0,1},{1,2},{2,3},{4,5},{5,6},{6,7},{8,9},{9,10},{10,11},{12,13},{... | collective-permute-start | bytes 4718600 | tf_op jit(solution)/shard_map/while/body/eval_jaxpr/ppermute | solution.py:20
  655.3 117.5 %collective-permute-start.1 = (bf16[2,512,768]{1,2,0:T(8,128)(2,1)}, bf16[2,512,768]{1,2,0:T(8,128)(2,1)}, u32[]{:S(2)}, u32[]{:S(2)}) collective-permute-start(bf16[2,512,768]{1,2,0:T(8,128)(2,1)} %copy.172), channel_id=1, source_target_pairs={{0,1},{1,2},{2,3},{4,5},{5,6},{6,7},{8,9},{9,10},{10,11},{12,13},{... | collective-permute-start | bytes 4718600 | tf_op jit(solution)/shard_map/while/body/eval_jaxpr/ppermute | solution.py:20
  830.3 54.8 %collective-permute-start.3 = (bf16[2,512,768]{1,2,0:T(8,128)(2,1)}, bf16[2,512,768]{1,2,0:T(8,128)(2,1)}, u32[]{:S(2)}, u32[]{:S(2)}) collective-permute-start(bf16[2,512,768]{1,2,0:T(8,128)(2,1)} %fusion.158), channel_id=1, source_target_pairs={{0,1},{1,2},{2,3},{3,0},{4,5},{5,6},{6,7},{7,4},{8,9},{9,10},{10,1... | collective-permute-start | bytes 4718600 | tf_op jit(solution)/shard_map/while/body/eval_jaxpr/ppermute | solution.py:26
  830.3 88.5 %collective-permute-start = (bf16[2,512,768]{1,2,0:T(8,128)(2,1)}, bf16[2,512,768]{1,2,0:T(8,128)(2,1)}, u32[]{:S(2)}, u32[]{:S(2)}) collective-permute-start(bf16[2,512,768]{1,2,0:T(8,128)(2,1)} %copy.171), channel_id=1, source_target_pairs={{0,1},{1,2},{2,3},{4,5},{5,6},{6,7},{8,9},{9,10},{10,11},{12,13},{... | collective-permute-start | bytes 4718600 | tf_op jit(solution)/shard_map/while/body/eval_jaxpr/ppermute | solution.py:20
  833.7 118.8 %collective-permute-start.1 = (bf16[2,512,768]{1,2,0:T(8,128)(2,1)}, bf16[2,512,768]{1,2,0:T(8,128)(2,1)}, u32[]{:S(2)}, u32[]{:S(2)}) collective-permute-start(bf16[2,512,768]{1,2,0:T(8,128)(2,1)} %copy.172), channel_id=1, source_target_pairs={{0,1},{1,2},{2,3},{4,5},{5,6},{6,7},{8,9},{9,10},{10,11},{12,13},{... | collective-permute-start | bytes 4718600 | tf_op jit(solution)/shard_map/while/body/eval_jaxpr/ppermute | solution.py:20
  1010.1 87.6 %collective-permute-start = (bf16[2,512,768]{1,2,0:T(8,128)(2,1)}, bf16[2,512,768]{1,2,0:T(8,128)(2,1)}, u32[]{:S(2)}, u32[]{:S(2)}) collective-permute-start(bf16[2,512,768]{1,2,0:T(8,128)(2,1)} %copy.171), channel_id=1, source_target_pairs={{0,1},{1,2},{2,3},{4,5},{5,6},{6,7},{8,9},{9,10},{10,11},{12,13},{... | collective-permute-start | bytes 4718600 | tf_op jit(solution)/shard_map/while/body/eval_jaxpr/ppermute | solution.py:20
  1013.4 117.9 %collective-permute-start.1 = (bf16[2,512,768]{1,2,0:T(8,128)(2,1)}, bf16[2,512,768]{1,2,0:T(8,128)(2,1)}, u32[]{:S(2)}, u32[]{:S(2)}) collective-permute-start(bf16[2,512,768]{1,2,0:T(8,128)(2,1)} %copy.172), channel_id=1, source_target_pairs={{0,1},{1,2},{2,3},{4,5},{5,6},{6,7},{8,9},{9,10},{10,11},{12,13},{... | collective-permute-start | bytes 4718600 | tf_op jit(solution)/shard_map/while/body/eval_jaxpr/ppermute | solution.py:20
  1188.9 86.6 %collective-permute-start = (bf16[2,512,768]{1,2,0:T(8,128)(2,1)}, bf16[2,512,768]{1,2,0:T(8,128)(2,1)}, u32[]{:S(2)}, u32[]{:S(2)}) collective-permute-start(bf16[2,512,768]{1,2,0:T(8,128)(2,1)} %copy.171), channel_id=1, source_target_pairs={{0,1},{1,2},{2,3},{4,5},{5,6},{6,7},{8,9},{9,10},{10,11},{12,13},{... | collective-permute-start | bytes 4718600 | tf_op jit(solution)/shard_map/while/body/eval_jaxpr/ppermute | solution.py:20
  1192.2 117.0 %collective-permute-start.1 = (bf16[2,512,768]{1,2,0:T(8,128)(2,1)}, bf16[2,512,768]{1,2,0:T(8,128)(2,1)}, u32[]{:S(2)}, u32[]{:S(2)}) collective-permute-start(bf16[2,512,768]{1,2,0:T(8,128)(2,1)} %copy.172), channel_id=1, source_target_pairs={{0,1},{1,2},{2,3},{4,5},{5,6},{6,7},{8,9},{9,10},{10,11},{12,13},{... | collective-permute-start | bytes 4718600 | tf_op jit(solution)/shard_map/while/body/eval_jaxpr/ppermute | solution.py:20
  1327.2 108.0 %reduce-scatter.19.cloned.1.call-start = ((), (), s32[]{:S(2)}) async-start(), calls=%async_computation.14 | async-start | bytes 5308416 | tf_op jit(solution)/shard_map/reduce_scatter | solution.py:284
  1337.9 155.1 %reduce-scatter.23.cloned.1.call-start = ((), (), s32[]{:S(2)}) async-start(), calls=%async_computation.17 | async-start | bytes 5308416 | tf_op jit(solution)/shard_map/reduce_scatter | solution.py:287
  1347.6 162.6 %reduce-scatter.27.cloned.1.call-start = ((), (), s32[]{:S(2)}) async-start(), calls=%async_computation.20 | async-start | bytes 245760
  1349.4 185.3 %reduce-scatter.25.cloned.1.call-start = ((), (), s32[]{:S(2)}) async-start(), calls=%async_computation.19 | async-start | bytes 737280
  1379.2 181.7 %reduce-scatter.21.cloned.1.call-start = ((), (), s32[]{:S(2)}) async-start(), calls=%async_computation.15 | async-start | bytes 737280 | tf_op jit(solution)/shard_map/reduce_scatter | solution.py:298
  1435.3 152.0 %reduce-scatter.29.cloned.1.call-start = ((), (), s32[]{:S(2)}) async-start(), calls=%async_computation.21 | async-start | bytes 737280
  1495.2 175.2 %all-gather.14.cloned.1.call-start = ((), (), s32[]{:S(2)}) async-start(), calls=%async_computation.13 | async-start | bytes 1327104 | tf_op jit(solution)/shard_map/all_gather | solution.py:323
  1525.2 148.1 %all-gather.12.cloned.1.call-start = ((), (), s32[]{:S(2)}) async-start(), calls=%async_computation.11 | async-start | bytes 3981312 | tf_op jit(solution)/shard_map/all_gather | solution.py:320
  1556.0 136.0 %all-gather.16.cloned.1.call-start = ((), (), s32[]{:S(2)}) async-start(), calls=%async_computation.16 | async-start | bytes 5308416 | tf_op jit(solution)/shard_map/all_gather | solution.py:326
  1578.3 155.3 %all-gather.18.cloned.1.call-start = ((), (), s32[]{:S(2)}) async-start(), calls=%async_computation.18 | async-start | bytes 5308416 | tf_op jit(solution)/shard_map/all_gather | solution.py:329
  (99 other events, 1218.1 us)
Sparse Core Ops, SparseCore 0:
  19.5 113.6 all-gather.7
  135.3 113.5 all-gather.9
  589.4 37.6 reduce-scatter.16
  1327.3 49.6 reduce-scatter.14
  1381.3 53.8 reduce-scatter.18
  1439.1 53.8 reduce-scatter.22
  1495.4 14.6 reduce-scatter.26
  1512.4 22.2 reduce-scatter.24
  1537.0 23.9 reduce-scatter.20
  1563.6 23.6 reduce-scatter.28
  1589.2 25.9 all-gather.13
  1617.0 34.1 all-gather.11
  1653.0 39.0 all-gather.15
  1693.8 39.7 all-gather.17
where the time goes:
time: 1760 us; the launch traced here: 1750 us
  waiting for transfers between devices  806 us (46%)
  matrix products  442 us (25%)
  other arithmetic  191 us (11%)
  local copies, waits for them, and re-layouts  150 us (9%)
  blocking collectives  106 us (6%)
  starting transfers between devices  33.1 us (2%)
    ppermute x8, waiting for transfers between devices, passed_along(): lax.ppermute(value, axis, [(source, source + steps) for source in range(i...  256 us
    all_gather x1, waiting for transfers between devices, per_device(): lax.all_gather(value_rows, 'seq', axis=1, tiled=True)  116 us
    dot_general x8, matrix products, scores(): jnp.einsum('rqhd,rkhd->rhqk', split_heads(queries), split_heads(key_rows)...  115 us
    ppermute x8, waiting for transfers between devices, from_behind(): return lax.ppermute(value, axis, pairs)  111 us
    all_gather x1, waiting for transfers between devices, per_device(): lax.all_gather(key_rows, 'seq', axis=1, tiled=True)  96.5 us
    dot_general x4, matrix products, back_block(): jnp.einsum('rqhd,rkhd->rhqk', split_heads(grad_rows), split_heads(value_r...  59.1 us
    reduce_scatter x1, waiting for transfers between devices, per_device(): lax.psum_scatter(down_term.astype(jnp.bfloat16), 'rows', scatter_dimensio...  57.7 us
    reduce_scatter x1, waiting for transfers between devices, per_device(): lax.psum_scatter(up_term.astype(jnp.bfloat16), 'rows', scatter_dimension=...  56 us
  transfers between devices with their start and end apart: 30, of which 23 were waited for; matrix products, arithmetic and copies ran while one was open for 24% of the time, Pallas kernels for 0%

commit v1 on v0

--- a/solution.py
+++ b/solution.py
@@ -1,8 +1,11 @@
+import functools
 import math
 
 import jax
 import jax.numpy as jnp
 from jax import lax
+from jax.experimental import pallas as pl
+from jax.experimental.pallas import tpu as pltpu
 from jax.sharding import PartitionSpec as P
 
 D = 768
@@ -154,7 +157,7 @@
     )
 
 
-def per_device(
+def ring_layer(
     tokens,
     segment_ids,
     cotangent,
@@ -347,6 +350,651 @@
     )
 
 
+FF = 3072
+SEQ = 4
+BLOCK = 512
+HEADS_OWN = HEADS // SEQ
+GROUP = HEADS_OWN * 3 * HEAD_DIM
+MESH = pl.DeviceIdType.MESH
+F32 = jnp.float32
+BF16 = jnp.bfloat16
+VMEM_LIMIT = 56 * 2**20
+
+
+def causal_mask(key_start, key_count, query_count):
+    key_pos = lax.broadcasted_iota(jnp.int32, (key_count, query_count), 0) + key_start
+    query_pos = lax.broadcasted_iota(jnp.int32, (key_count, query_count), 1)
+    return key_pos <= query_pos
+
+
+def attend_kernel(block_count, qkv_ref, o_ref, lse_ref):
+    for query_block in range(block_count):
+        here = slice(query_block * BLOCK, (query_block + 1) * BLOCK)
+        queries = (qkv_ref[0:64, here].astype(F32) * 0.125).astype(BF16)
+        peak = jnp.full((1, BLOCK), MASKED, F32)
+        total = jnp.zeros((1, BLOCK), F32)
+        accum = jnp.zeros((64, BLOCK), F32)
+        for key_block in range(query_block + 1):
+            there = slice(key_block * BLOCK, (key_block + 1) * BLOCK)
+            logits = matmul(qkv_ref[64:128, there].T, queries)
+            if key_block == query_block:
+                logits = jnp.where(causal_mask(0, BLOCK, BLOCK), logits, MASKED)
+            new_peak = jnp.maximum(peak, jnp.max(logits, axis=0, keepdims=True))
+            weights = jnp.exp(logits - new_peak)
+            factor = jnp.exp(peak - new_peak)
+            total = total * factor + jnp.sum(weights, axis=0, keepdims=True)
+            accum = accum * factor + matmul(qkv_ref[128:192, there], weights.astype(BF16))
+            peak = new_peak
+        o_ref[:, here] = accum / total
+        lse_ref[0:1, here] = peak + jnp.log(total)
+
+
+def attend_forward(qkv, heads):
+    length = qkv.shape[1]
+    pairs = heads * length * (length + BLOCK) // 2
+    return pl.pallas_call(
+        functools.partial(attend_kernel, length // BLOCK),
+        grid=(heads,),
+        in_specs=[pl.BlockSpec((192, length), lambda h: (h, 0))],
+        out_specs=[
+            pl.BlockSpec((64, length), lambda h: (h, 0)),
+            pl.BlockSpec((8, length), lambda h: (h, 0)),
+        ],
+        out_shape=[
+            jax.ShapeDtypeStruct((heads * 64, length), F32),
+            jax.ShapeDtypeStruct((heads * 8, length), F32),
+        ],
+        compiler_params=pltpu.CompilerParams(vmem_limit_bytes=VMEM_LIMIT),
+        cost_estimate=pl.CostEstimate(
+            flops=pairs * 1024, bytes_accessed=heads * length * 700, transcendentals=pairs
+        ),
+    )(qkv)
+
+
+def attend_back_kernel(block_count, qkv_ref, o_ref, lse_ref, do_ref, d_ref, dk_acc, dv_acc):
+    dk_acc[...] = jnp.zeros_like(dk_acc)
+    dv_acc[...] = jnp.zeros_like(dv_acc)
+    for query_block in range(block_count):
+        here = slice(query_block * BLOCK, (query_block + 1) * BLOCK)
+        queries_t = (qkv_ref[0:64, here].astype(F32) * 0.125).astype(BF16)
+        queries = queries_t.T
+        do_t = do_ref[:, here]
+        do_rows = do_t.T
+        lse = lse_ref[0:1, here]
+        delta = jnp.sum(do_t.astype(F32) * o_ref[:, here], axis=0, keepdims=True)
+        dq = jnp.zeros((64, BLOCK), F32)
+        for key_block in range(query_block + 1):
+            there = slice(key_block * BLOCK, (key_block + 1) * BLOCK)
+            keys_t = qkv_ref[64:128, there]
+            probs = jnp.exp(matmul(keys_t.T, queries_t) - lse)
+            if key_block == query_block:
+                probs = jnp.where(causal_mask(0, BLOCK, BLOCK), probs, 0.0)
+            dprobs = matmul(qkv_ref[128:192, there].T, do_t)
+            dlogits = (probs * (dprobs - delta)).astype(BF16)
+            dq = dq + matmul(keys_t, dlogits)
+            dv_acc[there, :] += matmul(probs.astype(BF16), do_rows)
+            dk_acc[there, :] += matmul(dlogits, queries)
+        d_ref[0:64, here] = (dq * 0.125).astype(BF16)
+    d_ref[64:128, :] = dk_acc[...].T.astype(BF16)
+    d_ref[128:192, :] = dv_acc[...].T.astype(BF16)
+
+
+def attend_backward(qkv, o_t, lse, do_t, heads):
+    length = qkv.shape[1]
+    pairs = heads * length * (length + BLOCK) // 2
+    spec = lambda rows: pl.BlockSpec((rows, length), lambda h: (h, 0))
+    return pl.pallas_call(
+        functools.partial(attend_back_kernel, length // BLOCK),
+        grid=(heads,),
+        in_specs=[spec(192), spec(64), spec(8), spec(64)],
+        out_specs=spec(192),
+        out_shape=jax.ShapeDtypeStruct((heads * 192, length), BF16),
+        scratch_shapes=[pltpu.VMEM((length, 64), F32), pltpu.VMEM((length, 64), F32)],
+        compiler_params=pltpu.CompilerParams(vmem_limit_bytes=VMEM_LIMIT),
+        cost_estimate=pl.CostEstimate(
+            flops=pairs * 2048, bytes_accessed=heads * length * 1300, transcendentals=pairs
+        ),
+    )(qkv, o_t, lse, do_t)
+
+
+def widened(gain, width):
+    return jnp.concatenate([gain] * (width // 128), axis=1)
+
+
+def column_stats(values):
+    size = values.shape[0]
+    average = jnp.sum(values, axis=0, keepdims=True) * (1.0 / size)
+    centred = values - average
+    spread = jnp.sum(centred * centred, axis=0, keepdims=True) * (1.0 / size)
+    return average, lax.rsqrt(spread + EPSILON)
+
+
+def gelu_both(values):
+    t = 1.0 / (1.0 + (0.3275911 * 0.7071067811865476) * jnp.abs(values))
+    density = jnp.exp(-0.5 * (values * values))
+    tail = 0.5 * -1.453152027 + t * (0.5 * 1.061405429)
+    tail = 0.5 * 1.421413741 + t * tail
+    tail = 0.5 * -0.284496736 + t * tail
+    tail = 0.5 * 0.254829592 + t * tail
+    tail = tail * t * density
+    below = jnp.where(values >= 0, 1.0 - tail, tail)
+    return values * below, below + values * (density * 0.3989422804014327)
+
+
+def feed_kernel(steps, chunk, sub, has_partial, *refs):
+    names = iter(refs)
+    o_ref, x_ref, dy_ref, ig_ref, fg_ref, hg_ref, wo_t, wo, wu_t, wd, wd_t, wu = [
+        next(names) for _ in range(12)
+    ]
+    if has_partial:
+        part_d, part_u, part_o = [next(names) for _ in range(3)]
+    out_ref, dh_ref, do_ref, gd_ref, gu_ref, go_ref = [next(names) for _ in range(6)]
+    b_s, h_s, c_s, cn_s, dyt_s, n_s, slope_s, t_s, out_s, dc_s, st = [next(names) for _ in range(11)]
+    width = x_ref.shape[0]
+    step = pl.program_id(0)
+
+    @pl.when(step == 0)
+    def _():
+        o = o_ref[...].astype(F32)
+        average, inverse = column_stats(o)
+        b = ((o - average) * inverse * widened(ig_ref[...], width)).astype(BF16)
+        b_s[...] = b
+        st[0:1] = average
+        st[1:2] = inverse
+        dyt_s[...] = dy_ref[...].T
+        h = x_ref[...].T.astype(F32) + matmul(wo_t[...], b)
+        h_s[...] = h
+        average, inverse = column_stats(h)
+        st[2:3] = average
+        st[3:4] = inverse
+        c = ((h - average) * inverse * widened(fg_ref[...], width)).astype(BF16)
+        c_s[...] = c
+        cn_s[...] = c.T
+
+    @pl.when(step < steps)
+    def _():
+        base = pl.multiple_of(step * chunk, chunk)
+        for k in range(chunk // sub):
+            z, slope = gelu_both(matmul(wu_t[k * sub : (k + 1) * sub, :], c_s[...]))
+            n_s[pl.ds(base + k * sub, sub), :] = z
+            slope_s[pl.ds(base + k * sub, sub), :] = slope.astype(BF16)
+
+    @pl.when(step == steps - 1)
+    def _():
+        total = jnp.zeros((1, width), F32)
+        for k in range(FF // sub):
+            total = total + jnp.sum(n_s[k * sub : (k + 1) * sub, :], axis=0, keepdims=True)
+        average = total * (1.0 / FF)
+        total = jnp.zeros((1, width), F32)
+        for k in range(FF // sub):
+            centred = n_s[k * sub : (k + 1) * sub, :] - average
+            total = total + jnp.sum(centred * centred, axis=0, keepdims=True)
+        st[4:5] = average
+        st[5:6] = lax.rsqrt(total * (1.0 / FF) + EPSILON)
+        st[6:8] = jnp.zeros((2, width), F32)
+        out_s[...] = h_s[...]
+
+    @pl.when((step >= steps) & (step < 2 * steps))
+    def _():
+        base = pl.multiple_of((step - steps) * chunk, chunk)
+        average = st[4:5]
+        inverse = st[5:6]
+        first = jnp.zeros((1, width), F32)
+        second = jnp.zeros((1, width), F32)
+        pieces = []
+        for k in range(chunk // sub):
+            rows = slice(k * sub, (k + 1) * sub)
+            n = (n_s[pl.ds(base + k * sub, sub), :] - average) * inverse
+            n_s[pl.ds(base + k * sub, sub), :] = n
+            gain = widened(hg_ref[rows, :], width)
+            e = (n * gain).astype(BF16)
+            pieces.append(e)
+            t = matmul(wd[rows, :], dyt_s[...]) * gain
+            t_s[pl.ds(base + k * sub, sub), :] = t
+            first = first + jnp.sum(t, axis=0, keepdims=True)
+            second = second + jnp.sum(t * n, axis=0, keepdims=True)
+            grad = matmul(e, dy_ref[...])
+            if has_partial:
+                grad = grad + part_d[rows, :]
+            gd_ref[rows, :] = grad.astype(gd_ref.dtype)
+        out_s[...] += matmul(wd_t[...], jnp.concatenate(pieces, axis=0))
+        st[6:7] += first
+        st[7:8] += second
+
+    @pl.when(step == 2 * steps - 1)
+    def _():
+        out_ref[...] = out_s[...].astype(BF16).T
+        st[6:8] = st[6:8] * (1.0 / FF)
+        dc_s[...] = jnp.zeros_like(dc_s)
+
+    @pl.when(step >= 2 * steps)
+    def _():
+        base = pl.multiple_of((step - 2 * steps) * chunk, chunk)
+        inverse = st[5:6]
+        first = st[6:7]
+        second = st[7:8]
+        pieces = []
+        for k in range(chunk // sub):
+            rows = pl.ds(base + k * sub, sub)
+            n = n_s[rows, :]
+            du = ((t_s[rows, :] - first - n * second) * inverse * slope_s[rows, :].astype(F32)).astype(BF16)
+            pieces.append(du)
+            grad = matmul(du, cn_s[...])
+            if has_partial:
+                grad = grad + part_u[k * sub : (k + 1) * sub, :]
+            gu_ref[k * sub : (k + 1) * sub, :] = grad.astype(gu_ref.dtype)
+        dc_s[...] += matmul(wu[...], jnp.concatenate(pieces, axis=0))
+
+    @pl.when(step == 3 * steps - 1)
+    def _():
+        n = (h_s[...] - st[2:3]) * st[3:4]
+        t = dc_s[...] * widened(fg_ref[...], width)
+        first = jnp.sum(t, axis=0, keepdims=True) * (1.0 / D)
+        second = jnp.sum(t * n, axis=0, keepdims=True) * (1.0 / D)
+        dh = dyt_s[...].astype(F32) + (t - first - n * second) * st[3:4]
+        dh_rows = dh.T
+        dh_ref[...] = dh_rows
+        grad = matmul(b_s[...], dh_rows.astype(BF16))
+        if has_partial:
+            grad = grad + part_o[...]
+        go_ref[...] = grad.astype(go_ref.dtype)
+        n = (o_ref[...].astype(F32) - st[0:1]) * st[1:2]
+        t = matmul(wo[...], dh.astype(BF16)) * widened(ig_ref[...], width)
+        first = jnp.sum(t, axis=0, keepdims=True) * (1.0 / D)
+        second = jnp.sum(t * n, axis=0, keepdims=True) * (1.0 / D)
+        do_ref[...] = ((t - first - n * second) * st[1:2]).astype(BF16)
+
+
+def feed_both(o_t, x, dy, gains, weights, partial=None, chunk=768, sub=256):
+    width = x.shape[0]
+    steps = FF // chunk
+    has_partial = partial is not None
+    once = lambda *shape: pl.BlockSpec(shape, lambda i: (0, 0), pipeline_mode=pl.Buffered(1))
+    first = lambda i: jnp.clip(i, 0, steps - 1)
+    second = lambda i: jnp.clip(i - steps, 0, steps - 1)
+    third = lambda i: jnp.clip(i - 2 * steps, 0, steps - 1)
+    by_rows = lambda phase: pl.BlockSpec((chunk, D), lambda i: (phase(i), 0))
+    by_columns = lambda phase: pl.BlockSpec((D, chunk), lambda i: (0, phase(i)))
+    in_specs = [once(D, width), once(width, D), once(width, D), once(D, 128), once(D, 128)]
+    in_specs += [pl.BlockSpec((chunk, 128), lambda i: (second(i), 0)), once(D, D), once(D, D)]
+    in_specs += [by_rows(first), by_rows(second), by_columns(second), by_columns(third)]
+    args = [o_t, x, dy, *gains, *weights]
+    kind = F32
+    if has_partial:
+        in_specs += [by_rows(second), by_rows(third), once(D, D)]
+        args += list(partial)
+        kind = BF16
+    whole = lambda *shape: pl.BlockSpec(shape, lambda i: (0, 0))
+    return pl.pallas_call(
+        functools.partial(feed_kernel, steps, chunk, sub, has_partial),
+        grid=(3 * steps,),
+        in_specs=in_specs,
+        out_specs=[
+            whole(width, D),
+            whole(width, D),
+            whole(D, width),
+            by_rows(second),
+            by_rows(third),
+            whole(D, D),
+        ],
+        out_shape=[
+            jax.ShapeDtypeStruct((width, D), BF16),
+            jax.ShapeDtypeStruct((width, D), F32),
+            jax.ShapeDtypeStruct((D, width), BF16),
+            jax.ShapeDtypeStruct((FF, D), kind),
+            jax.ShapeDtypeStruct((FF, D), kind),
+            jax.ShapeDtypeStruct((D, D), kind),
+        ],
+        scratch_shapes=[
+            pltpu.VMEM((D, width), BF16),
+            pltpu.VMEM((D, width), F32),
+            pltpu.VMEM((D, width), BF16),
+            pltpu.VMEM((width, D), BF16),
+            pltpu.VMEM((D, width), BF16),
+            pltpu.VMEM((FF, width), F32),
+            pltpu.VMEM((FF, width), BF16),
+            pltpu.VMEM((FF, width), F32),
+            pltpu.VMEM((D, width), F32),
+            pltpu.VMEM((D, width), F32),
+            pltpu.VMEM((8, width), F32),
+        ],
+        compiler_params=pltpu.CompilerParams(vmem_limit_bytes=62 * 2**20),
+        cost_estimate=pl.CostEstimate(
+            flops=6 * width * D * (D + 2 * FF), bytes_accessed=80 * 2**20, transcendentals=width * FF
+        ),
+    )(*args)
+
+
+PIECE = 768
+HALF = PIECE // 2
+COLS = D // 2
+
+
+def sum_kernel(counts, *refs):
+    piece_count = sum(counts)
+    grads = refs[: len(counts)]
+    out_ref, own, r0, r1, r2, r3, r4, fin, own_sem, send_sem, recv_sem, fin_sem = refs[len(counts) :]
+    r = lax.axis_index("rows")
+    s = lax.axis_index("seq")
+    core, xb, yb, z_low, z_high = r % 2, (r // 2) % 2, r // 4, s % 2, s // 2
+    to_core = (r + 1 - 2 * core, s)
+    to_x = (r + 2 - 4 * xb, s)
+    to_y = (r + 4 - 8 * yb, s)
+    to_z_low = (r, s + 1 - 2 * z_low)
+    to_z_high = (r, s + 2 - 4 * z_high)
+    barrier = pltpu.get_barrier_semaphore()
+    for device in (to_core, to_x, to_y, to_z_low, to_z_high):
+        pl.semaphore_signal(barrier, inc=1, device_id=device, device_id_type=MESH)
+    pl.semaphore_wait(barrier, 5)
+    bits = [(xb, yb), (yb, xb)]
+    partners = [(to_x, to_y), (to_y, to_x)]
+
+    def rows_at(start, count):
+        return pl.ds(pl.multiple_of(start, 16), count)
+
+    def remote(source, target, kind, p, device):
+        return pltpu.make_async_remote_copy(
+            src_ref=source,
+            dst_ref=target,
+            send_sem=send_sem.at[kind, p],
+            recv_sem=recv_sem.at[kind, p],
+            device_id=device,
+            device_id_type=MESH,
+        )
+
+    def columns(o):
+        return slice(o * COLS, (o + 1) * COLS)
+
+    def base(o):
+        return bits[o][0] * 192 + bits[o][1] * 96
+
+    def core_copy(ref, q, p):
+        return remote(ref.at[rows_at(q * PIECE + (1 - core) * HALF, HALF), :], r0.at[p], 0, p, to_core)
+
+    def own_copy(ref, q, p):
+        return pltpu.make_async_copy(
+            ref.at[rows_at(q * PIECE + core * HALF, HALF), :], own.at[p], own_sem.at[p]
+        )
+
+    def first_copy(p, o):
+        part = own.at[p, rows_at((1 - bits[o][0]) * 192, 192), columns(o)]
+        return remote(part, r1.at[p, o], 1 + o, p, partners[o][0])
+
+    def second_copy(p, o):
+        part = own.at[p, rows_at(bits[o][0] * 192 + (1 - bits[o][1]) * 96, 96), columns(o)]
+        return remote(part, r2.at[p, o], 3 + o, p, partners[o][1])
+
+    def low_copy(p, o):
+        part = own.at[p, rows_at(base(o) + (1 - z_low) * 48, 48), columns(o)]
+        return remote(part, r3.at[p, o], 5 + o, p, to_z_low)
+
+    def high_copy(p, o):
+        part = own.at[p, rows_at(base(o) + z_low * 48, 48), columns(o)]
+        return remote(part, r4.at[p, o], 7 + o, p, to_z_high)
+
+    def region(p, start, count, o):
+        return out_ref.at[rows_at(p * PIECE + core * HALF + start, count), columns(o)]
+
+    def fin_copy(p, o):
+        return pltpu.make_async_copy(
+            fin.at[p, o], region(p, base(o) + z_low * 48, 48, o), fin_sem.at[o, p]
+        )
+
+    def low_back(p, o):
+        return remote(fin.at[p, o], region(p, base(o) + z_low * 48, 48, o), 9 + o, p, to_z_low)
+
+    def second_back(p, o):
+        part = region(p, base(o), 96, o)
+        return remote(part, part, 11 + o, p, partners[o][1])
+
+    def first_back(p, o):
+        part = region(p, bits[o][0] * 192, 192, o)
+        return remote(part, part, 13 + o, p, partners[o][0])
+
+    def core_back(p):
+        part = out_ref.at[rows_at(p * PIECE + core * HALF, HALF), :]
+        return remote(part, part, 15, p, to_core)
+
+    offset = 0
+    for ref, count in zip(grads, counts):
+
+        def begin(q, carry, ref=ref, offset=offset):
+            core_copy(ref, q, q + offset).start()
+            own_copy(ref, q, q + offset).start()
+            return carry
+
+        lax.fori_loop(0, count, begin, 0)
+        offset += count
+
+    def added(index, other):
+        own[index] = (own[index].astype(F32) + other.astype(F32)).astype(BF16)
+
+    def after_core(p):
+        own_copy(grads[0], 0, p).wait()
+        core_copy(grads[0], 0, p).wait()
+        own[p] = (own[p].astype(F32) + r0[p].astype(F32)).astype(BF16)
+        for o in range(2):
+            first_copy(p, o).start()
+
+    def after_first(p):
+        for o in range(2):
+            first_copy(p, o).wait()
+            added((p, rows_at(bits[o][0] * 192, 192), columns(o)), r1[p, o])
+            second_copy(p, o).start()
+
+    def after_second(p):
+        for o in range(2):
+            second_copy(p, o).wait()
+            added((p, rows_at(base(o), 96), columns(o)), r2[p, o])
+            low_copy(p, o).start()
+
+    def after_low(p):
+        for o in range(2):
+            low_copy(p, o).wait()
+            added((p, rows_at(base(o) + z_low * 48, 48), columns(o)), r3[p, o])
+            high_copy(p, o).start()
+
+    def after_high(p):
+        for o in range(2):
+            high_copy(p, o).wait()
+            mine = own[p, rows_at(base(o) + z_low * 48, 48), columns(o)].astype(F32)
+            fin[p, o] = (mine + r4[p, o].astype(F32)).astype(BF16)
+            low_back(p, o).start()
+            fin_copy(p, o).start()
+
+    def after_low_back(p):
+        for o in range(2):
+            fin_copy(p, o).wait()
+            low_back(p, o).wait()
+            second_back(p, o).start()
+
+    def after_second_back(p):
+        for o in range(2):
+            second_back(p, o).wait()
+            first_back(p, o).start()
+
+    def after_first_back(p):
+        for o in range(2):
+            first_back(p, o).wait()
+        core_back(p).start()
+
+    def after_core_back(p):
+        core_back(p).wait()
+
+    stages = [
+        after_core,
+        after_first,
+        after_second,
+        after_low,
+        after_high,
+        after_low_back,
+        after_second_back,
+        after_first_back,
+        after_core_back,
+    ]
+
+    def tick(t, carry):
+        for lag, stage in enumerate(stages):
+            p = t - lag
+
+            @pl.when((p >= 0) & (p < piece_count))
+            def _():
+                stage(p)
+
+        return carry
+
+    lax.fori_loop(0, piece_count + len(stages) - 1, tick, 0)
+
+
+def summed_everywhere(grads, collective_id):
+    counts = [grad.shape[0] // PIECE for grad in grads]
+    n = sum(counts)
+    dma = pltpu.SemaphoreType.DMA
+    return pl.pallas_call(
+        functools.partial(sum_kernel, counts),
+        out_shape=jax.ShapeDtypeStruct((n * PIECE, D), BF16),
+        in_specs=[pl.BlockSpec(memory_space=pl.ANY)] * len(grads),
+        out_specs=pl.BlockSpec(memory_space=pl.ANY),
+        scratch_shapes=[
+            pltpu.VMEM((n, HALF, D), BF16),
+            pltpu.VMEM((n, HALF, D), BF16),
+            pltpu.VMEM((n, 2, 192, COLS), BF16),
+            pltpu.VMEM((n, 2, 96, COLS), BF16),
+            pltpu.VMEM((n, 2, 48, COLS), BF16),
+            pltpu.VMEM((n, 2, 48, COLS), BF16),
+            pltpu.VMEM((n, 2, 48, COLS), BF16),
+            dma((n,)),
+            dma((16, n)),
+            dma((16, n)),
+            dma((2, n)),
+        ],
+        compiler_params=pltpu.CompilerParams(
+            collective_id=collective_id, has_side_effects=True, vmem_limit_bytes=VMEM_LIMIT
+        ),
+        cost_estimate=pl.CostEstimate(flops=0, bytes_accessed=n * PIECE * D * 64, transcendentals=0),
+    )(*grads)
+
+
+def exchanged(pieces, own_index):
+    out = jnp.zeros_like(pieces)
+    own = lax.dynamic_index_in_dim(pieces, own_index, 0, keepdims=True)
+    out = lax.dynamic_update_slice_in_dim(out, own, own_index, 0)
+    for shift in range(1, SEQ):
+        leaving = lax.dynamic_index_in_dim(pieces, (own_index + shift) % SEQ, 0, keepdims=True)
+        arrived = lax.ppermute(leaving, "seq", [(i, (i + shift) % SEQ) for i in range(SEQ)])
+        out = lax.dynamic_update_slice_in_dim(out, arrived, (own_index - shift) % SEQ, 0)
+    return out
+
+
+def normed_rows(x, gain):
+    out, normed, inverse = layer_norm(x.astype(F32), gain)
+    return out.astype(BF16), normed, inverse
+
+
+def layer_back(upstream, normed, inverse, gain):
+    scaled = upstream * gain
+    return inverse * (
+        scaled
+        - jnp.mean(scaled, axis=-1, keepdims=True)
+        - normed * jnp.mean(scaled * normed, axis=-1, keepdims=True)
+    )
+
+
+def split_layer(
+    tokens,
+    segment_ids,
+    cotangent,
+    query_key_value,
+    out_weight,
+    up_weight,
+    down_weight,
+    attend_gain,
+    inner_gain,
+    feed_gain,
+    hidden_gain,
+):
+    place = lax.axis_index("seq")
+    long_first = segment_ids[0, -1] == 0
+    x_long = jnp.where(long_first, tokens[0], tokens[1])
+    x_pack = jnp.where(long_first, tokens[1], tokens[0])
+    dy_long = jnp.where(long_first, cotangent[0], cotangent[1])
+    dy_pack = jnp.where(long_first, cotangent[1], cotangent[0])
+    ring = [(i, (i + 1) % SEQ) for i in range(SEQ)]
+    x_blocks = [x_long]
+    for _ in range(1, SEQ):
+        x_blocks.append(lax.ppermute(x_blocks[-1], "seq", ring))
+    qkv_t = query_key_value.reshape(D, 3, HEADS, HEAD_DIM).transpose(2, 1, 3, 0).reshape(3 * D, D)
+    wide = lambda gain: jnp.broadcast_to(gain[:, None], (gain.shape[0], 128))
+    gains = (wide(inner_gain), wide(feed_gain), wide(hidden_gain))
+    weights = (out_weight.T, out_weight, up_weight.T, down_weight, down_weight.T, up_weight)
+    a_pack, pack_normed, pack_inverse = normed_rows(x_pack, attend_gain)
+    qkv_pack = right_t(qkv_t, a_pack).astype(BF16)
+    o_pack, lse_pack = attend_forward(qkv_pack, HEADS)
+    out_pack, dh_pack, do_pack, gd_pack, gu_pack, go_pack = feed_both(
+        o_pack, x_pack, dy_pack, gains, weights
+    )
+    dqkv_pack = attend_backward(qkv_pack, o_pack, lse_pack, do_pack, HEADS)
+    gq_pack = matmul(dqkv_pack, a_pack)
+    dxa_pack = layer_back(left_t(dqkv_pack, qkv_t), pack_normed, pack_inverse, attend_gain)
+    dx_pack = (dh_pack + dxa_pack).astype(BF16)
+    own_t = lax.dynamic_slice_in_dim(qkv_t, place * GROUP, GROUP, 0)
+    a_all = jnp.zeros((SEQ, BLOCK, D), BF16)
+    for shift, block in enumerate(x_blocks):
+        a_block, normed, inverse = normed_rows(block, attend_gain)
+        if shift == 0:
+            long_normed, long_inverse = normed, inverse
+        a_all = lax.dynamic_update_slice_in_dim(a_all, a_block[None], (place - shift) % SEQ, 0)
+    a_all = a_all.reshape(SEQ * BLOCK, D)
+    qkv_long = right_t(own_t, a_all).astype(BF16)
+    o_long, lse_long = attend_forward(qkv_long, HEADS_OWN)
+    o_pieces = o_long.astype(BF16).reshape(HEADS_OWN * HEAD_DIM, SEQ, BLOCK).transpose(1, 0, 2)
+    o_mine = exchanged(o_pieces, place).reshape(D, BLOCK)
+    out_long, dh_long, do_long, gd, gu, go = feed_both(
+        o_mine, x_long, dy_long, gains, weights, (gd_pack, gu_pack, go_pack)
+    )
+    do_own = exchanged(do_long.reshape(SEQ, HEADS_OWN * HEAD_DIM, BLOCK), place)
+    do_own = do_own.transpose(1, 0, 2).reshape(HEADS_OWN * HEAD_DIM, SEQ * BLOCK)
+    dqkv_own = attend_backward(qkv_long, o_long, lse_long, do_own, HEADS_OWN)
+    gq_long = matmul(dqkv_own, a_all)
+    gq_own = lax.dynamic_slice_in_dim(gq_pack, place * GROUP, GROUP, 0) + gq_long
+    gq = lax.dynamic_update_slice_in_dim(gq_pack, gq_own, place * GROUP, 0).astype(BF16)
+    dqkv_long = exchanged(dqkv_own.reshape(GROUP, SEQ, BLOCK).transpose(1, 0, 2), place)
+    dqkv_long = dqkv_long.reshape(3 * D, BLOCK)
+    dxa_long = layer_back(left_t(dqkv_long, qkv_t), long_normed, long_inverse, attend_gain)
+    dx_long = (dh_long + dxa_long).astype(BF16)
+    total = summed_everywhere((gd, gu, go, gq), 0)
+    down_grad = total[:FF].astype(F32)
+    up_grad_t = total[FF : 2 * FF].astype(F32)
+    out_grad = total[2 * FF : 2 * FF + D].astype(F32)
+    qkv_grad_t = total[2 * FF + D :].astype(F32)
+    qkv_grad = qkv_grad_t.reshape(HEADS, 3, HEAD_DIM, D).transpose(3, 1, 0, 2).reshape(D, 3 * D)
+    attend_total = jnp.sum(qkv_grad_t * qkv_t.astype(F32), axis=0) / attend_gain
+    inner_total = jnp.sum(out_grad * out_weight.astype(F32), axis=1) / inner_gain
+    feed_total = jnp.sum(up_grad_t * weights[2].astype(F32), axis=0) / feed_gain
+    hidden_total = jnp.sum(down_grad * down_weight.astype(F32), axis=1) / hidden_gain
+    output = jnp.where(long_first, jnp.stack([out_long, out_pack]), jnp.stack([out_pack, out_long]))
+    tokens_grad = jnp.where(long_first, jnp.stack([dx_long, dx_pack]), jnp.stack([dx_pack, dx_long]))
+    return (
+        output,
+        tokens_grad,
+        qkv_grad,
+        out_grad,
+        up_grad_t.T,
+        down_grad,
+        attend_total,
+        inner_total,
+        feed_total,
+        hidden_total,
+    )
+
+
+def per_device(tokens, *others):
+    split = lax.axis_size("seq") == SEQ and lax.axis_size("rows") == 8
+    if split and tokens.shape == (2, BLOCK, D):
+        return split_layer(tokens, *others)
+    return ring_layer(tokens, *others)
+
+
 def solution(mesh):
     return jax.shard_map(
         per_device,

time: 1760 us -> 585 us (0.33)
  waiting for transfers between devices: 806 us -> 89.6 us
  matrix products: 442 us -> 27 us
  Pallas kernels: 0 us -> 277 us
  other arithmetic: 191 us -> 56.3 us
  blocking collectives: 106 us -> 0 us
  local copies, waits for them, and re-layouts: 150 us -> 111 us
  starting transfers between devices: 33.1 us -> 13.5 us
    dot_general x28 -> x0, matrix products: 328 us -> none  [the longest x8 115 us: scores(): jnp.einsum('rqhd,rkhd->rhqk', split_heads(queries), split_heads(key_rows)...]
    pallas_call x0 -> x7, Pallas kernels: none -> 277 us  [the longest x1 130 us: summed_everywhere(): pl.pallas_call(functools.partial(sum_kernel, counts), out_shape=jax.Shape...]
    ppermute x16 -> x12, waiting for transfers between devices: 366 us -> 89.6 us  [the longest x9 59.6 us: exchanged(): lax.ppermute(leaving, 'seq', [(i, (i + shift) % SEQ) for i in range(SEQ)])]
    all_gather x6 -> x0, waiting for transfers between devices: 260 us -> none  [the longest x1 116 us: per_device(): lax.all_gather(value_rows, 'seq', axis=1, tiled=True)]
    reduce_scatter x5 -> x0, waiting for transfers between devices: 146 us -> none  [the longest x1 57.7 us: per_device(): lax.psum_scatter(down_term.astype(jnp.bfloat16), 'rows', scatter_dimensio...]
    convert_element_type x23 -> x3, other arithmetic: 88.4 us -> 12.3 us  [the longest x1 5.51 us: split_layer(): qkv_grad_t = total[2 * FF + D:].astype(F32)]
    all_gather x4 -> x0, blocking collectives: 60.9 us -> none  [the longest x1 17.3 us: per_device(): lax.all_gather(seq_sectioned[2].astype(jnp.bfloat16), 'seq', axis=1, tile...]
    while x119 -> x0, local copies, waits for them, and re-layouts: 48.5 us -> none
  transfers between devices with their start and end apart: 30 -> 12, of which waited for: 23 -> 9; matrix products, arithmetic and copies ran while one was open for 24% -> 19% of each run, Pallas kernels for 0% -> 11%
where the time goes in v1:
time: 585 us; the launch traced here: 577 us
  Pallas kernels  277 us (47%)
  local copies, waits for them, and re-layouts  111 us (19%)
  waiting for transfers between devices  89.6 us (15%)
  other arithmetic  56.3 us (10%)
  matrix products  27 us (5%)
  starting transfers between devices  13.5 us (2%)
    pallas_call x1, Pallas kernels, summed_everywhere(): pl.pallas_call(functools.partial(sum_kernel, counts), out_shape=jax.Shape...  130 us
    pallas_call x2, Pallas kernels, feed_both(): pl.pallas_call(functools.partial(feed_kernel, steps, chunk, sub, has_part...  80 us
    ppermute x9, waiting for transfers between devices, exchanged(): lax.ppermute(leaving, 'seq', [(i, (i + shift) % SEQ) for i in range(SEQ)])  59.6 us
    unnamed x98, local copies, waits for them, and re-layouts  48.7 us
    pallas_call x2, Pallas kernels, attend_backward(): pl.pallas_call(functools.partial(attend_back_kernel, length // BLOCK), gr...  41.3 us
    dynamic_update_slice x10, local copies, waits for them, and re-layouts, exchanged(): lax.dynamic_update_slice_in_dim(out, arrived, (own_index - shift) % SEQ, 0)  32.5 us
    ppermute x3, waiting for transfers between devices, split_layer(): x_blocks.append(lax.ppermute(x_blocks[-1], 'seq', ring))  30 us
    pallas_call x2, Pallas kernels, attend_forward(): pl.pallas_call(functools.partial(attend_kernel, length // BLOCK), grid=(h...  26.2 us
  transfers between devices with their start and end apart: 12, of which 9 were waited for; matrix products, arithmetic and copies ran while one was open for 19% of the time, Pallas kernels for 11%

profile of v1, /device:TPU:9, one launch (start us, length us, event | category | flops | bytes accessed | tf_op | source)
XLA Modules:
  0.0 576.9 jit_solution(2931236713471884964)
XLA Ops:
  19.5 10.9 %shard_map.187 = (f32[768,512]{1,0:T(8,128)}, f32[96,512]{1,0:T(8,128)}) custom-call(bf16[2304,512]{1,0:T(8,128)(2,1)} %fusion.1.qkv_ref), custom_call_target="tpu_custom_call" | custom-call | flops 3221225472 | bytes 4300800 | tf_op jit(solution)/shard_map/pallas_call | solution.py:395
  31.6 6.7 %copy.37 = bf16[768,3072]{0,1:T(8,128)(2,1)} copy(bf16[768,3072]{1,0:T(8,128)(2,1)} %refs_11_.3) | data formatting | bytes 9437184 | tf_op args[5]
  38.3 6.7 %copy.38 = bf16[3072,768]{0,1:T(8,128)(2,1)} copy(bf16[3072,768]{1,0:T(8,128)(2,1)} %refs_9_.3) | data formatting | bytes 9437184 | tf_op args[6]
  49.9 39.0 %shard_map.188 = (bf16[512,768]{1,0:T(8,128)(2,1)}, f32[512,768]{1,0:T(8,128)}, bf16[768,512]{1,0:T(8,128)(2,1)}, f32[3072,768]{1,0:T(8,128)}, f32[3072,768]{1,0:T(8,128)}, /*index=5*/f32[768,768]{1,0:T(8,128)}) custom-call(f32[768,512]{1,0:T(8,128)} %get-tuple-element.27.refs_0_.o_ref, bf16[512,768]{1,0:T(8,128)(2,1)} %get-tuple-element.82.refs_1_, ...), custom_call_target="tpu_custom_call" | custom-call | flops 16307453952 | bytes 83886080 | tf_op jit(solution)/shard_map/pallas_call | solution.py:628
  89.0 15.5 %shard_map.191 = bf16[2304,512]{1,0:T(8,128)(2,1)} custom-call(bf16[2304,512]{1,0:T(8,128)(2,1)} %fusion.1.qkv_ref, f32[768,512]{1,0:T(8,128)} %get-tuple-element.27.refs_0_.o_ref, f32[96,512]{1,0:T(8,128)} %get-tuple-element.37.lse_ref, bf16[768,512]{1,0:T(8,128)(2,1)} %get-tuple-element.38.do_ref), custom_call_target="tpu_custom_call" | custom-call | flops 6442450944 | bytes 7987200 | tf_op jit(solution)/shard_map/pallas_call | solution.py:446
  104.5 5.6 fusion.64
  124.4 14.1 %collective-permute-done.1 = bf16[512,768]{1,0:T(8,128)(2,1)S(1)} collective-permute-done((bf16[512,768]{1,0:T(8,128)(2,1)}, bf16[512,768]{1,0:T(8,128)(2,1)S(1)}, u32[]{:S(2)}, u32[]{:S(2)}) %collective-permute-start.1) | collective-permute-done | bytes 786464 | tf_op jit(solution)/shard_map/ppermute | solution.py:925
  140.6 16.0 %collective-permute-done.2 = bf16[512,768]{1,0:T(8,128)(2,1)S(1)} collective-permute-done((bf16[512,768]{1,0:T(8,128)(2,1)S(1)}, bf16[512,768]{1,0:T(8,128)(2,1)S(1)}, u32[]{:S(2)}, u32[]{:S(2)}) %collective-permute-start.2) | collective-permute-done | bytes 786464 | tf_op jit(solution)/shard_map/ppermute | solution.py:925
  162.5 15.3 %shard_map.186 = (f32[192,2048]{1,0:T(8,128)}, f32[24,2048]{1,0:T(8,128)}) custom-call(bf16[576,2048]{1,0:T(8,128)(2,1)} %convolution_convert_fusion.1.qkv_ref), custom_call_target="tpu_custom_call" | custom-call | flops 8053063680 | bytes 4300800 | tf_op jit(solution)/shard_map/pallas_call | solution.py:395
  194.6 18.5 %collective-permute-done.4 = bf16[1,192,512]{2,0,1:T(2,128)(2,1)S(1)} collective-permute-done((bf16[1,192,512]{2,0,1:T(2,128)(2,1)S(1)}, bf16[1,192,512]{2,0,1:T(2,128)(2,1)S(1)}, u32[]{:S(2)}, u32[]{:S(2)}) %collective-permute-start.4) | collective-permute-done | bytes 196640 | tf_op jit(solution)/shard_map/ppermute | solution.py:884
  224.2 41.0 %shard_map.189 = (bf16[512,768]{1,0:T(8,128)(2,1)}, f32[512,768]{1,0:T(8,128)}, bf16[768,512]{1,0:T(8,128)(2,1)}, bf16[3072,768]{1,0:T(8,128)(2,1)}, bf16[3072,7...) custom-call(bf16[768,512]{1,0:T(8,128)(2,1)} %bitcast.110, bf16[512,768]{1,0:T(8,128)(2,1)} %get-tuple-element.71.refs_1_, ...), custom_call_target="tpu_custom_call" | custom-call | flops 16307453952 | bytes 83886080 | tf_op jit(solution)/shard_map/pallas_call | solution.py:628
  277.4 6.4 %dynamic_update_slice.60 = bf16[4,192,512]{2,0,1:T(4,128)(2,1)S(1)} dynamic-update-slice(bf16[4,192,512]{2,0,1:T(4,128)(2,1)S(1)} %dynamic_update_slice.59, bf16[1,192,512]{2,0,1:T(2,128)(2,1)} %collective-permute-done.6, s32[]{:T(128)S(6)} %select_n.160, s32[]{:T(128)} %constant.129.clone.1, s32[]{:T(128)} %constant.129.clone.1) | dynamic-update-slice | bytes 393220 | tf_op jit(solution)/shard_map/dynamic_update_slice | solution.py:885
  283.8 17.0 %collective-permute-done.7 = bf16[1,192,512]{2,0,1:T(2,128)(2,1)} collective-permute-done((bf16[1,192,512]{2,0,1:T(2,128)(2,1)}, bf16[1,192,512]{2,0,1:T(2,128)(2,1)}, u32[]{:S(2)}, u32[]{:S(2)}) %collective-permute-start.7) | collective-permute-done | bytes 196640 | tf_op jit(solution)/shard_map/ppermute | solution.py:884
  300.8 6.4 %dynamic_update_slice.61 = bf16[4,192,512]{2,0,1:T(4,128)(2,1)S(1)} dynamic-update-slice(bf16[4,192,512]{2,0,1:T(4,128)(2,1)S(1)} %dynamic_update_slice.60, bf16[1,192,512]{2,0,1:T(2,128)(2,1)} %collective-permute-done.7, s32[]{:T(128)S(6)} %select_n.162, s32[]{:T(128)} %constant.129.clone.1, s32[]{:T(128)} %constant.129.clone.1) | dynamic-update-slice | bytes 393220 | tf_op jit(solution)/shard_map/dynamic_update_slice | solution.py:885
  307.2 6.4 %dynamic_update_slice.62 = bf16[4,192,512]{2,0,1:T(4,128)(2,1)S(1)} dynamic-update-slice(bf16[4,192,512]{2,0,1:T(4,128)(2,1)S(1)} %dynamic_update_slice.61, bf16[1,192,512]{2,0,1:T(2,128)(2,1)} %collective-permute-done.8, s32[]{:T(128)S(6)} %select_n.164, s32[]{:T(128)} %constant.129.clone.1, s32[]{:T(128)} %constant.129.clone.1) | dynamic-update-slice | bytes 393220 | tf_op jit(solution)/shard_map/dynamic_update_slice | solution.py:885
  314.7 25.8 %shard_map.190 = bf16[576,2048]{1,0:T(8,128)(2,1)} custom-call(bf16[576,2048]{1,0:T(8,128)(2,1)} %convolution_convert_fusion.1.qkv_ref, f32[192,2048]{1,0:T(8,128)} %get-tuple-element.26.o_ref, f32[24,2048]{1,0:T(8,128)} %get-tuple-element.34.lse_ref, bf16[192,2048]{1,0:T(8,128)(2,1)} %bitcast.111), custom_call_target="tpu_custom_call" | custom-call | flops 16106127360 | bytes 7987200 | tf_op jit(solution)/shard_map/pallas_call | solution.py:446
  340.5 5.4 add_dynamic-update-slice_fusion
  351.1 129.8 %shard_map.192 = bf16[9216,768]{1,0:T(8,128)(2,1)} custom-call(bf16[3072,768]{1,0:T(8,128)(2,1)} %get-tuple-element.39.refs_0_, bf16[3072,768]{1,0:T(8,128)(2,1)} %get-tuple-element.40.refs_1_, bf16[768,768]{1,0:T(8,128)(2,1)} %get-tuple-element.41.refs_2_, bf16[2304,768]{1,0:T(8,128)(2,1)} %convert_element_type.106.refs_3_), custom_call_target="tpu_custom_call" | custom-call | bytes 452984832 | tf_op jit(solution)/shard_map/pallas_call | solution.py:853
  480.9 5.5 slice_convert_fusion.1
  486.5 8.0 %convert_bitcast_fusion = f32[768,3072]{0,1:T(8,128)} fusion(bf16[9216,768]{1,0:T(8,128)(2,1)} %shard_map.192), kind=kLoop, calls=%fused_computation.1 | loop fusion | flops 2359296 | bytes 14155776 | tf_op jit(solution)/shard_map/transpose | solution.py:982
  496.3 6.8 %multiply_reduce_fusion = (f32[3072]{0:T(1024)S(1)}, f32[3072,768]{1,0:T(8,128)}, f32[768]{0:T(1024)}) fusion(bf16[3072,768]{1,0:T(8,128)(2,1)S(1)} %bitcast.91, bf16[9216,768]{1,0:T(8,128)(2,1)S(1)} %copy-done, bf16[768,3072]{0,1:T(8,128)(2,1)} %copy.37), kind=kLoop, calls=%fused_computation.3 | loop fusion | flops 18870528 | bytes 28326912 | tf_op jit(solution)/shard_map/reduce_sum | solution.py:974
  525.2 8.2 %copy.49 = f32[768,2304]{1,0:T(8,128)} copy(f32[768,2304]{0,1:T(8,128)} %bitcast.86) | data formatting | bytes 14155776
  533.4 9.6 %copy.50 = f32[768,3072]{1,0:T(8,128)} copy(f32[768,3072]{0,1:T(8,128)} %convert_bitcast_fusion) | data formatting | bytes 18874368
  549.8 16.1 %collective-permute-done.10 = bf16[1,576,512]{2,1,0:T(8,128)(2,1)} collective-permute-done((bf16[1,576,512]{2,1,0:T(8,128)(2,1)S(1)}, bf16[1,576,512]{2,1,0:T(8,128)(2,1)}, u32[]{:S(2)}, u32[]{:S(2)}) %collective-permute-start.10) | collective-permute-done | bytes 589856 | tf_op jit(solution)/shard_map/ppermute | solution.py:884
  (183 shorter events, 134.1 us)
Async XLA Ops:
  6.0 112.7 %collective-permute-start = (bf16[512,768]{1,0:T(8,128)(2,1)}, bf16[512,768]{1,0:T(8,128)(2,1)}, u32[]{:S(2)}, u32[]{:S(2)}) collective-permute-start(bf16[512,768]{1,0:T(8,128)(2,1)} %get-tuple-element.71.refs_1_), channel_id=1, source_target_pairs={{0,1},{1,2},{2,3},{3,0},{4,5},{5,6},{6,7},{7,4},{8,9},{9,10},{10,1... | collective-permute-start | bytes 2359304 | tf_op jit(solution)/shard_map/ppermute | solution.py:925
  7.3 103.7 %copy-start.24 = (f32[512]{0:T(512)}, f32[512]{0:T(512)S(1)}, u32[]{:S(2)}) copy-start(f32[512]{0:T(512)S(1)} %broadcast_multiply_fusion.8) | copy-start | bytes 6148
  8.8 102.1 %copy-start.26 = (f32[512]{0:T(512)}, f32[512]{0:T(512)S(1)}, u32[]{:S(2)}) copy-start(f32[512]{0:T(512)S(1)} %add_rsqrt_fusion.4) | copy-start | bytes 6148
  88.9 15.6 %copy-start.2 = (bf16[12,3,64,768]{3,2,1,0:T(8,128)(2,1)S(1)}, bf16[12,3,64,768]{3,2,1,0:T(8,128)(2,1)}, u32[]{:S(2)}) copy-start(bf16[12,3,64,768]{3,2,1,0:T(8,128)(2,1)} %copy-done.1) | copy-start | bytes 10616836
  89.0 15.6 %copy-start.6 = (bf16[512,768]{1,0:T(8,128)(2,1)S(1)}, bf16[512,768]{1,0:T(8,128)(2,1)}, u32[]{:S(2)}) copy-start(bf16[512,768]{1,0:T(8,128)(2,1)} %get-tuple-element.82.refs_1_) | copy-start | bytes 2359300
  89.0 15.6 %copy-start.31 = (f32[512]{0:T(512)S(1)}, f32[512]{0:T(512)}, u32[]{:S(2)}) copy-start(f32[512]{0:T(512)} %copy-done.30) | copy-start | bytes 6148
  120.1 18.4 %collective-permute-start.1 = (bf16[512,768]{1,0:T(8,128)(2,1)}, bf16[512,768]{1,0:T(8,128)(2,1)S(1)}, u32[]{:S(2)}, u32[]{:S(2)}) collective-permute-start(bf16[512,768]{1,0:T(8,128)(2,1)} %collective-permute-done), channel_id=1, source_target_pairs={{0,1},{1,2},{2,3},{3,0},{4,5},{5,6},{6,7},{7,4},{8,9},{9,10},{10,1... | collective-permute-start | bytes 2359304 | tf_op jit(solution)/shard_map/ppermute | solution.py:925
  138.6 18.0 %collective-permute-start.2 = (bf16[512,768]{1,0:T(8,128)(2,1)S(1)}, bf16[512,768]{1,0:T(8,128)(2,1)S(1)}, u32[]{:S(2)}, u32[]{:S(2)}) collective-permute-start(bf16[512,768]{1,0:T(8,128)(2,1)S(1)} %collective-permute-done.1), channel_id=1, source_target_pairs={{0,1},{1,2},{2,3},{3,0},{4,5},{5,6},{6,7},{7,4},{8,9},{9,10},{10,1... | collective-permute-start | bytes 2359304 | tf_op jit(solution)/shard_map/ppermute | solution.py:925
  181.6 9.7 %collective-permute-start.3 = (bf16[1,192,512]{2,0,1:T(2,128)(2,1)S(1)}, bf16[1,192,512]{2,0,1:T(2,128)(2,1)S(1)}, u32[]{:S(2)}, u32[]{:S(2)}) collective-permute-start(bf16[1,192,512]{2,0,1:T(2,128)(2,1)S(1)} %get-tuple-element.89), channel_id=1, source_target_pairs={{0,1},{1,2},{2,3},{3,0},{4,5},{5,6},{6,7},{7,4},{8,9},{9,10},{10,1... | collective-permute-start | bytes 589832 | tf_op jit(solution)/shard_map/ppermute | solution.py:884
  182.2 30.9 %collective-permute-start.4 = (bf16[1,192,512]{2,0,1:T(2,128)(2,1)S(1)}, bf16[1,192,512]{2,0,1:T(2,128)(2,1)S(1)}, u32[]{:S(2)}, u32[]{:S(2)}) collective-permute-start(bf16[1,192,512]{2,0,1:T(2,128)(2,1)S(1)} %get-tuple-element.88), channel_id=1, source_target_pairs={{0,2},{1,3},{2,0},{3,1},{4,6},{5,7},{6,4},{7,5},{8,10},{9,11},{10,... | collective-permute-start | bytes 589832 | tf_op jit(solution)/shard_map/ppermute | solution.py:884
  186.7 33.2 %collective-permute-start.5 = (bf16[1,192,512]{2,0,1:T(2,128)(2,1)S(1)}, bf16[1,192,512]{2,0,1:T(2,128)(2,1)S(1)}, u32[]{:S(2)}, u32[]{:S(2)}) collective-permute-start(bf16[1,192,512]{2,0,1:T(2,128)(2,1)S(1)} %get-tuple-element.87), channel_id=1, source_target_pairs={{0,3},{1,0},{2,1},{3,2},{4,7},{5,4},{6,5},{7,6},{8,11},{9,8},{10,9... | collective-permute-start | bytes 589832 | tf_op jit(solution)/shard_map/ppermute | solution.py:884
  224.2 46.6 %copy-start.18 = (f32[512,768]{1,0:T(8,128)S(1)}, f32[512,768]{1,0:T(8,128)}, u32[]{:S(2)}) copy-start(f32[512,768]{1,0:T(8,128)} %get-tuple-element.91) | copy-start | bytes 4718596
  267.7 9.7 %collective-permute-start.6 = (bf16[1,192,512]{2,0,1:T(2,128)(2,1)}, bf16[1,192,512]{2,0,1:T(2,128)(2,1)}, u32[]{:S(2)}, u32[]{:S(2)}) collective-permute-start(bf16[1,192,512]{2,0,1:T(2,128)(2,1)} %copy.53), channel_id=1, source_target_pairs={{0,1},{1,2},{2,3},{3,0},{4,5},{5,6},{6,7},{7,4},{8,9},{9,10},{10,1... | collective-permute-start | bytes 589832 | tf_op jit(solution)/shard_map/ppermute | solution.py:884
  269.0 31.8 %collective-permute-start.7 = (bf16[1,192,512]{2,0,1:T(2,128)(2,1)}, bf16[1,192,512]{2,0,1:T(2,128)(2,1)}, u32[]{:S(2)}, u32[]{:S(2)}) collective-permute-start(bf16[1,192,512]{2,0,1:T(2,128)(2,1)} %copy.54), channel_id=1, source_target_pairs={{0,2},{1,3},{2,0},{3,1},{4,6},{5,7},{6,4},{7,5},{8,10},{9,11},{10,... | collective-permute-start | bytes 589832 | tf_op jit(solution)/shard_map/ppermute | solution.py:884
  269.3 37.9 %collective-permute-start.8 = (bf16[1,192,512]{2,0,1:T(2,128)(2,1)S(1)}, bf16[1,192,512]{2,0,1:T(2,128)(2,1)}, u32[]{:S(2)}, u32[]{:S(2)}) collective-permute-start(bf16[1,192,512]{2,0,1:T(2,128)(2,1)S(1)} %copy.55), channel_id=1, source_target_pairs={{0,3},{1,0},{2,1},{3,2},{4,7},{5,4},{6,5},{7,6},{8,11},{9,8},{10,9... | collective-permute-start | bytes 589832 | tf_op jit(solution)/shard_map/ppermute | solution.py:884
  314.7 25.8 %copy-start.15 = (bf16[4,512,768]{2,1,0:T(8,128)(2,1)S(1)}, bf16[4,512,768]{2,1,0:T(8,128)(2,1)}, u32[]{:S(2)}) copy-start(bf16[4,512,768]{2,1,0:T(8,128)(2,1)} %copy-done.14) | copy-start | bytes 9437188
  345.8 148.6 %slice-start.2 = ((s8[4718592]{0:T(1024)(128)(4,1)}), s8[4194304]{0:T(1024)(128)(4,1)S(1)}, s32[]{:S(2)}) async-start(s8[4718592]{0:T(1024)(128)(4,1)} %bitcast.90), calls=%async_computation.2 | async-start | bytes 8388608
  351.1 143.3 %slice-start.3 = ((s8[4718592]{0:T(1024)(128)(4,1)}), s8[524288]{0:T(1024)(128)(4,1)S(1)}, s32[]{:S(2)}) async-start(s8[4718592]{0:T(1024)(128)(4,1)} %bitcast.90), calls=%async_computation.3 | async-start | bytes 1048576
  515.1 33.5 %collective-permute-start.9 = (bf16[1,576,512]{2,1,0:T(8,128)(2,1)S(1)}, bf16[1,576,512]{2,1,0:T(8,128)(2,1)}, u32[]{:S(2)}, u32[]{:S(2)}) collective-permute-start(bf16[1,576,512]{2,1,0:T(8,128)(2,1)S(1)} %bitcast.114), channel_id=1, source_target_pairs={{0,1},{1,2},{2,3},{3,0},{4,5},{5,6},{6,7},{7,4},{8,9},{9,10},{10,1... | collective-permute-start | bytes 1769480 | tf_op jit(solution)/shard_map/ppermute | solution.py:884
  515.6 50.4 %collective-permute-start.10 = (bf16[1,576,512]{2,1,0:T(8,128)(2,1)S(1)}, bf16[1,576,512]{2,1,0:T(8,128)(2,1)}, u32[]{:S(2)}, u32[]{:S(2)}) collective-permute-start(bf16[1,576,512]{2,1,0:T(8,128)(2,1)S(1)} %bitcast.113), channel_id=1, source_target_pairs={{0,2},{1,3},{2,0},{3,1},{4,6},{5,7},{6,4},{7,5},{8,10},{9,11},{10,... | collective-permute-start | bytes 1769480 | tf_op jit(solution)/shard_map/ppermute | solution.py:884
  517.7 51.4 %collective-permute-start.11 = (bf16[1,576,512]{2,1,0:T(8,128)(2,1)S(1)}, bf16[1,576,512]{2,1,0:T(8,128)(2,1)S(1)}, u32[]{:S(2)}, u32[]{:S(2)}) collective-permute-start(bf16[1,576,512]{2,1,0:T(8,128)(2,1)S(1)} %bitcast.112), channel_id=1, source_target_pairs={{0,3},{1,0},{2,1},{3,2},{4,7},{5,4},{6,5},{7,6},{8,11},{9,8},{10,9... | collective-permute-start | bytes 1769480 | tf_op jit(solution)/shard_map/ppermute | solution.py:884
  548.4 20.8 %copy-start.27 = (f32[512]{0:T(512)S(1)}, f32[512]{0:T(512)}, u32[]{:S(2)}) copy-start(f32[512]{0:T(512)} %copy-done.26) | copy-start | bytes 6148
  548.5 20.7 %copy-start.4 = (bf16[12,3,64,768]{3,2,1,0:T(8,128)(2,1)S(1)}, bf16[12,3,64,768]{3,2,1,0:T(8,128)(2,1)}, u32[]{:S(2)}) copy-start(bf16[12,3,64,768]{3,2,1,0:T(8,128)(2,1)} %copy-done.1) | copy-start | bytes 10616836
  548.5 20.7 %copy-start.25 = (f32[512]{0:T(512)S(1)}, f32[512]{0:T(512)}, u32[]{:S(2)}) copy-start(f32[512]{0:T(512)} %copy-done.24) | copy-start | bytes 6148
  (30 other events, 117.9 us)

commit v2 on v1

--- a/solution.py
+++ b/solution.py
@@ -370,32 +370,32 @@
 def attend_kernel(block_count, qkv_ref, o_ref, lse_ref):
     for query_block in range(block_count):
         here = slice(query_block * BLOCK, (query_block + 1) * BLOCK)
-        queries = (qkv_ref[0:64, here].astype(F32) * 0.125).astype(BF16)
+        queries = (qkv_ref[0, :, here].astype(F32) * 0.125).astype(BF16)
         peak = jnp.full((1, BLOCK), MASKED, F32)
         total = jnp.zeros((1, BLOCK), F32)
         accum = jnp.zeros((64, BLOCK), F32)
         for key_block in range(query_block + 1):
             there = slice(key_block * BLOCK, (key_block + 1) * BLOCK)
-            logits = matmul(qkv_ref[64:128, there].T, queries)
+            logits = matmul(qkv_ref[1, :, there].T, queries)
             if key_block == query_block:
                 logits = jnp.where(causal_mask(0, BLOCK, BLOCK), logits, MASKED)
             new_peak = jnp.maximum(peak, jnp.max(logits, axis=0, keepdims=True))
             weights = jnp.exp(logits - new_peak)
             factor = jnp.exp(peak - new_peak)
             total = total * factor + jnp.sum(weights, axis=0, keepdims=True)
-            accum = accum * factor + matmul(qkv_ref[128:192, there], weights.astype(BF16))
+            accum = accum * factor + matmul(qkv_ref[2, :, there], weights.astype(BF16))
             peak = new_peak
         o_ref[:, here] = accum / total
         lse_ref[0:1, here] = peak + jnp.log(total)
 
 
 def attend_forward(qkv, heads):
-    length = qkv.shape[1]
+    length = qkv.shape[2]
     pairs = heads * length * (length + BLOCK) // 2
     return pl.pallas_call(
         functools.partial(attend_kernel, length // BLOCK),
         grid=(heads,),
-        in_specs=[pl.BlockSpec((192, length), lambda h: (h, 0))],
+        in_specs=[pl.BlockSpec((3, 64, length), lambda h: (0, h, 0))],
         out_specs=[
             pl.BlockSpec((64, length), lambda h: (h, 0)),
             pl.BlockSpec((8, length), lambda h: (h, 0)),
@@ -416,7 +416,7 @@
     dv_acc[...] = jnp.zeros_like(dv_acc)
     for query_block in range(block_count):
         here = slice(query_block * BLOCK, (query_block + 1) * BLOCK)
-        queries_t = (qkv_ref[0:64, here].astype(F32) * 0.125).astype(BF16)
+        queries_t = (qkv_ref[0, :, here].astype(F32) * 0.125).astype(BF16)
         queries = queries_t.T
         do_t = do_ref[:, here]
         do_rows = do_t.T
@@ -425,30 +425,31 @@
         dq = jnp.zeros((64, BLOCK), F32)
         for key_block in range(query_block + 1):
             there = slice(key_block * BLOCK, (key_block + 1) * BLOCK)
-            keys_t = qkv_ref[64:128, there]
+            keys_t = qkv_ref[1, :, there]
             probs = jnp.exp(matmul(keys_t.T, queries_t) - lse)
             if key_block == query_block:
                 probs = jnp.where(causal_mask(0, BLOCK, BLOCK), probs, 0.0)
-            dprobs = matmul(qkv_ref[128:192, there].T, do_t)
+            dprobs = matmul(qkv_ref[2, :, there].T, do_t)
             dlogits = (probs * (dprobs - delta)).astype(BF16)
             dq = dq + matmul(keys_t, dlogits)
             dv_acc[there, :] += matmul(probs.astype(BF16), do_rows)
             dk_acc[there, :] += matmul(dlogits, queries)
-        d_ref[0:64, here] = (dq * 0.125).astype(BF16)
-    d_ref[64:128, :] = dk_acc[...].T.astype(BF16)
-    d_ref[128:192, :] = dv_acc[...].T.astype(BF16)
+        d_ref[0, :, here] = (dq * 0.125).astype(BF16)
+    d_ref[1] = dk_acc[...].T.astype(BF16)
+    d_ref[2] = dv_acc[...].T.astype(BF16)
 
 
 def attend_backward(qkv, o_t, lse, do_t, heads):
-    length = qkv.shape[1]
+    length = qkv.shape[2]
     pairs = heads * length * (length + BLOCK) // 2
     spec = lambda rows: pl.BlockSpec((rows, length), lambda h: (h, 0))
+    triple = pl.BlockSpec((3, 64, length), lambda h: (0, h, 0))
     return pl.pallas_call(
         functools.partial(attend_back_kernel, length // BLOCK),
         grid=(heads,),
-        in_specs=[spec(192), spec(64), spec(8), spec(64)],
-        out_specs=spec(192),
-        out_shape=jax.ShapeDtypeStruct((heads * 192, length), BF16),
+        in_specs=[triple, spec(64), spec(8), spec(64)],
+        out_specs=triple,
+        out_shape=jax.ShapeDtypeStruct((3, heads * 64, length), BF16),
         scratch_shapes=[pltpu.VMEM((length, 64), F32), pltpu.VMEM((length, 64), F32)],
         compiler_params=pltpu.CompilerParams(vmem_limit_bytes=VMEM_LIMIT),
         cost_estimate=pl.CostEstimate(
@@ -483,8 +484,8 @@
 
 def feed_kernel(steps, chunk, sub, has_partial, *refs):
     names = iter(refs)
-    o_ref, x_ref, dy_ref, ig_ref, fg_ref, hg_ref, wo_t, wo, wu_t, wd, wd_t, wu = [
-        next(names) for _ in range(12)
+    o_ref, x_ref, dy_ref, ig_ref, fg_ref, hg_ref, wo, wu_first, wd, wu_last = [
+        next(names) for _ in range(10)
     ]
     if has_partial:
         part_d, part_u, part_o = [next(names) for _ in range(3)]
@@ -502,7 +503,7 @@
         st[0:1] = average
         st[1:2] = inverse
         dyt_s[...] = dy_ref[...].T
-        h = x_ref[...].T.astype(F32) + matmul(wo_t[...], b)
+        h = x_ref[...].T.astype(F32) + left_t(wo[...], b)
         h_s[...] = h
         average, inverse = column_stats(h)
         st[2:3] = average
@@ -515,7 +516,7 @@
     def _():
         base = pl.multiple_of(step * chunk, chunk)
         for k in range(chunk // sub):
-            z, slope = gelu_both(matmul(wu_t[k * sub : (k + 1) * sub, :], c_s[...]))
+            z, slope = gelu_both(left_t(wu_first[:, k * sub : (k + 1) * sub], c_s[...]))
             n_s[pl.ds(base + k * sub, sub), :] = z
             slope_s[pl.ds(base + k * sub, sub), :] = slope.astype(BF16)
 
@@ -555,9 +556,9 @@
             second = second + jnp.sum(t * n, axis=0, keepdims=True)
             grad = matmul(e, dy_ref[...])
             if has_partial:
-                grad = grad + part_d[rows, :]
-            gd_ref[rows, :] = grad.astype(gd_ref.dtype)
-        out_s[...] += matmul(wd_t[...], jnp.concatenate(pieces, axis=0))
+                grad = grad + part_d[rows, :].astype(F32)
+            gd_ref[rows, :] = grad.astype(BF16)
+        out_s[...] += left_t(wd[...], jnp.concatenate(pieces, axis=0))
         st[6:7] += first
         st[7:8] += second
 
@@ -581,9 +582,9 @@
             pieces.append(du)
             grad = matmul(du, cn_s[...])
             if has_partial:
-                grad = grad + part_u[k * sub : (k + 1) * sub, :]
-            gu_ref[k * sub : (k + 1) * sub, :] = grad.astype(gu_ref.dtype)
-        dc_s[...] += matmul(wu[...], jnp.concatenate(pieces, axis=0))
+                grad = grad + part_u[k * sub : (k + 1) * sub, :].astype(F32)
+            gu_ref[k * sub : (k + 1) * sub, :] = grad.astype(BF16)
+        dc_s[...] += matmul(wu_last[...], jnp.concatenate(pieces, axis=0))
 
     @pl.when(step == 3 * steps - 1)
     def _():
@@ -596,8 +597,8 @@
         dh_ref[...] = dh_rows
         grad = matmul(b_s[...], dh_rows.astype(BF16))
         if has_partial:
-            grad = grad + part_o[...]
-        go_ref[...] = grad.astype(go_ref.dtype)
+            grad = grad + part_o[...].astype(F32)
+        go_ref[...] = grad.astype(BF16)
         n = (o_ref[...].astype(F32) - st[0:1]) * st[1:2]
         t = matmul(wo[...], dh.astype(BF16)) * widened(ig_ref[...], width)
         first = jnp.sum(t, axis=0, keepdims=True) * (1.0 / D)
@@ -616,14 +617,12 @@
     by_rows = lambda phase: pl.BlockSpec((chunk, D), lambda i: (phase(i), 0))
     by_columns = lambda phase: pl.BlockSpec((D, chunk), lambda i: (0, phase(i)))
     in_specs = [once(D, width), once(width, D), once(width, D), once(D, 128), once(D, 128)]
-    in_specs += [pl.BlockSpec((chunk, 128), lambda i: (second(i), 0)), once(D, D), once(D, D)]
-    in_specs += [by_rows(first), by_rows(second), by_columns(second), by_columns(third)]
+    in_specs += [pl.BlockSpec((chunk, 128), lambda i: (second(i), 0)), once(D, D)]
+    in_specs += [by_columns(first), by_rows(second), by_columns(third)]
     args = [o_t, x, dy, *gains, *weights]
-    kind = F32
     if has_partial:
         in_specs += [by_rows(second), by_rows(third), once(D, D)]
         args += list(partial)
-        kind = BF16
     whole = lambda *shape: pl.BlockSpec(shape, lambda i: (0, 0))
     return pl.pallas_call(
         functools.partial(feed_kernel, steps, chunk, sub, has_partial),
@@ -641,9 +640,9 @@
             jax.ShapeDtypeStruct((width, D), BF16),
             jax.ShapeDtypeStruct((width, D), F32),
             jax.ShapeDtypeStruct((D, width), BF16),
-            jax.ShapeDtypeStruct((FF, D), kind),
-            jax.ShapeDtypeStruct((FF, D), kind),
-            jax.ShapeDtypeStruct((D, D), kind),
+            jax.ShapeDtypeStruct((FF, D), BF16),
+            jax.ShapeDtypeStruct((FF, D), BF16),
+            jax.ShapeDtypeStruct((D, D), BF16),
         ],
         scratch_shapes=[
             pltpu.VMEM((D, width), BF16),
@@ -668,40 +667,51 @@
 PIECE = 768
 HALF = PIECE // 2
 COLS = D // 2
-
-
-def sum_kernel(counts, *refs):
-    piece_count = sum(counts)
-    grads = refs[: len(counts)]
-    out_ref, own, r0, r1, r2, r3, r4, fin, own_sem, send_sem, recv_sem, fin_sem = refs[len(counts) :]
+FEED_PIECES = (2 * FF + D) // PIECE
+QKV_PIECES = 3 * D // PIECE
+PIECES = FEED_PIECES + QKV_PIECES
+ATTEND_TICK = 2
+GAP = 0
+
+
+def sum_kernel(*refs):
+    gd, gu, go, gq, do_ref, qkv_ref, o_ref, lse_ref, a_ref, total_ref, back_ref = refs[:11]
+    own, r0, r1, r2, r3, r4, fin, qkv, o_own, lse_own, a_all, gq_own, do_own, d_own = refs[11:25]
+    dk_acc, dv_acc, own_sem, send_sem, recv_sem, fin_sem, in_sem, swap_send, swap_recv = refs[25:]
     r = lax.axis_index("rows")
     s = lax.axis_index("seq")
-    core, xb, yb, z_low, z_high = r % 2, (r // 2) % 2, r // 4, s % 2, s // 2
+    core, xb, yb = r % 2, (r // 2) % 2, r // 4
+    inside = (s == 1) | (s == 2)
+    outside = (s == 0) | (s == 3)
     to_core = (r + 1 - 2 * core, s)
     to_x = (r + 2 - 4 * xb, s)
     to_y = (r + 4 - 8 * yb, s)
-    to_z_low = (r, s + 1 - 2 * z_low)
-    to_z_high = (r, s + 2 - 4 * z_high)
+    to_pair = (r, s + 1 - 2 * (s % 2))
+    to_middle = (r, 3 - s)
+    shifted = [(r, (s + shift) % SEQ) for shift in range(SEQ)]
     barrier = pltpu.get_barrier_semaphore()
-    for device in (to_core, to_x, to_y, to_z_low, to_z_high):
+    for device in (to_core, to_x, to_y, *shifted[1:]):
         pl.semaphore_signal(barrier, inc=1, device_id=device, device_id_type=MESH)
-    pl.semaphore_wait(barrier, 5)
+    pl.semaphore_wait(barrier, 6)
     bits = [(xb, yb), (yb, xb)]
     partners = [(to_x, to_y), (to_y, to_x)]
 
     def rows_at(start, count):
         return pl.ds(pl.multiple_of(start, 16), count)
 
-    def remote(source, target, kind, p, device):
+    def remote(source, target, send, recv, device):
         return pltpu.make_async_remote_copy(
             src_ref=source,
             dst_ref=target,
-            send_sem=send_sem.at[kind, p],
-            recv_sem=recv_sem.at[kind, p],
+            send_sem=send,
+            recv_sem=recv,
             device_id=device,
             device_id_type=MESH,
         )
 
+    def numbered(source, target, kind, p, device):
+        return remote(source, target, send_sem.at[kind, p], recv_sem.at[kind, p], device)
+
     def columns(o):
         return slice(o * COLS, (o + 1) * COLS)
 
@@ -709,69 +719,98 @@
         return bits[o][0] * 192 + bits[o][1] * 96
 
     def core_copy(ref, q, p):
-        return remote(ref.at[rows_at(q * PIECE + (1 - core) * HALF, HALF), :], r0.at[p], 0, p, to_core)
+        part = ref.at[rows_at(q * PIECE + (1 - core) * HALF, HALF), :]
+        return numbered(part, r0.at[p], 0, p, to_core)
 
     def own_copy(ref, q, p):
-        return pltpu.make_async_copy(
-            ref.at[rows_at(q * PIECE + core * HALF, HALF), :], own.at[p], own_sem.at[p]
-        )
+        part = ref.at[rows_at(q * PIECE + core * HALF, HALF), :]
+        return pltpu.make_async_copy(part, own.at[p], own_sem.at[p])
 
     def first_copy(p, o):
         part = own.at[p, rows_at((1 - bits[o][0]) * 192, 192), columns(o)]
-        return remote(part, r1.at[p, o], 1 + o, p, partners[o][0])
+        return numbered(part, r1.at[p, o], 1 + o, p, partners[o][0])
 
     def second_copy(p, o):
         part = own.at[p, rows_at(bits[o][0] * 192 + (1 - bits[o][1]) * 96, 96), columns(o)]
-        return remote(part, r2.at[p, o], 3 + o, p, partners[o][1])
-
-    def low_copy(p, o):
-        part = own.at[p, rows_at(base(o) + (1 - z_low) * 48, 48), columns(o)]
-        return remote(part, r3.at[p, o], 5 + o, p, to_z_low)
-
-    def high_copy(p, o):
-        part = own.at[p, rows_at(base(o) + z_low * 48, 48), columns(o)]
-        return remote(part, r4.at[p, o], 7 + o, p, to_z_high)
+        return numbered(part, r2.at[p, o], 3 + o, p, partners[o][1])
+
+    def pair_copy(p, o):
+        part = own.at[p, rows_at(base(o), 96), columns(o)]
+        return numbered(part, r3.at[p, o], 5 + o, p, to_pair)
+
+    def middle_copy(p, o):
+        part = own.at[p, rows_at(base(o), 96), columns(o)]
+        return numbered(part, r4.at[p, o], 7 + o, p, to_middle)
 
     def region(p, start, count, o):
-        return out_ref.at[rows_at(p * PIECE + core * HALF + start, count), columns(o)]
+        return total_ref.at[rows_at(p * PIECE + core * HALF + start, count), columns(o)]
 
     def fin_copy(p, o):
-        return pltpu.make_async_copy(
-            fin.at[p, o], region(p, base(o) + z_low * 48, 48, o), fin_sem.at[o, p]
-        )
-
-    def low_back(p, o):
-        return remote(fin.at[p, o], region(p, base(o) + z_low * 48, 48, o), 9 + o, p, to_z_low)
+        return pltpu.make_async_copy(fin.at[p, o], region(p, base(o), 96, o), fin_sem.at[o, p])
+
+    def pair_back(p, o):
+        return numbered(fin.at[p, o], region(p, base(o), 96, o), 9 + o, p, to_pair)
 
     def second_back(p, o):
         part = region(p, base(o), 96, o)
-        return remote(part, part, 11 + o, p, partners[o][1])
+        return numbered(part, part, 11 + o, p, partners[o][1])
 
     def first_back(p, o):
         part = region(p, bits[o][0] * 192, 192, o)
-        return remote(part, part, 13 + o, p, partners[o][0])
+        return numbered(part, part, 13 + o, p, partners[o][0])
 
     def core_back(p):
-        part = out_ref.at[rows_at(p * PIECE + core * HALF, HALF), :]
-        return remote(part, part, 15, p, to_core)
-
+        part = total_ref.at[rows_at(p * PIECE + core * HALF, HALF), :]
+        return numbered(part, part, 15, p, to_core)
+
+    def do_copy(shift):
+        part = do_ref.at[(s + shift) % SEQ]
+        if shift == 0:
+            return pltpu.make_async_copy(part, do_own.at[s], in_sem.at[5])
+        return remote(
+            part, do_own.at[s], swap_send.at[0, shift], swap_recv.at[0, shift], shifted[shift]
+        )
+
+    def back_copy(h, shift):
+        part = d_own.at[(s + shift) % SEQ, :, rows_at(h * HEAD_DIM, HEAD_DIM), :]
+        target = back_ref.at[
+            :, rows_at(s * (HEADS_OWN * HEAD_DIM) + h * HEAD_DIM, HEAD_DIM), :
+        ]
+        if shift == 0:
+            return pltpu.make_async_copy(part, target, in_sem.at[6 + h])
+        return remote(
+            part, target, swap_send.at[1 + h, shift], swap_recv.at[1 + h, shift], shifted[shift]
+        )
+
+    loads = [
+        pltpu.make_async_copy(qkv_ref, qkv, in_sem.at[0]),
+        pltpu.make_async_copy(o_ref, o_own, in_sem.at[1]),
+        pltpu.make_async_copy(lse_ref, lse_own, in_sem.at[2]),
+        pltpu.make_async_copy(a_ref, a_all, in_sem.at[3]),
+        pltpu.make_async_copy(gq, gq_own, in_sem.at[4]),
+    ]
+    for shift in range(1, SEQ):
+        do_copy(shift).start()
     offset = 0
-    for ref, count in zip(grads, counts):
+    for ref in (gd, gu, go):
 
         def begin(q, carry, ref=ref, offset=offset):
             core_copy(ref, q, q + offset).start()
             own_copy(ref, q, q + offset).start()
             return carry
 
-        lax.fori_loop(0, count, begin, 0)
-        offset += count
+        lax.fori_loop(0, ref.shape[0] // PIECE, begin, 0)
+        offset += ref.shape[0] // PIECE
+    do_copy(0).start()
+    for load in loads:
+        load.start()
 
     def added(index, other):
         own[index] = (own[index].astype(F32) + other.astype(F32)).astype(BF16)
 
     def after_core(p):
-        own_copy(grads[0], 0, p).wait()
-        core_copy(grads[0], 0, p).wait()
+        own_copy(gd, 0, p).wait()
+        core_copy(gd, 0, p).wait()
         own[p] = (own[p].astype(F32) + r0[p].astype(F32)).astype(BF16)
         for o in range(2):
             first_copy(p, o).start()
@@ -786,26 +825,47 @@
         for o in range(2):
             second_copy(p, o).wait()
             added((p, rows_at(base(o), 96), columns(o)), r2[p, o])
-            low_copy(p, o).start()
-
-    def after_low(p):
+
+            @pl.when(outside)
+            def _():
+                pair_copy(p, o).start()
+
+    def after_pair(p):
         for o in range(2):
-            low_copy(p, o).wait()
-            added((p, rows_at(base(o) + z_low * 48, 48), columns(o)), r3[p, o])
-            high_copy(p, o).start()
-
-    def after_high(p):
+
+            @pl.when(outside)
+            def _():
+                pair_copy(p, o).wait_send()
+
+            @pl.when(inside)
+            def _():
+                pair_copy(p, o).wait_recv()
+                added((p, rows_at(base(o), 96), columns(o)), r3[p, o])
+                middle_copy(p, o).start()
+
+    def after_middle(p):
         for o in range(2):
-            high_copy(p, o).wait()
-            mine = own[p, rows_at(base(o) + z_low * 48, 48), columns(o)].astype(F32)
-            fin[p, o] = (mine + r4[p, o].astype(F32)).astype(BF16)
-            low_back(p, o).start()
-            fin_copy(p, o).start()
-
-    def after_low_back(p):
+
+            @pl.when(inside)
+            def _():
+                middle_copy(p, o).wait()
+                mine = own[p, rows_at(base(o), 96), columns(o)].astype(F32)
+                fin[p, o] = (mine + r4[p, o].astype(F32)).astype(BF16)
+                pair_back(p, o).start()
+                fin_copy(p, o).start()
+
+    def after_pair_back(p):
         for o in range(2):
-            fin_copy(p, o).wait()
-            low_back(p, o).wait()
+
+            @pl.when(inside)
+            def _():
+                fin_copy(p, o).wait()
+                pair_back(p, o).wait_send()
+
+            @pl.when(outside)
+            def _():
+                pair_back(p, o).wait_recv()
+
             second_back(p, o).start()
 
     def after_second_back(p):
@@ -825,65 +885,239 @@
         after_core,
         after_first,
         after_second,
-        after_low,
-        after_high,
-        after_low_back,
+        after_pair,
+        after_middle,
+        after_pair_back,
         after_second_back,
         after_first_back,
         after_core_back,
     ]
 
+    def head_rows(h):
+        return rows_at(h * HEAD_DIM, HEAD_DIM)
+
+    def attend(h, query_block):
+        rows = head_rows(h)
+        here = slice(query_block * BLOCK, (query_block + 1) * BLOCK)
+        queries_t = (qkv[0, rows, here].astype(F32) * 0.125).astype(BF16)
+        queries = queries_t.T
+        do_t = do_own[query_block, rows, :]
+        do_rows = do_t.T
+        lse = lse_own[h, 0:1, here]
+        delta = jnp.sum(do_t.astype(F32) * o_own[rows, here], axis=0, keepdims=True)
+        dq = jnp.zeros((HEAD_DIM, BLOCK), F32)
+        for key_block in range(query_block + 1):
+            there = slice(key_block * BLOCK, (key_block + 1) * BLOCK)
+            keys_t = qkv[1, rows, there]
+            probs = jnp.exp(matmul(keys_t.T, queries_t) - lse)
+            if key_block == query_block:
+                probs = jnp.where(causal_mask(0, BLOCK, BLOCK), probs, 0.0)
+            dprobs = matmul(qkv[2, rows, there].T, do_t)
+            dlogits = (probs * (dprobs - delta)).astype(BF16)
+            dq = dq + matmul(keys_t, dlogits)
+            dv_acc[there, :] += matmul(probs.astype(BF16), do_rows)
+            dk_acc[there, :] += matmul(dlogits, queries)
+        d_own[query_block, 0, rows, :] = (dq * 0.125).astype(BF16)
+
+    def finish_head(h):
+        rows = head_rows(h)
+        total = jnp.zeros((3 * HEAD_DIM, D), F32)
+        for block in range(SEQ):
+            here = slice(block * BLOCK, (block + 1) * BLOCK)
+            d_own[block, 1, rows, :] = dk_acc[here, :].T.astype(BF16)
+            d_own[block, 2, rows, :] = dv_acc[here, :].T.astype(BF16)
+            joined = d_own[block, :, rows, :].reshape(3 * HEAD_DIM, BLOCK)
+            total = total + matmul(joined, a_all[here, :])
+        for part in range(3):
+            place = rows_at(part * D + s * (HEADS_OWN * HEAD_DIM) + h * HEAD_DIM, HEAD_DIM)
+            term = total[part * HEAD_DIM : (part + 1) * HEAD_DIM, :]
+            gq_own[place, :] = (gq_own[place, :].astype(F32) + term).astype(BF16)
+        for shift in range(SEQ):
+            back_copy(h, shift).start()
+
     def tick(t, carry):
         for lag, stage in enumerate(stages):
-            p = t - lag
-
-            @pl.when((p >= 0) & (p < piece_count))
+            v = t - lag
+
+            @pl.when((v >= 0) & ((v < FEED_PIECES) | (v >= FEED_PIECES + GAP)) & (v < PIECES + GAP))
             def _():
-                stage(p)
+                stage(jnp.where(v < FEED_PIECES, v, v - GAP))
+
+        @pl.when(t == ATTEND_TICK)
+        def _():
+            for load in loads:
+                load.wait()
+            for shift in range(SEQ):
+                do_copy(shift).wait()
+
+        turn = t - ATTEND_TICK
+        h = turn // 2
+
+        @pl.when((turn >= 0) & (turn < 2 * HEADS_OWN) & (turn % 2 == 0))
+        def _():
+            dk_acc[...] = jnp.zeros_like(dk_acc)
+            dv_acc[...] = jnp.zeros_like(dv_acc)
+            attend(h, 0)
+            attend(h, 3)
+
+        @pl.when((turn >= 0) & (turn < 2 * HEADS_OWN) & (turn % 2 == 1))
+        def _():
+            attend(h, 1)
+            attend(h, 2)
+            finish_head(h)
+
+        @pl.when(turn == 2 * HEADS_OWN - 1)
+        def _():
+            for q in range(QKV_PIECES):
+                core_copy(gq_own, q, FEED_PIECES + q).start()
+                own_copy(gq_own, q, FEED_PIECES + q).start()
 
         return carry
 
-    lax.fori_loop(0, piece_count + len(stages) - 1, tick, 0)
-
-
-def summed_everywhere(grads, collective_id):
-    counts = [grad.shape[0] // PIECE for grad in grads]
-    n = sum(counts)
+    lax.fori_loop(0, PIECES + GAP + len(stages) - 1, tick, 0)
+    for h in range(HEADS_OWN):
+        for shift in range(SEQ):
+            back_copy(h, shift).wait()
+
+
+def summed_everywhere(gd, gu, go, gq, do_pieces, qkv_own, o_own, lse, a_all, collective_id):
+    n = PIECES
+    length = SEQ * BLOCK
+    own_rows = HEADS_OWN * HEAD_DIM
     dma = pltpu.SemaphoreType.DMA
+    anywhere = pl.BlockSpec(memory_space=pl.ANY)
     return pl.pallas_call(
-        functools.partial(sum_kernel, counts),
-        out_shape=jax.ShapeDtypeStruct((n * PIECE, D), BF16),
-        in_specs=[pl.BlockSpec(memory_space=pl.ANY)] * len(grads),
-        out_specs=pl.BlockSpec(memory_space=pl.ANY),
+        sum_kernel,
+        out_shape=[
+            jax.ShapeDtypeStruct((n * PIECE, D), BF16),
+            jax.ShapeDtypeStruct((3, D, BLOCK), BF16),
+        ],
+        in_specs=[anywhere] * 9,
+        out_specs=[anywhere] * 2,
         scratch_shapes=[
             pltpu.VMEM((n, HALF, D), BF16),
             pltpu.VMEM((n, HALF, D), BF16),
             pltpu.VMEM((n, 2, 192, COLS), BF16),
             pltpu.VMEM((n, 2, 96, COLS), BF16),
-            pltpu.VMEM((n, 2, 48, COLS), BF16),
-            pltpu.VMEM((n, 2, 48, COLS), BF16),
-            pltpu.VMEM((n, 2, 48, COLS), BF16),
+            pltpu.VMEM((n, 2, 96, COLS), BF16),
+            pltpu.VMEM((n, 2, 96, COLS), BF16),
+            pltpu.VMEM((n, 2, 96, COLS), BF16),
+            pltpu.VMEM((3, own_rows, length), BF16),
+            pltpu.VMEM((own_rows, length), F32),
+            pltpu.VMEM((HEADS_OWN, 8, length), F32),
+            pltpu.VMEM((length, D), BF16),
+            pltpu.VMEM((3 * D, D), BF16),
+            pltpu.VMEM((SEQ, own_rows, BLOCK), BF16),
+            pltpu.VMEM((SEQ, 3, own_rows, BLOCK), BF16),
+            pltpu.VMEM((length, HEAD_DIM), F32),
+            pltpu.VMEM((length, HEAD_DIM), F32),
             dma((n,)),
             dma((16, n)),
             dma((16, n)),
             dma((2, n)),
+            dma((6 + HEADS_OWN,)),
+            dma((1 + HEADS_OWN, SEQ)),
+            dma((1 + HEADS_OWN, SEQ)),
         ],
         compiler_params=pltpu.CompilerParams(
             collective_id=collective_id, has_side_effects=True, vmem_limit_bytes=VMEM_LIMIT
         ),
         cost_estimate=pl.CostEstimate(flops=0, bytes_accessed=n * PIECE * D * 64, transcendentals=0),
-    )(*grads)
-
-
-def exchanged(pieces, own_index):
-    out = jnp.zeros_like(pieces)
-    own = lax.dynamic_index_in_dim(pieces, own_index, 0, keepdims=True)
-    out = lax.dynamic_update_slice_in_dim(out, own, own_index, 0)
-    for shift in range(1, SEQ):
-        leaving = lax.dynamic_index_in_dim(pieces, (own_index + shift) % SEQ, 0, keepdims=True)
-        arrived = lax.ppermute(leaving, "seq", [(i, (i + shift) % SEQ) for i in range(SEQ)])
-        out = lax.dynamic_update_slice_in_dim(out, arrived, (own_index - shift) % SEQ, 0)
-    return out
+    )(gd, gu, go, gq, do_pieces, qkv_own, o_own, lse, a_all)
+
+
+def by_block(relative, place):
+    blocks = [lax.dynamic_index_in_dim(relative, (place - j) % SEQ, 0) for j in range(SEQ)]
+    return jnp.concatenate(blocks, axis=0)
+
+
+def shifted_by(value, shift):
+    return lax.ppermute(value, "seq", [(i, (i + shift) % SEQ) for i in range(SEQ)])
+
+
+FINISH = PIECES
+
+
+def finish_kernel(total, wd, wu, wo, wq, ig, fg, hg, ag, gd, gu, go, gq, si, sf, sh, sa, acc):
+    step = pl.program_id(0)
+
+    def lanes(values):
+        folded = values[:, 0:128]
+        for k in range(1, D // 128):
+            folded = folded + values[:, k * 128 : (k + 1) * 128]
+        return folded
+
+    def as_row(folded):
+        return jnp.sum(folded.T, axis=0, keepdims=True)
+
+    @pl.when(step < 4)
+    def _():
+        grad = total[...].astype(F32)
+        gd[...] = grad
+        sh[...] = as_row(lanes(grad * wd[...].astype(F32))) / hg[...]
+
+    @pl.when((step >= 4) & (step < 8))
+    def _():
+        grad = total[...].T.astype(F32)
+        gu[...] = grad
+        acc[0] = lanes(grad * wu[...].astype(F32)) + jnp.where(step == 4, 0.0, acc[0])
+
+    @pl.when(step == 8)
+    def _():
+        sf[...] = as_row(acc[0]) / fg[...]
+        grad = total[...].astype(F32)
+        go[...] = grad
+        si[...] = as_row(lanes(grad * wo[...].astype(F32))) / ig[...]
+
+    @pl.when(step >= 9)
+    def _():
+        grad = total[...].T.astype(F32)
+        gq[...] = grad
+        acc[1] = lanes(grad * wq[...].astype(F32)) + jnp.where(step == 9, 0.0, acc[1])
+
+    @pl.when(step == 11)
+    def _():
+        sa[...] = as_row(acc[1]) / ag[...]
+
+
+def finished(total, down_weight, up_weight, out_weight, query_key_value, gains):
+    square = lambda index: pl.BlockSpec((D, D), index)
+    row = lambda index: pl.BlockSpec((1, D), index)
+    at_down = lambda i: (jnp.clip(i, 0, 3), 0)
+    at_up = lambda i: (0, jnp.clip(i - 4, 0, 3))
+    at_qkv = lambda i: (0, jnp.clip(i - 9, 0, 2))
+    still = lambda i: (0, 0)
+    hidden = lambda i: (0, jnp.clip(i, 0, 3))
+    shapes = [(FF, D), (D, FF), (D, D), (D, 3 * D), (1, D), (1, D), (1, FF), (1, D)]
+    return pl.pallas_call(
+        finish_kernel,
+        grid=(FINISH,),
+        in_specs=[
+            square(lambda i: (i, 0)),
+            square(at_down),
+            square(at_up),
+            square(still),
+            square(at_qkv),
+            row(still),
+            row(still),
+            row(hidden),
+            row(still),
+        ],
+        out_specs=[
+            square(at_down),
+            square(at_up),
+            square(still),
+            square(at_qkv),
+            row(still),
+            row(still),
+            row(hidden),
+            row(still),
+        ],
+        out_shape=[jax.ShapeDtypeStruct(shape, F32) for shape in shapes],
+        scratch_shapes=[pltpu.VMEM((2, D, 128), F32)],
+        compiler_params=pltpu.CompilerParams(vmem_limit_bytes=VMEM_LIMIT),
+        cost_estimate=pl.CostEstimate(flops=10**8, bytes_accessed=56 * 2**20, transcendentals=0),
+    )(total, down_weight, up_weight, out_weight, query_key_value, *[g[None] for g in gains])
 
 
 def normed_rows(x, gain):
@@ -919,59 +1153,76 @@
     x_pack = jnp.where(long_first, tokens[1], tokens[0])
     dy_long = jnp.where(long_first, cotangent[0], cotangent[1])
     dy_pack = jnp.where(long_first, cotangent[1], cotangent[0])
-    ring = [(i, (i + 1) % SEQ) for i in range(SEQ)]
-    x_blocks = [x_long]
-    for _ in range(1, SEQ):
-        x_blocks.append(lax.ppermute(x_blocks[-1], "seq", ring))
-    qkv_t = query_key_value.reshape(D, 3, HEADS, HEAD_DIM).transpose(2, 1, 3, 0).reshape(3 * D, D)
+    x_blocks = [x_long] + [shifted_by(x_long, shift) for shift in range(1, SEQ)]
     wide = lambda gain: jnp.broadcast_to(gain[:, None], (gain.shape[0], 128))
     gains = (wide(inner_gain), wide(feed_gain), wide(hidden_gain))
-    weights = (out_weight.T, out_weight, up_weight.T, down_weight, down_weight.T, up_weight)
+    weights = (out_weight, up_weight, down_weight, up_weight)
     a_pack, pack_normed, pack_inverse = normed_rows(x_pack, attend_gain)
-    qkv_pack = right_t(qkv_t, a_pack).astype(BF16)
+    qkv_pack = lax.dot_general(
+        query_key_value, a_pack, (((0,), (1,)), ((), ())), preferred_element_type=F32
+    )
+    qkv_pack = qkv_pack.astype(BF16).reshape(3, D, BLOCK)
     o_pack, lse_pack = attend_forward(qkv_pack, HEADS)
     out_pack, dh_pack, do_pack, gd_pack, gu_pack, go_pack = feed_both(
         o_pack, x_pack, dy_pack, gains, weights
     )
-    dqkv_pack = attend_backward(qkv_pack, o_pack, lse_pack, do_pack, HEADS)
-    gq_pack = matmul(dqkv_pack, a_pack)
-    dxa_pack = layer_back(left_t(dqkv_pack, qkv_t), pack_normed, pack_inverse, attend_gain)
+    *x_blocks, do_pack = lax.optimization_barrier((*x_blocks, do_pack))
+    own_rows = HEADS_OWN * HEAD_DIM
+    w_own = lax.dynamic_slice_in_dim(
+        query_key_value.reshape(D, 3, D), place * own_rows, own_rows, 2
+    ).reshape(D, 3 * own_rows)
+    x_all = by_block(jnp.stack(x_blocks), place).reshape(SEQ * BLOCK, D)
+    a_all, _, _ = normed_rows(x_all, attend_gain)
+    qkv_long = lax.dot_general(w_own, a_all, (((0,), (1,)), ((), ())), preferred_element_type=F32)
+    qkv_long = qkv_long.astype(BF16).reshape(3, own_rows, SEQ * BLOCK)
+    o_long, lse_long = attend_forward(qkv_long, HEADS_OWN)
+    o_low = o_long.astype(BF16)
+    o_parts = []
+    for shift in range(SEQ):
+        leaving = lax.dynamic_slice_in_dim(o_low, ((place + shift) % SEQ) * BLOCK, BLOCK, 1)
+        o_parts.append(shifted_by(leaving, shift) if shift else leaving)
+    do_pack, _ = lax.optimization_barrier((do_pack, o_low))
+    dqkv_pack = attend_backward(qkv_pack, o_pack, lse_pack, do_pack, HEADS).reshape(3 * D, BLOCK)
+    gq_pack = matmul(dqkv_pack, a_pack).astype(BF16)
+    dxa_pack = layer_back(
+        left_t(dqkv_pack, query_key_value.T), pack_normed, pack_inverse, attend_gain
+    )
     dx_pack = (dh_pack + dxa_pack).astype(BF16)
-    own_t = lax.dynamic_slice_in_dim(qkv_t, place * GROUP, GROUP, 0)
-    a_all = jnp.zeros((SEQ, BLOCK, D), BF16)
-    for shift, block in enumerate(x_blocks):
-        a_block, normed, inverse = normed_rows(block, attend_gain)
-        if shift == 0:
-            long_normed, long_inverse = normed, inverse
-        a_all = lax.dynamic_update_slice_in_dim(a_all, a_block[None], (place - shift) % SEQ, 0)
-    a_all = a_all.reshape(SEQ * BLOCK, D)
-    qkv_long = right_t(own_t, a_all).astype(BF16)
-    o_long, lse_long = attend_forward(qkv_long, HEADS_OWN)
-    o_pieces = o_long.astype(BF16).reshape(HEADS_OWN * HEAD_DIM, SEQ, BLOCK).transpose(1, 0, 2)
-    o_mine = exchanged(o_pieces, place).reshape(D, BLOCK)
+    *o_parts, gq_pack, dx_pack = lax.optimization_barrier((*o_parts, gq_pack, dx_pack))
+    o_mine = by_block(jnp.stack(o_parts), place).reshape(D, BLOCK)
     out_long, dh_long, do_long, gd, gu, go = feed_both(
         o_mine, x_long, dy_long, gains, weights, (gd_pack, gu_pack, go_pack)
     )
-    do_own = exchanged(do_long.reshape(SEQ, HEADS_OWN * HEAD_DIM, BLOCK), place)
-    do_own = do_own.transpose(1, 0, 2).reshape(HEADS_OWN * HEAD_DIM, SEQ * BLOCK)
-    dqkv_own = attend_backward(qkv_long, o_long, lse_long, do_own, HEADS_OWN)
-    gq_long = matmul(dqkv_own, a_all)
-    gq_own = lax.dynamic_slice_in_dim(gq_pack, place * GROUP, GROUP, 0) + gq_long
-    gq = lax.dynamic_update_slice_in_dim(gq_pack, gq_own, place * GROUP, 0).astype(BF16)
-    dqkv_long = exchanged(dqkv_own.reshape(GROUP, SEQ, BLOCK).transpose(1, 0, 2), place)
-    dqkv_long = dqkv_long.reshape(3 * D, BLOCK)
-    dxa_long = layer_back(left_t(dqkv_long, qkv_t), long_normed, long_inverse, attend_gain)
+    total, dqkv_long = summed_everywhere(
+        gd,
+        gu,
+        go,
+        gq_pack,
+        do_long.reshape(SEQ, own_rows, BLOCK),
+        qkv_long,
+        o_long,
+        lse_long.reshape(HEADS_OWN, 8, SEQ * BLOCK),
+        a_all,
+        0,
+    )
+    _, long_normed, long_inverse = normed_rows(x_long, attend_gain)
+    dxa_long = layer_back(
+        left_t(dqkv_long.reshape(3 * D, BLOCK), query_key_value.T),
+        long_normed,
+        long_inverse,
+        attend_gain,
+    )
     dx_long = (dh_long + dxa_long).astype(BF16)
-    total = summed_everywhere((gd, gu, go, gq), 0)
-    down_grad = total[:FF].astype(F32)
-    up_grad_t = total[FF : 2 * FF].astype(F32)
-    out_grad = total[2 * FF : 2 * FF + D].astype(F32)
-    qkv_grad_t = total[2 * FF + D :].astype(F32)
-    qkv_grad = qkv_grad_t.reshape(HEADS, 3, HEAD_DIM, D).transpose(3, 1, 0, 2).reshape(D, 3 * D)
-    attend_total = jnp.sum(qkv_grad_t * qkv_t.astype(F32), axis=0) / attend_gain
-    inner_total = jnp.sum(out_grad * out_weight.astype(F32), axis=1) / inner_gain
-    feed_total = jnp.sum(up_grad_t * weights[2].astype(F32), axis=0) / feed_gain
-    hidden_total = jnp.sum(down_grad * down_weight.astype(F32), axis=1) / hidden_gain
+    down_grad, up_grad, out_grad, qkv_grad, inner_total, feed_total, hidden_total, attend_total = (
+        finished(
+            total,
+            down_weight,
+            up_weight,
+            out_weight,
+            query_key_value,
+            (inner_gain, feed_gain, hidden_gain, attend_gain),
+        )
+    )
     output = jnp.where(long_first, jnp.stack([out_long, out_pack]), jnp.stack([out_pack, out_long]))
     tokens_grad = jnp.where(long_first, jnp.stack([dx_long, dx_pack]), jnp.stack([dx_pack, dx_long]))
     return (
@@ -979,12 +1230,12 @@
         tokens_grad,
         qkv_grad,
         out_grad,
-        up_grad_t.T,
+        up_grad,
         down_grad,
-        attend_total,
-        inner_total,
-        feed_total,
-        hidden_total,
+        attend_total[0],
+        inner_total[0],
+        feed_total[0],
+        hidden_total[0],
     )
 
 

time: 585 us -> 392 us (0.67)
  local copies, waits for them, and re-layouts: 111 us -> 18.3 us
  waiting for transfers between devices: 89.6 us -> 9.36 us
  other arithmetic: 56.3 us -> 24.7 us
  Pallas kernels: 277 us -> 303 us
  matrix products: 27 us -> 20.3 us
    ppermute x12 -> x6, waiting for transfers between devices: 89.6 us -> 9.36 us  [shifted_by(): lax.ppermute(value, 'seq', [(i, (i + shift) % SEQ) for i in range(SEQ)])]
    pallas_call x1 -> x2, Pallas kernels: 130 us -> 188 us  [the longest x1 163 us: summed_everywhere(): pl.pallas_call(sum_kernel, out_shape=[jax.ShapeDtypeStruct((n * PIECE, D)...]
    unnamed x98 -> x39, local copies, waits for them, and re-layouts: 48.7 us -> 5.84 us
    dynamic_update_slice x13 -> x0, local copies, waits for them, and re-layouts: 39.3 us -> none  [the longest x10 32.5 us: exchanged(): lax.dynamic_update_slice_in_dim(out, arrived, (own_index - shift) % SEQ, 0)]
    pallas_call x2 -> x1, Pallas kernels: 41.3 us -> 15.4 us  [attend_backward(): pl.pallas_call(functools.partial(attend_back_kernel, length // BLOCK), gr...]
    reduce_sum x3 -> x0, other arithmetic: 12.1 us -> none  [the longest x1 6.77 us: split_layer(): jnp.sum(down_grad * down_weight.astype(F32), axis=1) / hidden_gain]
    reshape x3 -> x0, local copies, waits for them, and re-layouts: 9.09 us -> none  [the longest x1 5.08 us: split_layer(): dqkv_own.reshape(GROUP, SEQ, BLOCK).transpose(1, 0, 2)]
    transpose x1 -> x0, other arithmetic: 8.01 us -> none  [split_layer(): return (output, tokens_grad, qkv_grad, out_grad, up_grad_t.T, down_grad,...]
  transfers between devices with their start and end apart: 12 -> 6, of which waited for: 9 -> 2; matrix products, arithmetic and copies ran while one was open for 19% -> 7% of each run, Pallas kernels for 11% -> 12%
where the time goes in v2:
time: 392 us; the launch traced here: 386 us
  Pallas kernels  303 us (77%)
  other arithmetic  24.7 us (6%)
  matrix products  20.3 us (5%)
  local copies, waits for them, and re-layouts  18.3 us (5%)
  waiting for transfers between devices  9.36 us (2%)
  starting transfers between devices  8.03 us (2%)
    pallas_call x1, Pallas kernels, summed_everywhere(): pl.pallas_call(sum_kernel, out_shape=[jax.ShapeDtypeStruct((n * PIECE, D)...  163 us
    pallas_call x2, Pallas kernels, feed_both(): pl.pallas_call(functools.partial(feed_kernel, steps, chunk, sub, has_part...  73.6 us
    pallas_call x2, Pallas kernels, attend_forward(): pl.pallas_call(functools.partial(attend_kernel, length // BLOCK), grid=(h...  25.9 us
    pallas_call x1, Pallas kernels, finished(): pl.pallas_call(finish_kernel, grid=(FINISH,), in_specs=[square(lambda i:...  24.9 us
    pallas_call x1, Pallas kernels, attend_backward(): pl.pallas_call(functools.partial(attend_back_kernel, length // BLOCK), gr...  15.4 us
    ppermute x6, waiting for transfers between devices, shifted_by(): lax.ppermute(value, 'seq', [(i, (i + shift) % SEQ) for i in range(SEQ)])  9.36 us
    dot_general x2, matrix products, left_t(): lax.dot_general(left, right, (((0,), (0,)), ((), ())), preferred_element_...  9.27 us
    ppermute x6, starting transfers between devices, shifted_by(): lax.ppermute(value, 'seq', [(i, (i + shift) % SEQ) for i in range(SEQ)])  8.03 us
  transfers between devices with their start and end apart: 6, of which 2 were waited for; matrix products, arithmetic and copies ran while one was open for 7% of the time, Pallas kernels for 12%

profile of v2, /device:TPU:9, one launch (start us, length us, event | category | flops | bytes accessed | tf_op | source)
XLA Modules:
  0.0 385.7 jit_solution(16365729025344942295)
XLA Ops:
  2.7 2.0 convert_reduce_fusion.1
  4.8 2.5 collective-permute-start.1
  7.3 2.2 collective-permute-start
  11.1 3.6 fusion.3
  14.7 4.3 %copy.23 = bf16[2304,512]{1,0:T(8,128)(2,1)} copy(bf16[2304,512]{0,1:T(8,128)(2,1)} %fusion.3) | data formatting | bytes 4718592 | tf_op jit(solution)/shard_map/convert_element_type | solution.py:1164
  19.0 10.8 %shard_map.186 = (f32[768,512]{1,0:T(8,128)}, f32[96,512]{1,0:T(8,128)}) custom-call(bf16[3,768,512]{2,1,0:T(8,128)(2,1)} %bitcast.67), custom_call_target="tpu_custom_call" | custom-call | flops 3221225472 | bytes 4300800 | tf_op jit(solution)/shard_map/pallas_call | solution.py:395
  33.2 36.0 %shard_map.187 = (bf16[512,768]{1,0:T(8,128)(2,1)}, f32[512,768]{1,0:T(8,128)}, bf16[768,512]{1,0:T(8,128)(2,1)}, bf16[3072,768]{1,0:T(8,128)(2,1)}, bf16[3072,7...) custom-call(f32[768,512]{1,0:T(8,128)} %get-tuple-element.48.refs_0_.o_ref, bf16[512,768]{1,0:T(8,128)(2,1)} %copy-done.5, ...), custom_call_target="tpu_custom_call" | custom-call | flops 16307453952 | bytes 83886080 | tf_op jit(solution)/shard_map/pallas_call | solution.py:627
  71.1 5.7 %copy.22 = bf16[768,2304]{0,1:T(8,128)(2,1)} copy(bf16[768,2304]{1,0:T(8,128)(2,1)} %wq.1) | data formatting | bytes 7077888 | tf_op args[3]
  78.5 2.0 pad_maximum_fusion
  83.9 3.4 convolution_convert_fusion.2
  87.3 15.1 %shard_map.188 = (f32[192,2048]{1,0:T(8,128)}, f32[24,2048]{1,0:T(8,128)}) custom-call(bf16[3,192,2048]{2,1,0:T(8,128)(2,1)} %bitcast.69), custom_call_target="tpu_custom_call" | custom-call | flops 8053063680 | bytes 4300800 | tf_op jit(solution)/shard_map/pallas_call | solution.py:395
  104.0 15.4 %shard_map.189 = bf16[3,768,512]{2,1,0:T(8,128)(2,1)} custom-call(bf16[3,768,512]{2,1,0:T(8,128)(2,1)} %bitcast.68, f32[768,512]{1,0:T(8,128)} %get-tuple-element.48.refs_0_.o_ref, f32[96,512]{1,0:T(8,128)} %get-tuple-element.55.lse_ref, bf16[768,512]{1,0:T(8,128)(2,1)} %get-tuple-element.57.do_ref), custom_call_target="tpu_custom_call" | custom-call | flops 6442450944 | bytes 7987200 | tf_op jit(solution)/shard_map/pallas_call | solution.py:447
  119.4 4.2 %fusion.40 = (f32[512]{0:T(512)S(1)}, f32[512]{0:T(512)S(1)}, f32[512,768]{1,0:T(8,128)S(1)}) fusion(f32[512]{0:T(512)S(1)} %add_rsqrt_fusion.2, f32[512]{0:T(512)S(1)} %broadcast_multiply_fusion.6, bf16[512,768]{1,0:T(8,128)(2,1)S(1)} %copy-done.6, f32[768]{0:T(1024)S(1)} %copy-done.14, bf16[2304,512]{1,0:T(8,128)(2,1)} %bitcast.87, ...), kind=kOutput, calls=%fused_computation.85 | convolution fusion | flops 1814690816 | bytes 8268800 | tf_op jit(solution)/shard_map/dot_general | solution.py:59
  123.6 4.0 %convolution_convert_fusion.refs_3_ = bf16[2304,768]{1,0:T(8,128)(2,1)} fusion(bf16[2304,512]{1,0:T(8,128)(2,1)S(1)} %bitcast.88, f32[768]{0:T(1024)S(1)} %copy-done.14, f32[512]{0:T(512)S(1)} %add_rsqrt_fusion.2, f32[512]{0:T(512)S(1)} %broadcast_multiply_fusion.6, pred[]{:T(512)} %bitcast, bf16[2,512,768]{2,1,0:T(8,128)(2,1)S(1)} %copy-done.8), kind=kOutput, calls=%fused_computation.7 | convolution fusion | flops 1816068096 | bytes 7478273 | tf_op jit(solution)/shard_map/dot_general | solution.py:55
  128.9 2.1 collective-permute-start.3
  131.0 4.6 %fusion.2.refs_8_ = bf16[2048,768]{1,0:T(8,128)(2,1)} fusion(f32[768]{0:T(1024)S(1)} %copy-done.14, f32[2048]{0:T(1024)S(1)} %bitcast.84, f32[2048]{0:T(1024)S(1)} %bitcast.83, bf16[1,512,768]{2,1,0:T(8,128)(2,1)S(1)} %get-tuple-element.95, bf16[1,512,768]{2,1,0:T(8,128)(2,1)S(1)} %get-tuple-element.96, bf16[1,512,768]{2,1,0:T(8,128)(2,1)S(1)} %get-tuple-element.97, ...), kind=kLoop, calls=%fused_computation.3 | loop fusion | flops 12582912 | bytes 6310912 | tf_op jit(solution)/shard_map/convert_element_type | solution.py:1125
  136.2 5.1 %collective-permute-done.4 = bf16[192,512]{1,0:T(8,128)(2,1)S(1)} collective-permute-done((bf16[192,512]{1,0:T(8,128)(2,1)S(1)}, bf16[192,512]{1,0:T(8,128)(2,1)S(1)}, u32[]{:S(2)}, u32[]{:S(2)}) %collective-permute-start.4) | collective-permute-done | bytes 196640 | tf_op jit(solution)/shard_map/ppermute | solution.py:1035
  141.3 4.2 %collective-permute-done.3 = bf16[192,512]{1,0:T(8,128)(2,1)S(1)} collective-permute-done((bf16[192,512]{1,0:T(8,128)(2,1)S(1)}, bf16[192,512]{1,0:T(8,128)(2,1)S(1)}, u32[]{:S(2)}, u32[]{:S(2)}) %collective-permute-start.3) | collective-permute-done | bytes 196640 | tf_op jit(solution)/shard_map/ppermute | solution.py:1035
  146.8 37.6 %shard_map.190 = (bf16[512,768]{1,0:T(8,128)(2,1)}, f32[512,768]{1,0:T(8,128)}, bf16[768,512]{1,0:T(8,128)(2,1)}, bf16[3072,768]{1,0:T(8,128)(2,1)}, bf16[3072,7...) custom-call(bf16[768,512]{1,0:T(8,128)(2,1)} %bitcast.77, bf16[512,768]{1,0:T(8,128)(2,1)} %copy-done.3, ...), custom_call_target="tpu_custom_call" | custom-call | flops 16307453952 | bytes 83886080 | tf_op jit(solution)/shard_map/pallas_call | solution.py:627
  184.4 163.2 %shard_map.191 = (bf16[9216,768]{1,0:T(8,128)(2,1)}, bf16[3,768,512]{2,1,0:T(8,128)(2,1)}) custom-call(bf16[3072,768]{1,0:T(8,128)(2,1)} %get-tuple-element.69.refs_0_, bf16[3072,768]{1,0:T(8,128)(2,1)} %get-tuple-element.70.refs_1_, bf16[768,768]{1,0:T(8,128)(2,1)} %get-tuple-element.71.refs_2_, bf16[2304,768]{1,0:T(8,128)(2,1)} %convolution_convert_fusion.refs_3_, ...), custom_call_target="tpu_custom_call" | custom-call | bytes 452984832 | tf_op jit(solution)/shard_map/pallas_call | solution.py:989
  347.7 5.1 %fusion.39 = (f32[512]{0:T(512)S(1)}, f32[512]{0:T(512)S(1)}, f32[512,768]{1,0:T(8,128)}) fusion(f32[512]{0:T(512)S(1)} %add_rsqrt_fusion.1, f32[512]{0:T(512)S(1)} %broadcast_multiply_fusion.3, bf16[512,768]{1,0:T(8,128)(2,1)S(1)} %copy-done.4, f32[768]{0:T(1024)S(1)} %copy-done.14, bf16[2304,512]{1,0:T(8,128)(2,1)} %bitcast.85, ...), kind=kOutput, calls=%fused_computation.84 | convolution fusion | flops 1814690816 | bytes 8268800 | tf_op jit(solution)/shard_map/dot_general | solution.py:59
  352.8 24.9 %shard_map.192 = (f32[3072,768]{1,0:T(8,128)}, f32[768,3072]{1,0:T(8,128)}, f32[768,768]{1,0:T(8,128)}, f32[768,2304]{1,0:T(8,128)}, f32[1,768]{1,0:T(1,128)}, /...) custom-call(bf16[9216,768]{1,0:T(8,128)(2,1)} %get-tuple-element.77.total, bf16[3072,768]{1,0:T(8,128)(2,1)} %wd.1, ...), custom_call_target="tpu_custom_call" | custom-call | flops 100000000 | bytes 58720256 | tf_op jit(solution)/shard_map/pallas_call | solution.py:1092
  381.5 2.0 fusion.29
  383.5 1.9 maximum_select_fusion
  (79 shorter events, 21.7 us)
Async XLA Ops:
  0.6 8.8 %copy-start.7 = (bf16[2,512,768]{2,1,0:T(8,128)(2,1)S(1)}, bf16[2,512,768]{2,1,0:T(8,128)(2,1)}, u32[]{:S(2)}) copy-start(bf16[2,512,768]{2,1,0:T(8,128)(2,1)} %param.13) | copy-start | bytes 4718596
  4.7 10.0 %copy-start.5 = (bf16[512,768]{1,0:T(8,128)(2,1)}, bf16[512,768]{1,0:T(8,128)(2,1)S(1)}, u32[]{:S(2)}) copy-start(bf16[512,768]{1,0:T(8,128)(2,1)S(1)} %get-tuple-element.101.refs_1_) | copy-start | bytes 2359300
  4.7 73.8 %copy-start.3 = (bf16[512,768]{1,0:T(8,128)(2,1)}, bf16[512,768]{1,0:T(8,128)(2,1)S(1)}, u32[]{:S(2)}) copy-start(bf16[512,768]{1,0:T(8,128)(2,1)S(1)} %get-tuple-element.50.refs_1_) | copy-start | bytes 2359300
  4.7 6.4 %copy-start = (bf16[768,2304]{1,0:T(8,128)(2,1)S(1)}, bf16[768,2304]{1,0:T(8,128)(2,1)}, u32[]{:S(2)}) copy-start(bf16[768,2304]{1,0:T(8,128)(2,1)} %wq.1) | copy-start | bytes 10616836
  4.7 6.4 %copy-start.14 = (f32[768]{0:T(1024)S(1)}, f32[768]{0:T(1024)}, u32[]{:S(2)}) copy-start(f32[768]{0:T(1024)} %param.18) | copy-start | bytes 9220
  4.8 73.7 %collective-permute-start.2 = (bf16[512,768]{1,0:T(8,128)(2,1)S(1)}, bf16[512,768]{1,0:T(8,128)(2,1)S(1)}, u32[]{:S(2)}, u32[]{:S(2)}) collective-permute-start(bf16[512,768]{1,0:T(8,128)(2,1)S(1)} %get-tuple-element.50.refs_1_), channel_id=1, source_target_pairs={{0,3},{1,0},{2,1},{3,2},{4,7},{5,4},{6,5},{7,6},{8,11},{9,8},{10,9... | collective-permute-start | bytes 2359304 | tf_op jit(solution)/shard_map/ppermute | solution.py:1035
  4.8 73.7 %collective-permute-start.1 = (bf16[512,768]{1,0:T(8,128)(2,1)S(1)}, bf16[512,768]{1,0:T(8,128)(2,1)}, u32[]{:S(2)}, u32[]{:S(2)}) collective-permute-start(bf16[512,768]{1,0:T(8,128)(2,1)S(1)} %get-tuple-element.50.refs_1_), channel_id=1, source_target_pairs={{0,2},{1,3},{2,0},{3,1},{4,6},{5,7},{6,4},{7,5},{8,10},{9,11},{10,... | collective-permute-start | bytes 2359304 | tf_op jit(solution)/shard_map/ppermute | solution.py:1035
  7.3 71.2 %collective-permute-start = (bf16[512,768]{1,0:T(8,128)(2,1)S(1)}, bf16[512,768]{1,0:T(8,128)(2,1)}, u32[]{:S(2)}, u32[]{:S(2)}) collective-permute-start(bf16[512,768]{1,0:T(8,128)(2,1)S(1)} %get-tuple-element.50.refs_1_), channel_id=1, source_target_pairs={{0,1},{1,2},{2,3},{3,0},{4,5},{5,6},{6,7},{7,4},{8,9},{9,10},{10,1... | collective-permute-start | bytes 2359304 | tf_op jit(solution)/shard_map/ppermute | solution.py:1035
  19.0 10.8 %copy-start.15 = (f32[768]{0:T(1024)S(1)}, f32[768]{0:T(1024)}, u32[]{:S(2)}) copy-start(f32[768]{0:T(1024)} %param.19) | copy-start | bytes 9220
  19.0 11.7 %copy-start.16 = (f32[768]{0:T(1024)S(1)}, f32[768]{0:T(1024)}, u32[]{:S(2)}) copy-start(f32[768]{0:T(1024)} %param.20) | copy-start | bytes 9220
  19.0 12.7 %copy-start.13 = (f32[3072]{0:T(1024)S(1)}, f32[3072]{0:T(1024)}, u32[]{:S(2)}) copy-start(f32[3072]{0:T(1024)} %param.21) | copy-start | bytes 36868
  104.0 15.4 %copy-start.1 = (bf16[768,2304]{1,0:T(8,128)(2,1)S(1)}, bf16[768,2304]{1,0:T(8,128)(2,1)}, u32[]{:S(2)}) copy-start(bf16[768,2304]{1,0:T(8,128)(2,1)} %wq.1) | copy-start | bytes 10616836
  104.0 15.4 %copy-start.6 = (bf16[512,768]{1,0:T(8,128)(2,1)S(1)}, bf16[512,768]{1,0:T(8,128)(2,1)}, u32[]{:S(2)}) copy-start(bf16[512,768]{1,0:T(8,128)(2,1)} %copy-done.5) | copy-start | bytes 2359300
  119.3 4.2 %copy-start.8 = (bf16[2,512,768]{2,1,0:T(8,128)(2,1)S(1)}, bf16[2,512,768]{2,1,0:T(8,128)(2,1)}, u32[]{:S(2)}) copy-start(bf16[2,512,768]{2,1,0:T(8,128)(2,1)} %param.11) | copy-start | bytes 4718596
  119.4 4.2 %copy-start.17 = (bf16[3,768,512]{2,1,0:T(8,128)(2,1)S(1)}, bf16[3,768,512]{2,1,0:T(8,128)(2,1)}, u32[]{:S(2)}) copy-start(bf16[3,768,512]{2,1,0:T(8,128)(2,1)} %shard_map.189) | copy-start | bytes 7077892
  127.7 8.5 %collective-permute-start.5 = (bf16[192,512]{1,0:T(8,128)(2,1)S(1)}, bf16[192,512]{1,0:T(8,128)(2,1)S(1)}, u32[]{:S(2)}, u32[]{:S(2)}) collective-permute-start(bf16[192,512]{1,0:T(8,128)(2,1)S(1)} %get-tuple-element.106), channel_id=1, source_target_pairs={{0,3},{1,0},{2,1},{3,2},{4,7},{5,4},{6,5},{7,6},{8,11},{9,8},{10,9... | collective-permute-start | bytes 589832 | tf_op jit(solution)/shard_map/ppermute | solution.py:1035
  127.8 13.6 %collective-permute-start.4 = (bf16[192,512]{1,0:T(8,128)(2,1)S(1)}, bf16[192,512]{1,0:T(8,128)(2,1)S(1)}, u32[]{:S(2)}, u32[]{:S(2)}) collective-permute-start(bf16[192,512]{1,0:T(8,128)(2,1)S(1)} %get-tuple-element.107), channel_id=1, source_target_pairs={{0,2},{1,3},{2,0},{3,1},{4,6},{5,7},{6,4},{7,5},{8,10},{9,11},{10,... | collective-permute-start | bytes 589832 | tf_op jit(solution)/shard_map/ppermute | solution.py:1035
  128.9 16.6 %collective-permute-start.3 = (bf16[192,512]{1,0:T(8,128)(2,1)S(1)}, bf16[192,512]{1,0:T(8,128)(2,1)S(1)}, u32[]{:S(2)}, u32[]{:S(2)}) collective-permute-start(bf16[192,512]{1,0:T(8,128)(2,1)S(1)} %get-tuple-element.108), channel_id=1, source_target_pairs={{0,1},{1,2},{2,3},{3,0},{4,5},{5,6},{6,7},{7,4},{8,9},{9,10},{10,1... | collective-permute-start | bytes 589832 | tf_op jit(solution)/shard_map/ppermute | solution.py:1035
  131.0 4.6 %copy-start.9 = (f32[512,768]{1,0:T(8,128)S(1)}, f32[512,768]{1,0:T(8,128)}, u32[]{:S(2)}) copy-start(f32[512,768]{1,0:T(8,128)} %get-tuple-element.58) | copy-start | bytes 4718596
  184.4 163.2 %copy-start.2 = (bf16[768,2304]{1,0:T(8,128)(2,1)S(1)}, bf16[768,2304]{1,0:T(8,128)(2,1)}, u32[]{:S(2)}) copy-start(bf16[768,2304]{1,0:T(8,128)(2,1)} %wq.1) | copy-start | bytes 10616836
  184.4 163.2 %copy-start.4 = (bf16[512,768]{1,0:T(8,128)(2,1)S(1)}, bf16[512,768]{1,0:T(8,128)(2,1)}, u32[]{:S(2)}) copy-start(bf16[512,768]{1,0:T(8,128)(2,1)} %copy-done.3) | copy-start | bytes 2359300
  352.8 28.7 %copy-start.10 = (f32[512,768]{1,0:T(8,128)S(1)}, f32[512,768]{1,0:T(8,128)}, u32[]{:S(2)}) copy-start(f32[512,768]{1,0:T(8,128)} %get-tuple-element.68) | copy-start | bytes 4718596
  381.4 2.0 copy-start.11
  381.4 2.1 copy-start.12

commit v3 on v2

--- a/solution.py
+++ b/solution.py
@@ -367,95 +367,89 @@
     return key_pos <= query_pos
 
 
-def attend_kernel(block_count, qkv_ref, o_ref, lse_ref):
+def attend_head(read, write, block_count):
     for query_block in range(block_count):
         here = slice(query_block * BLOCK, (query_block + 1) * BLOCK)
-        queries = (qkv_ref[0, :, here].astype(F32) * 0.125).astype(BF16)
+        queries = (read(0, here).astype(F32) * 0.125).astype(BF16)
         peak = jnp.full((1, BLOCK), MASKED, F32)
         total = jnp.zeros((1, BLOCK), F32)
-        accum = jnp.zeros((64, BLOCK), F32)
+        accum = jnp.zeros((HEAD_DIM, BLOCK), F32)
         for key_block in range(query_block + 1):
             there = slice(key_block * BLOCK, (key_block + 1) * BLOCK)
-            logits = matmul(qkv_ref[1, :, there].T, queries)
+            logits = matmul(read(1, there).T, queries)
             if key_block == query_block:
                 logits = jnp.where(causal_mask(0, BLOCK, BLOCK), logits, MASKED)
             new_peak = jnp.maximum(peak, jnp.max(logits, axis=0, keepdims=True))
             weights = jnp.exp(logits - new_peak)
             factor = jnp.exp(peak - new_peak)
             total = total * factor + jnp.sum(weights, axis=0, keepdims=True)
-            accum = accum * factor + matmul(qkv_ref[2, :, there], weights.astype(BF16))
+            accum = accum * factor + matmul(read(2, there), weights.astype(BF16))
             peak = new_peak
-        o_ref[:, here] = accum / total
-        lse_ref[0:1, here] = peak + jnp.log(total)
-
-
-def attend_forward(qkv, heads):
-    length = qkv.shape[2]
-    pairs = heads * length * (length + BLOCK) // 2
+        write(query_block, here, accum / total, peak + jnp.log(total))
+
+
+def norm_in(x, gain):
+    average = jnp.mean(x, axis=-1, keepdims=True)
+    centred = x - average
+    inverse = lax.rsqrt(jnp.mean(centred * centred, axis=-1, keepdims=True) + EPSILON)
+    return (centred * inverse * gain).astype(BF16)
+
+
+def pack_kernel(slot_ref, x_ref, w_ref, gain_ref, a_ref, qkv_ref, o_ref, lse_ref, x_out, at):
+    h = pl.program_id(0)
+
+    @pl.when(h == 0)
+    def _():
+        x_out[...] = x_ref[0]
+        a = norm_in(x_ref[0].astype(F32), gain_ref[:, 0:D])
+        a_ref[...] = a
+        at[...] = a.T
+        for part in range(3):
+            for k in range(0, D, 256):
+                columns = slice(part * D + k, part * D + k + 256)
+                qkv_ref[part, k : k + 256, :] = left_t(w_ref[:, columns], at[...]).astype(BF16)
+
+    rows = pl.ds(pl.multiple_of(h * HEAD_DIM, HEAD_DIM), HEAD_DIM)
+
+    def write(query_block, here, o, lse):
+        o_ref[...] = o
+        lse_ref[0:1, :] = lse
+
+    attend_head(lambda part, columns: qkv_ref[part, rows, :], write, 1)
+
+
+def pack_forward(slot, tokens, weight, gain):
+    still = lambda *shape: pl.BlockSpec(shape, lambda h, slot: (0,) * len(shape))
+    once = lambda *shape: pl.BlockSpec(
+        shape, lambda h, slot: (0,) * len(shape), pipeline_mode=pl.Buffered(1)
+    )
+    by_head = lambda rows: pl.BlockSpec((rows, BLOCK), lambda h, slot: (h, 0))
     return pl.pallas_call(
-        functools.partial(attend_kernel, length // BLOCK),
-        grid=(heads,),
-        in_specs=[pl.BlockSpec((3, 64, length), lambda h: (0, h, 0))],
-        out_specs=[
-            pl.BlockSpec((64, length), lambda h: (h, 0)),
-            pl.BlockSpec((8, length), lambda h: (h, 0)),
-        ],
+        pack_kernel,
+        grid_spec=pltpu.PrefetchScalarGridSpec(
+            num_scalar_prefetch=1,
+            grid=(HEADS,),
+            in_specs=[
+                pl.BlockSpec((1, BLOCK, D), lambda h, slot: (slot[0], 0, 0)),
+                once(D, 3 * D),
+                once(1, 3 * D + FF),
+            ],
+            out_specs=[still(BLOCK, D), still(3, D, BLOCK), by_head(HEAD_DIM), by_head(8)]
+            + [still(BLOCK, D)],
+            scratch_shapes=[pltpu.VMEM((D, BLOCK), BF16)],
+        ),
         out_shape=[
-            jax.ShapeDtypeStruct((heads * 64, length), F32),
-            jax.ShapeDtypeStruct((heads * 8, length), F32),
+            jax.ShapeDtypeStruct((BLOCK, D), BF16),
+            jax.ShapeDtypeStruct((3, D, BLOCK), BF16),
+            jax.ShapeDtypeStruct((D, BLOCK), F32),
+            jax.ShapeDtypeStruct((HEADS * 8, BLOCK), F32),
+            jax.ShapeDtypeStruct((BLOCK, D), BF16),
         ],
         compiler_params=pltpu.CompilerParams(vmem_limit_bytes=VMEM_LIMIT),
         cost_estimate=pl.CostEstimate(
-            flops=pairs * 1024, bytes_accessed=heads * length * 700, transcendentals=pairs
-        ),
-    )(qkv)
-
-
-def attend_back_kernel(block_count, qkv_ref, o_ref, lse_ref, do_ref, d_ref, dk_acc, dv_acc):
-    dk_acc[...] = jnp.zeros_like(dk_acc)
-    dv_acc[...] = jnp.zeros_like(dv_acc)
-    for query_block in range(block_count):
-        here = slice(query_block * BLOCK, (query_block + 1) * BLOCK)
-        queries_t = (qkv_ref[0, :, here].astype(F32) * 0.125).astype(BF16)
-        queries = queries_t.T
-        do_t = do_ref[:, here]
-        do_rows = do_t.T
-        lse = lse_ref[0:1, here]
-        delta = jnp.sum(do_t.astype(F32) * o_ref[:, here], axis=0, keepdims=True)
-        dq = jnp.zeros((64, BLOCK), F32)
-        for key_block in range(query_block + 1):
-            there = slice(key_block * BLOCK, (key_block + 1) * BLOCK)
-            keys_t = qkv_ref[1, :, there]
-            probs = jnp.exp(matmul(keys_t.T, queries_t) - lse)
-            if key_block == query_block:
-                probs = jnp.where(causal_mask(0, BLOCK, BLOCK), probs, 0.0)
-            dprobs = matmul(qkv_ref[2, :, there].T, do_t)
-            dlogits = (probs * (dprobs - delta)).astype(BF16)
-            dq = dq + matmul(keys_t, dlogits)
-            dv_acc[there, :] += matmul(probs.astype(BF16), do_rows)
-            dk_acc[there, :] += matmul(dlogits, queries)
-        d_ref[0, :, here] = (dq * 0.125).astype(BF16)
-    d_ref[1] = dk_acc[...].T.astype(BF16)
-    d_ref[2] = dv_acc[...].T.astype(BF16)
-
-
-def attend_backward(qkv, o_t, lse, do_t, heads):
-    length = qkv.shape[2]
-    pairs = heads * length * (length + BLOCK) // 2
-    spec = lambda rows: pl.BlockSpec((rows, length), lambda h: (h, 0))
-    triple = pl.BlockSpec((3, 64, length), lambda h: (0, h, 0))
-    return pl.pallas_call(
-        functools.partial(attend_back_kernel, length // BLOCK),
-        grid=(heads,),
-        in_specs=[triple, spec(64), spec(8), spec(64)],
-        out_specs=triple,
-        out_shape=jax.ShapeDtypeStruct((3, heads * 64, length), BF16),
-        scratch_shapes=[pltpu.VMEM((length, 64), F32), pltpu.VMEM((length, 64), F32)],
-        compiler_params=pltpu.CompilerParams(vmem_limit_bytes=VMEM_LIMIT),
-        cost_estimate=pl.CostEstimate(
-            flops=pairs * 2048, bytes_accessed=heads * length * 1300, transcendentals=pairs
-        ),
-    )(qkv, o_t, lse, do_t)
+            flops=8 * 10**9, bytes_accessed=10 * 2**20, transcendentals=HEADS * BLOCK * BLOCK
+        ),
+    )(slot, tokens, weight, gain)
 
 
 def widened(gain, width):
@@ -482,41 +476,85 @@
     return values * below, below + values * (density * 0.3989422804014327)
 
 
-def feed_kernel(steps, chunk, sub, has_partial, *refs):
+def feed_kernel(steps, chunk, sub, has_partial, slot, *refs):
     names = iter(refs)
-    o_ref, x_ref, dy_ref, ig_ref, fg_ref, hg_ref, wo, wu_first, wd, wu_last = [
-        next(names) for _ in range(10)
-    ]
-    if has_partial:
-        part_d, part_u, part_o = [next(names) for _ in range(3)]
-    out_ref, dh_ref, do_ref, gd_ref, gu_ref, go_ref = [next(names) for _ in range(6)]
-    b_s, h_s, c_s, cn_s, dyt_s, n_s, slope_s, t_s, out_s, dc_s, st = [next(names) for _ in range(11)]
-    width = x_ref.shape[0]
+    take = lambda count: [next(names) for _ in range(count)]
+    o_in, x_in, dy_in, gain_ref, wo_in, wu_in, wd_in = take(7)
+    part_in = take(3) if has_partial else []
+    out_to, dh_to, do_to, go_to, gd_ref, gu_ref = take(6)
+    o_ref, x_ref, dy_ref, wo, wu, wd, out_s, dh_s, do_s, go_s = take(10)
+    ig, fg, hg, b_s, h_s, c_s, cn_s, dyt_s, n_s, slope_s, t_s, sum_s, dc_s, st = take(14)
+    parts, part_o = take(2) if has_partial else (None, None)
+    load_sem, wu_sem, wd_sem, part_sem, save_sem = take(5)
+    width = BLOCK
     step = pl.program_id(0)
+    o_load = pltpu.make_async_copy(o_in, o_ref, load_sem.at[0])
+    wo_load = pltpu.make_async_copy(wo_in, wo, load_sem.at[1])
+    x_load = pltpu.make_async_copy(x_in.at[slot[0]], x_ref, load_sem.at[2])
+    dy_load = pltpu.make_async_copy(dy_in.at[slot[0]], dy_ref, load_sem.at[3])
+
+    def span(k):
+        return pl.ds(pl.multiple_of(k * chunk, chunk), chunk)
+
+    def wu_load(k):
+        return pltpu.make_async_copy(wu_in.at[:, span(k)], wu.at[:, span(k)], wu_sem.at[k])
+
+    def wd_load(k):
+        return pltpu.make_async_copy(wd_in.at[span(k), :], wd.at[span(k), :], wd_sem.at[k])
+
+    def part_load(which, k):
+        return pltpu.make_async_copy(
+            part_in[which].at[span(k), :], parts.at[k], part_sem.at[which, k]
+        )
+
+    def save(k):
+        source, target = [(out_s, out_to), (dh_s, dh_to), (do_s, do_to), (go_s, go_to)][k]
+        return pltpu.make_async_copy(source, target, save_sem.at[k])
 
     @pl.when(step == 0)
     def _():
+        for load in (o_load, wo_load, x_load):
+            load.start()
+        ig[...] = jnp.broadcast_to(gain_ref[:, D : 2 * D], (128, D)).T
+        fg[...] = jnp.broadcast_to(gain_ref[:, 2 * D : 3 * D], (128, D)).T
+        hg[...] = jnp.broadcast_to(gain_ref[:, 3 * D :], (128, FF)).T
+        o_load.wait()
         o = o_ref[...].astype(F32)
         average, inverse = column_stats(o)
-        b = ((o - average) * inverse * widened(ig_ref[...], width)).astype(BF16)
+        b = ((o - average) * inverse * widened(ig[...], width)).astype(BF16)
         b_s[...] = b
         st[0:1] = average
         st[1:2] = inverse
-        dyt_s[...] = dy_ref[...].T
+        wo_load.wait()
+        x_load.wait()
+        wu_load(0).start()
+        dy_load.start()
         h = x_ref[...].T.astype(F32) + left_t(wo[...], b)
         h_s[...] = h
         average, inverse = column_stats(h)
         st[2:3] = average
         st[3:4] = inverse
-        c = ((h - average) * inverse * widened(fg_ref[...], width)).astype(BF16)
+        c = ((h - average) * inverse * widened(fg[...], width)).astype(BF16)
         c_s[...] = c
         cn_s[...] = c.T
+        dy_load.wait()
+        dyt_s[...] = dy_ref[...].T
+        for k in range(1, steps):
+            wu_load(k).start()
+        for k in range(steps):
+            wd_load(k).start()
+        if has_partial:
+            for k in range(steps):
+                part_load(0, k).start()
+            pltpu.make_async_copy(part_in[2], part_o, load_sem.at[4]).start()
 
     @pl.when(step < steps)
     def _():
+        wu_load(step).wait()
         base = pl.multiple_of(step * chunk, chunk)
         for k in range(chunk // sub):
-            z, slope = gelu_both(left_t(wu_first[:, k * sub : (k + 1) * sub], c_s[...]))
+            u = left_t(wu[:, pl.ds(base + k * sub, sub)], c_s[...])
+            z, slope = gelu_both(u)
             n_s[pl.ds(base + k * sub, sub), :] = z
             slope_s[pl.ds(base + k * sub, sub), :] = slope.astype(BF16)
 
@@ -533,11 +571,15 @@
         st[4:5] = average
         st[5:6] = lax.rsqrt(total * (1.0 / FF) + EPSILON)
         st[6:8] = jnp.zeros((2, width), F32)
-        out_s[...] = h_s[...]
+        sum_s[...] = h_s[...]
 
     @pl.when((step >= steps) & (step < 2 * steps))
     def _():
-        base = pl.multiple_of((step - steps) * chunk, chunk)
+        turn = step - steps
+        wd_load(turn).wait()
+        if has_partial:
+            part_load(0, turn).wait()
+        base = pl.multiple_of(turn * chunk, chunk)
         average = st[4:5]
         inverse = st[5:6]
         first = jnp.zeros((1, width), F32)
@@ -545,123 +587,328 @@
         pieces = []
         for k in range(chunk // sub):
             rows = slice(k * sub, (k + 1) * sub)
-            n = (n_s[pl.ds(base + k * sub, sub), :] - average) * inverse
-            n_s[pl.ds(base + k * sub, sub), :] = n
-            gain = widened(hg_ref[rows, :], width)
+            here = pl.ds(base + k * sub, sub)
+            n = (n_s[here, :] - average) * inverse
+            n_s[here, :] = n
+            gain = widened(hg[here, :], width)
             e = (n * gain).astype(BF16)
             pieces.append(e)
-            t = matmul(wd[rows, :], dyt_s[...]) * gain
-            t_s[pl.ds(base + k * sub, sub), :] = t
+            t = matmul(wd[here, :], dyt_s[...]) * gain
+            t_s[here, :] = t
             first = first + jnp.sum(t, axis=0, keepdims=True)
             second = second + jnp.sum(t * n, axis=0, keepdims=True)
             grad = matmul(e, dy_ref[...])
             if has_partial:
-                grad = grad + part_d[rows, :].astype(F32)
+                grad = grad + parts[turn, rows, :].astype(F32)
             gd_ref[rows, :] = grad.astype(BF16)
-        out_s[...] += left_t(wd[...], jnp.concatenate(pieces, axis=0))
+        sum_s[...] += left_t(wd[pl.ds(base, chunk), :], jnp.concatenate(pieces, axis=0))
         st[6:7] += first
         st[7:8] += second
+        if has_partial:
+            part_load(1, turn).start()
 
     @pl.when(step == 2 * steps - 1)
     def _():
-        out_ref[...] = out_s[...].astype(BF16).T
+        out_s[...] = sum_s[...].astype(BF16).T
+        save(0).start()
         st[6:8] = st[6:8] * (1.0 / FF)
         dc_s[...] = jnp.zeros_like(dc_s)
 
     @pl.when(step >= 2 * steps)
     def _():
-        base = pl.multiple_of((step - 2 * steps) * chunk, chunk)
+        turn = step - 2 * steps
+        if has_partial:
+            part_load(1, turn).wait()
+        base = pl.multiple_of(turn * chunk, chunk)
         inverse = st[5:6]
         first = st[6:7]
         second = st[7:8]
         pieces = []
         for k in range(chunk // sub):
-            rows = pl.ds(base + k * sub, sub)
-            n = n_s[rows, :]
-            du = ((t_s[rows, :] - first - n * second) * inverse * slope_s[rows, :].astype(F32)).astype(BF16)
+            rows = slice(k * sub, (k + 1) * sub)
+            here = pl.ds(base + k * sub, sub)
+            n = n_s[here, :]
+            du = ((t_s[here, :] - first - n * second) * inverse * slope_s[here, :].astype(F32)).astype(BF16)
             pieces.append(du)
             grad = matmul(du, cn_s[...])
             if has_partial:
-                grad = grad + part_u[k * sub : (k + 1) * sub, :].astype(F32)
-            gu_ref[k * sub : (k + 1) * sub, :] = grad.astype(BF16)
-        dc_s[...] += matmul(wu_last[...], jnp.concatenate(pieces, axis=0))
+                grad = grad + parts[turn, rows, :].astype(F32)
+            gu_ref[rows, :] = grad.astype(BF16)
+        dc_s[...] += matmul(wu[:, pl.ds(base, chunk)], jnp.concatenate(pieces, axis=0))
 
     @pl.when(step == 3 * steps - 1)
     def _():
         n = (h_s[...] - st[2:3]) * st[3:4]
-        t = dc_s[...] * widened(fg_ref[...], width)
+        t = dc_s[...] * widened(fg[...], width)
         first = jnp.sum(t, axis=0, keepdims=True) * (1.0 / D)
         second = jnp.sum(t * n, axis=0, keepdims=True) * (1.0 / D)
         dh = dyt_s[...].astype(F32) + (t - first - n * second) * st[3:4]
-        dh_rows = dh.T
-        dh_ref[...] = dh_rows
-        grad = matmul(b_s[...], dh_rows.astype(BF16))
-        if has_partial:
-            grad = grad + part_o[...].astype(F32)
-        go_ref[...] = grad.astype(BF16)
+        dh_s[...] = dh
+        save(1).start()
+        dh_low = dh.astype(BF16)
         n = (o_ref[...].astype(F32) - st[0:1]) * st[1:2]
-        t = matmul(wo[...], dh.astype(BF16)) * widened(ig_ref[...], width)
+        t = matmul(wo[...], dh_low) * widened(ig[...], width)
         first = jnp.sum(t, axis=0, keepdims=True) * (1.0 / D)
         second = jnp.sum(t * n, axis=0, keepdims=True) * (1.0 / D)
-        do_ref[...] = ((t - first - n * second) * st[1:2]).astype(BF16)
-
-
-def feed_both(o_t, x, dy, gains, weights, partial=None, chunk=768, sub=256):
-    width = x.shape[0]
+        do_s[...] = ((t - first - n * second) * st[1:2]).astype(BF16)
+        save(2).start()
+        grad = matmul(b_s[...], dh_low.T)
+        if has_partial:
+            pltpu.make_async_copy(part_in[2], part_o, load_sem.at[4]).wait()
+            grad = grad + part_o[...].astype(F32)
+        go_s[...] = grad.astype(BF16)
+        save(3).start()
+        for k in range(4):
+            save(k).wait()
+
+
+def feed_both(slot, o_t, tokens, cotangent, gains, weights, partial=None, chunk=1536, sub=256):
+    width = BLOCK
     steps = FF // chunk
     has_partial = partial is not None
-    once = lambda *shape: pl.BlockSpec(shape, lambda i: (0, 0), pipeline_mode=pl.Buffered(1))
-    first = lambda i: jnp.clip(i, 0, steps - 1)
-    second = lambda i: jnp.clip(i - steps, 0, steps - 1)
-    third = lambda i: jnp.clip(i - 2 * steps, 0, steps - 1)
-    by_rows = lambda phase: pl.BlockSpec((chunk, D), lambda i: (phase(i), 0))
-    by_columns = lambda phase: pl.BlockSpec((D, chunk), lambda i: (0, phase(i)))
-    in_specs = [once(D, width), once(width, D), once(width, D), once(D, 128), once(D, 128)]
-    in_specs += [pl.BlockSpec((chunk, 128), lambda i: (second(i), 0)), once(D, D)]
-    in_specs += [by_columns(first), by_rows(second), by_columns(third)]
-    args = [o_t, x, dy, *gains, *weights]
+    anywhere = pl.BlockSpec(memory_space=pl.ANY)
+    second = lambda i, slot: (jnp.clip(i - steps, 0, steps - 1), 0)
+    third = lambda i, slot: (jnp.clip(i - 2 * steps, 0, steps - 1), 0)
+    dma = pltpu.SemaphoreType.DMA
+    scratch = [
+        pltpu.VMEM((D, width), o_t.dtype),
+        pltpu.VMEM((width, D), BF16),
+        pltpu.VMEM((width, D), BF16),
+        pltpu.VMEM((D, D), BF16),
+        pltpu.VMEM((D, FF), BF16),
+        pltpu.VMEM((FF, D), BF16),
+        pltpu.VMEM((width, D), BF16),
+        pltpu.VMEM((D, width), F32),
+        pltpu.VMEM((D, width), BF16),
+        pltpu.VMEM((D, D), BF16),
+        pltpu.VMEM((D, 128), F32),
+        pltpu.VMEM((D, 128), F32),
+        pltpu.VMEM((FF, 128), F32),
+        pltpu.VMEM((D, width), BF16),
+        pltpu.VMEM((D, width), F32),
+        pltpu.VMEM((D, width), BF16),
+        pltpu.VMEM((width, D), BF16),
+        pltpu.VMEM((D, width), BF16),
+        pltpu.VMEM((FF, width), F32),
+        pltpu.VMEM((FF, width), BF16),
+        pltpu.VMEM((FF, width), F32),
+        pltpu.VMEM((D, width), F32),
+        pltpu.VMEM((D, width), F32),
+        pltpu.VMEM((8, width), F32),
+    ]
+    args = [o_t, tokens, cotangent, gains, *weights]
     if has_partial:
-        in_specs += [by_rows(second), by_rows(third), once(D, D)]
         args += list(partial)
-    whole = lambda *shape: pl.BlockSpec(shape, lambda i: (0, 0))
+        scratch += [pltpu.VMEM((steps, chunk, D), BF16), pltpu.VMEM((D, D), BF16)]
+    scratch += [dma((5,)), dma((steps,)), dma((steps,)), dma((2, steps)), dma((4,))]
     return pl.pallas_call(
         functools.partial(feed_kernel, steps, chunk, sub, has_partial),
-        grid=(3 * steps,),
-        in_specs=in_specs,
-        out_specs=[
-            whole(width, D),
-            whole(width, D),
-            whole(D, width),
-            by_rows(second),
-            by_rows(third),
-            whole(D, D),
-        ],
+        grid_spec=pltpu.PrefetchScalarGridSpec(
+            num_scalar_prefetch=1,
+            grid=(3 * steps,),
+            in_specs=[anywhere] * 3
+            + [pl.BlockSpec(gains.shape, lambda i, slot: (0, 0), pipeline_mode=pl.Buffered(1))]
+            + [anywhere] * (len(args) - 4),
+            out_specs=[anywhere] * 4
+            + [pl.BlockSpec((chunk, D), second), pl.BlockSpec((chunk, D), third)],
+            scratch_shapes=scratch,
+        ),
         out_shape=[
             jax.ShapeDtypeStruct((width, D), BF16),
-            jax.ShapeDtypeStruct((width, D), F32),
+            jax.ShapeDtypeStruct((D, width), F32),
             jax.ShapeDtypeStruct((D, width), BF16),
+            jax.ShapeDtypeStruct((D, D), BF16),
             jax.ShapeDtypeStruct((FF, D), BF16),
             jax.ShapeDtypeStruct((FF, D), BF16),
-            jax.ShapeDtypeStruct((D, D), BF16),
-        ],
-        scratch_shapes=[
-            pltpu.VMEM((D, width), BF16),
-            pltpu.VMEM((D, width), F32),
-            pltpu.VMEM((D, width), BF16),
-            pltpu.VMEM((width, D), BF16),
-            pltpu.VMEM((D, width), BF16),
-            pltpu.VMEM((FF, width), F32),
-            pltpu.VMEM((FF, width), BF16),
-            pltpu.VMEM((FF, width), F32),
-            pltpu.VMEM((D, width), F32),
-            pltpu.VMEM((D, width), F32),
-            pltpu.VMEM((8, width), F32),
         ],
         compiler_params=pltpu.CompilerParams(vmem_limit_bytes=62 * 2**20),
         cost_estimate=pl.CostEstimate(
-            flops=6 * width * D * (D + 2 * FF), bytes_accessed=80 * 2**20, transcendentals=width * FF
-        ),
-    )(*args)
+            flops=6 * width * D * (D + 2 * FF), bytes_accessed=50 * 2**20, transcendentals=width * FF
+        ),
+    )(slot, *args)
+
+
+def long_kernel(*refs):
+    x0, x1, x2, x3, w_ref, gain_ref = refs[:6]
+    qkv_ref, o_ref, lse_ref, do_ref, a_ref, x_ref, dh_ref = refs[6:13]
+    a_out, qkv_out, o_out, lse_out, mine_out, gq_out, dx_out = refs[13:20]
+    a_all, qkv, o_own, lse_own, o_low, w, qp, op, lp, dop, ap, xp, dhp, dp, gq, dx = refs[20:36]
+    w_near, w_own, load_sem, save_sem, swap_send, swap_recv = refs[36:]
+    gain_row = gain_ref[:, 0:D]
+    r = lax.axis_index("rows")
+    s = lax.axis_index("seq")
+    shifted = [(r, (s + shift) % SEQ) for shift in range(SEQ)]
+    barrier = pltpu.get_barrier_semaphore()
+    for device in shifted[1:]:
+        pl.semaphore_signal(barrier, inc=1, device_id=device, device_id_type=MESH)
+    pl.semaphore_wait(barrier, SEQ - 1)
+    sources = [qkv_ref, o_ref, lse_ref, do_ref, a_ref, x_ref, dh_ref, w_ref]
+    targets = [qp, op, lp, dop, ap, xp, dhp, w]
+    loads = [
+        pltpu.make_async_copy(source, target, load_sem.at[k])
+        for k, (source, target) in enumerate(zip(sources, targets))
+    ]
+    nears = [
+        pltpu.make_async_copy(
+            w_ref.at[:, pl.ds(pl.multiple_of(part * D + (3 * s // 2) * 128, 128), 256)],
+            w_near.at[part],
+            load_sem.at[8 + part],
+        )
+        for part in range(3)
+    ]
+    for load in nears + loads:
+        load.start()
+    saves = [
+        pltpu.make_async_copy(source, target, save_sem.at[k])
+        for k, (source, target) in enumerate(
+            [(a_all, a_out), (qkv, qkv_out), (o_own, o_out), (lse_own, lse_out)]
+            + [(gq, gq_out), (dx, dx_out)]
+        )
+    ]
+
+    def o_copy(h, shift):
+        part = o_low.at[(s + shift) % SEQ, pl.ds(h * HEAD_DIM, HEAD_DIM), :]
+        place = pl.ds(pl.multiple_of(s * (HEADS_OWN * HEAD_DIM) + h * HEAD_DIM, 16), HEAD_DIM)
+        target = mine_out.at[place, :]
+        if shift == 0:
+            return pltpu.make_async_copy(part, target, save_sem.at[6 + h])
+        return pltpu.make_async_remote_copy(
+            src_ref=part,
+            dst_ref=target,
+            send_sem=swap_send.at[h, shift],
+            recv_sem=swap_recv.at[h, shift],
+            device_id=shifted[shift],
+            device_id_type=MESH,
+        )
+
+    for part in range(3):
+        nears[part].wait()
+
+        @pl.when(s % 2 == 0)
+        def _():
+            w_own[part] = w_near[part, :, 0:192]
+
+        @pl.when(s % 2 == 1)
+        def _():
+            w_own[part] = w_near[part, :, 64:256]
+
+    for shift, x in enumerate((x0, x1, x2, x3)):
+        start = pl.multiple_of(((s - shift) % SEQ) * BLOCK, BLOCK)
+        a = norm_in(x[...].astype(F32), gain_row)
+        a_all[pl.ds(start, BLOCK), :] = a
+        a_t = a.T
+        for part in range(3):
+            qkv[part, :, pl.ds(start, BLOCK)] = left_t(w_own[part], a_t).astype(BF16)
+    saves[0].start()
+    saves[1].start()
+    for h in range(HEADS_OWN):
+        rows = slice(h * HEAD_DIM, (h + 1) * HEAD_DIM)
+
+        def write(query_block, here, o, lse):
+            o_own[rows, here] = o
+            lse_own[h, 0:1, here] = lse
+            o_low[query_block, rows, :] = o.astype(BF16)
+
+        attend_head(lambda part, columns: qkv[part, rows, columns], write, SEQ)
+        for shift in range(SEQ):
+            o_copy(h, shift).start()
+    saves[2].start()
+    saves[3].start()
+    for load in loads:
+        load.wait()
+
+    def back(h, carry):
+        rows = pl.ds(pl.multiple_of(h * HEAD_DIM, HEAD_DIM), HEAD_DIM)
+        queries_t = (qp[0, rows, :].astype(F32) * 0.125).astype(BF16)
+        keys_t = qp[1, rows, :]
+        do_t = dop[rows, :]
+        lse = lp[pl.ds(pl.multiple_of(h * 8, 8), 8), :][0:1]
+        delta = jnp.sum(do_t.astype(F32) * op[rows, :], axis=0, keepdims=True)
+        probs = jnp.exp(matmul(keys_t.T, queries_t) - lse)
+        probs = jnp.where(causal_mask(0, BLOCK, BLOCK), probs, 0.0)
+        dprobs = matmul(qp[2, rows, :].T, do_t)
+        dlogits = (probs * (dprobs - delta)).astype(BF16)
+        dp[0, rows, :] = (matmul(keys_t, dlogits) * 0.125).astype(BF16)
+        dp[1, rows, :] = matmul(dlogits, queries_t.T).T.astype(BF16)
+        dp[2, rows, :] = matmul(probs.astype(BF16), do_t.T).T.astype(BF16)
+        return carry
+
+    lax.fori_loop(0, HEADS, back, 0)
+    for part in range(3):
+        gq[part * D : (part + 1) * D, :] = matmul(dp[part], ap[...]).astype(BF16)
+    saves[4].start()
+    dx[...] = first_norm_back(xp[...], dhp[...], w, dp, gain_row)
+    saves[5].start()
+    for save in saves:
+        save.wait()
+    for h in range(HEADS_OWN):
+        for shift in range(SEQ):
+            o_copy(h, shift).wait()
+
+
+def first_norm_back(x, dh_t, w, dqkv, gain):
+    x_t = x.T.astype(F32)
+    average, inverse = column_stats(x_t)
+    n = (x_t - average) * inverse
+    t = matmul(w[:, 0:D], dqkv[0])
+    for part in range(1, 3):
+        t = t + matmul(w[:, part * D : (part + 1) * D], dqkv[part])
+    t = t * widened(jnp.broadcast_to(gain, (128, D)).T, BLOCK)
+    first = jnp.sum(t, axis=0, keepdims=True) * (1.0 / D)
+    second = jnp.sum(t * n, axis=0, keepdims=True) * (1.0 / D)
+    return (dh_t + (t - first - n * second) * inverse).astype(BF16).T
+
+
+def long_forward(x_blocks, weight, gains, pack, collective_id):
+    own_rows = HEADS_OWN * HEAD_DIM
+    length = SEQ * BLOCK
+    dma = pltpu.SemaphoreType.DMA
+    anywhere = pl.BlockSpec(memory_space=pl.ANY)
+    resident = pl.BlockSpec(memory_space=pltpu.VMEM)
+    return pl.pallas_call(
+        long_kernel,
+        in_specs=[resident] * 4 + [anywhere] + [resident] + [anywhere] * 7,
+        out_specs=[anywhere] * 7,
+        out_shape=[
+            jax.ShapeDtypeStruct((length, D), BF16),
+            jax.ShapeDtypeStruct((3, own_rows, length), BF16),
+            jax.ShapeDtypeStruct((own_rows, length), F32),
+            jax.ShapeDtypeStruct((HEADS_OWN, 8, length), F32),
+            jax.ShapeDtypeStruct((D, BLOCK), BF16),
+            jax.ShapeDtypeStruct((3 * D, D), BF16),
+            jax.ShapeDtypeStruct((BLOCK, D), BF16),
+        ],
+        scratch_shapes=[
+            pltpu.VMEM((length, D), BF16),
+            pltpu.VMEM((3, own_rows, length), BF16),
+            pltpu.VMEM((own_rows, length), F32),
+            pltpu.VMEM((HEADS_OWN, 8, length), F32),
+            pltpu.VMEM((SEQ, own_rows, BLOCK), BF16),
+            pltpu.VMEM((D, 3 * D), BF16),
+            pltpu.VMEM((3, D, BLOCK), BF16),
+            pltpu.VMEM((D, BLOCK), F32),
+            pltpu.VMEM((HEADS * 8, BLOCK), F32),
+            pltpu.VMEM((D, BLOCK), BF16),
+            pltpu.VMEM((BLOCK, D), BF16),
+            pltpu.VMEM((BLOCK, D), BF16),
+            pltpu.VMEM((D, BLOCK), F32),
+            pltpu.VMEM((3, D, BLOCK), BF16),
+            pltpu.VMEM((3 * D, D), BF16),
+            pltpu.VMEM((BLOCK, D), BF16),
+            pltpu.VMEM((3, D, 256), BF16),
+            pltpu.VMEM((3, D, own_rows), BF16),
+            dma((11,)),
+            dma((6 + HEADS_OWN,)),
+            dma((HEADS_OWN, SEQ)),
+            dma((HEADS_OWN, SEQ)),
+        ],
+        compiler_params=pltpu.CompilerParams(
+            collective_id=collective_id, has_side_effects=True, vmem_limit_bytes=VMEM_LIMIT
+        ),
+        cost_estimate=pl.CostEstimate(
+            flops=20 * 10**9, bytes_accessed=40 * 2**20, transcendentals=10**7
+        ),
+    )(*x_blocks, weight, gains, *pack)
 
 
 PIECE = 768
@@ -671,7 +918,9 @@
 QKV_PIECES = 3 * D // PIECE
 PIECES = FEED_PIECES + QKV_PIECES
 ATTEND_TICK = 2
-GAP = 0
+QKV_TICK = 5
+BACK_TICK = 3
+BACKS = 1
 
 
 def sum_kernel(*refs):
@@ -932,16 +1181,22 @@
             place = rows_at(part * D + s * (HEADS_OWN * HEAD_DIM) + h * HEAD_DIM, HEAD_DIM)
             term = total[part * HEAD_DIM : (part + 1) * HEAD_DIM, :]
             gq_own[place, :] = (gq_own[place, :].astype(F32) + term).astype(BF16)
-        for shift in range(SEQ):
-            back_copy(h, shift).start()
+        back_copy(h, 0).start()
 
     def tick(t, carry):
         for lag, stage in enumerate(stages):
-            v = t - lag
-
-            @pl.when((v >= 0) & ((v < FEED_PIECES) | (v >= FEED_PIECES + GAP)) & (v < PIECES + GAP))
-            def _():
-                stage(jnp.where(v < FEED_PIECES, v, v - GAP))
+            for sub in range(2):
+                p = 2 * (t - lag) + sub
+
+                @pl.when((p >= 0) & (p < FEED_PIECES))
+                def _():
+                    stage(p)
+
+                q = 2 * (t - lag - QKV_TICK) + sub
+
+                @pl.when((q >= 0) & (q < QKV_PIECES))
+                def _():
+                    stage(FEED_PIECES + q)
 
         @pl.when(t == ATTEND_TICK)
         def _():
@@ -950,31 +1205,32 @@
             for shift in range(SEQ):
                 do_copy(shift).wait()
 
-        turn = t - ATTEND_TICK
-        h = turn // 2
-
-        @pl.when((turn >= 0) & (turn < 2 * HEADS_OWN) & (turn % 2 == 0))
+        h = t - ATTEND_TICK
+
+        @pl.when((h >= 0) & (h < HEADS_OWN))
         def _():
             dk_acc[...] = jnp.zeros_like(dk_acc)
             dv_acc[...] = jnp.zeros_like(dv_acc)
-            attend(h, 0)
-            attend(h, 3)
-
-        @pl.when((turn >= 0) & (turn < 2 * HEADS_OWN) & (turn % 2 == 1))
-        def _():
-            attend(h, 1)
-            attend(h, 2)
+            for query_block in range(SEQ):
+                attend(h, query_block)
             finish_head(h)
 
-        @pl.when(turn == 2 * HEADS_OWN - 1)
+        @pl.when(h == HEADS_OWN - 1)
         def _():
             for q in range(QKV_PIECES):
                 core_copy(gq_own, q, FEED_PIECES + q).start()
                 own_copy(gq_own, q, FEED_PIECES + q).start()
 
+        for unit in range(3 * HEADS_OWN):
+
+            @pl.when(t == BACK_TICK + unit // BACKS)
+            def _():
+                back_copy(unit // 3, unit % 3 + 1).start()
+
         return carry
 
-    lax.fori_loop(0, PIECES + GAP + len(stages) - 1, tick, 0)
+    last = QKV_TICK + (QKV_PIECES - 1) // 2 + len(stages)
+    lax.fori_loop(0, last, tick, 0)
     for h in range(HEADS_OWN):
         for shift in range(SEQ):
             back_copy(h, shift).wait()
@@ -1026,20 +1282,32 @@
     )(gd, gu, go, gq, do_pieces, qkv_own, o_own, lse, a_all)
 
 
-def by_block(relative, place):
-    blocks = [lax.dynamic_index_in_dim(relative, (place - j) % SEQ, 0) for j in range(SEQ)]
-    return jnp.concatenate(blocks, axis=0)
-
-
 def shifted_by(value, shift):
     return lax.ppermute(value, "seq", [(i, (i + shift) % SEQ) for i in range(SEQ)])
 
 
-FINISH = PIECES
-
-
-def finish_kernel(total, wd, wu, wo, wq, ig, fg, hg, ag, gd, gu, go, gq, si, sf, sh, sa, acc):
+def finish_kernel(slots, *refs):
+    total, wd, wu, wo, wq, gain_ref = refs[:6]
+    dqkv_ref, dh_ref, tokens, out_pack, out_long, dx_pack = refs[6:12]
+    gd, gu, go, gq, si, sf, sh, sa, output, grad_out = refs[12:22]
+    acc, dqkv, dh_t, x_long, dx, rows, load_sem, copy_sem = refs[22:]
     step = pl.program_id(0)
+    sources = [dqkv_ref, dh_ref, tokens.at[slots[0]]]
+    targets = [dqkv, dh_t, x_long]
+    loads = [
+        pltpu.make_async_copy(source, target, load_sem.at[k])
+        for k, (source, target) in enumerate(zip(sources, targets))
+    ]
+    fetches = [
+        pltpu.make_async_copy(source, rows.at[k], load_sem.at[3 + k])
+        for k, source in enumerate((out_long, out_pack, dx_pack))
+    ]
+    copies = [
+        pltpu.make_async_copy(rows.at[0], output.at[slots[0]], copy_sem.at[0]),
+        pltpu.make_async_copy(rows.at[1], output.at[slots[1]], copy_sem.at[1]),
+        pltpu.make_async_copy(rows.at[2], grad_out.at[slots[1]], copy_sem.at[2]),
+    ]
+    last = pltpu.make_async_copy(dx, grad_out.at[slots[0]], copy_sem.at[3])
 
     def lanes(values):
         folded = values[:, 0:128]
@@ -1047,14 +1315,27 @@
             folded = folded + values[:, k * 128 : (k + 1) * 128]
         return folded
 
-    def as_row(folded):
-        return jnp.sum(folded.T, axis=0, keepdims=True)
+    def as_row(folded, start):
+        gain = gain_ref[:, pl.ds(pl.multiple_of(start, D), D)]
+        return (jnp.sum(folded.T, axis=0, keepdims=True) / gain)[0]
+
+    @pl.when(step == 0)
+    def _():
+        for copy in loads + fetches:
+            copy.start()
+
+    @pl.when(step == 4)
+    def _():
+        for fetch, copy in zip(fetches, copies):
+            fetch.wait()
+            copy.start()
 
     @pl.when(step < 4)
     def _():
         grad = total[...].astype(F32)
         gd[...] = grad
-        sh[...] = as_row(lanes(grad * wd[...].astype(F32))) / hg[...]
+        rows_here = pl.ds(pl.multiple_of(step * D, D), D)
+        sh[rows_here] = as_row(lanes(grad * wd[...].astype(F32)), (3 + step) * D)
 
     @pl.when((step >= 4) & (step < 8))
     def _():
@@ -1064,73 +1345,83 @@
 
     @pl.when(step == 8)
     def _():
-        sf[...] = as_row(acc[0]) / fg[...]
+        sf[...] = as_row(acc[0], 2 * D)
         grad = total[...].astype(F32)
         go[...] = grad
-        si[...] = as_row(lanes(grad * wo[...].astype(F32))) / ig[...]
+        si[...] = as_row(lanes(grad * wo[...].astype(F32)), D)
+
+    @pl.when(step == 6)
+    def _():
+        for load in loads:
+            load.wait()
+        dx[...] = first_norm_back(x_long[...], dh_t[...], wq, dqkv, gain_ref[:, 0:D])
+        last.start()
 
     @pl.when(step >= 9)
     def _():
         grad = total[...].T.astype(F32)
         gq[...] = grad
-        acc[1] = lanes(grad * wq[...].astype(F32)) + jnp.where(step == 9, 0.0, acc[1])
+        columns = pl.ds(pl.multiple_of((step - 9) * D, D), D)
+        acc[1] = lanes(grad * wq[:, columns].astype(F32)) + jnp.where(step == 9, 0.0, acc[1])
 
     @pl.when(step == 11)
     def _():
-        sa[...] = as_row(acc[1]) / ag[...]
-
-
-def finished(total, down_weight, up_weight, out_weight, query_key_value, gains):
+        sa[...] = as_row(acc[1], 0)
+        for copy in copies:
+            copy.wait()
+        last.wait()
+
+
+def finished(slots, total, weights, gains, rows):
+    down_weight, up_weight, out_weight, query_key_value = weights
     square = lambda index: pl.BlockSpec((D, D), index)
-    row = lambda index: pl.BlockSpec((1, D), index)
-    at_down = lambda i: (jnp.clip(i, 0, 3), 0)
-    at_up = lambda i: (0, jnp.clip(i - 4, 0, 3))
-    at_qkv = lambda i: (0, jnp.clip(i - 9, 0, 2))
-    still = lambda i: (0, 0)
-    hidden = lambda i: (0, jnp.clip(i, 0, 3))
-    shapes = [(FF, D), (D, FF), (D, D), (D, 3 * D), (1, D), (1, D), (1, FF), (1, D)]
+    row = lambda index: pl.BlockSpec((D,), index)
+    at_down = lambda i, slots: (jnp.clip(i, 0, 3), 0)
+    at_up = lambda i, slots: (0, jnp.clip(i - 4, 0, 3))
+    at_qkv = lambda i, slots: (0, jnp.clip(i - 9, 0, 2))
+    still = lambda i, slots: (0, 0)
+    only = lambda i, slots: (0,)
+    once = lambda *shape: pl.BlockSpec(shape, still, pipeline_mode=pl.Buffered(1))
+    anywhere = pl.BlockSpec(memory_space=pl.ANY)
+    shapes = [(FF, D), (D, FF), (D, D), (D, 3 * D), (D,), (D,), (FF,), (D,)]
+    pair = jax.ShapeDtypeStruct((2, BLOCK, D), BF16)
+    dma = pltpu.SemaphoreType.DMA
     return pl.pallas_call(
         finish_kernel,
-        grid=(FINISH,),
-        in_specs=[
-            square(lambda i: (i, 0)),
-            square(at_down),
-            square(at_up),
-            square(still),
-            square(at_qkv),
-            row(still),
-            row(still),
-            row(hidden),
-            row(still),
-        ],
-        out_specs=[
-            square(at_down),
-            square(at_up),
-            square(still),
-            square(at_qkv),
-            row(still),
-            row(still),
-            row(hidden),
-            row(still),
-        ],
-        out_shape=[jax.ShapeDtypeStruct(shape, F32) for shape in shapes],
-        scratch_shapes=[pltpu.VMEM((2, D, 128), F32)],
+        grid_spec=pltpu.PrefetchScalarGridSpec(
+            num_scalar_prefetch=1,
+            grid=(PIECES,),
+            in_specs=[square(lambda i, slots: (i, 0)), square(at_down), square(at_up)]
+            + [once(D, D), once(D, 3 * D), once(1, 3 * D + FF)]
+            + [anywhere] * 6,
+            out_specs=[square(at_down), square(at_up), square(still), square(at_qkv)]
+            + [row(only), row(only), pl.BlockSpec((FF,), only), row(only)]
+            + [anywhere] * 2,
+            scratch_shapes=[
+                pltpu.VMEM((2, D, 128), F32),
+                pltpu.VMEM((3, D, BLOCK), BF16),
+                pltpu.VMEM((D, BLOCK), F32),
+                pltpu.VMEM((BLOCK, D), BF16),
+                pltpu.VMEM((BLOCK, D), BF16),
+                pltpu.VMEM((3, BLOCK, D), BF16),
+                dma((6,)),
+                dma((4,)),
+            ],
+        ),
+        out_shape=[jax.ShapeDtypeStruct(shape, F32) for shape in shapes] + [pair, pair],
         compiler_params=pltpu.CompilerParams(vmem_limit_bytes=VMEM_LIMIT),
-        cost_estimate=pl.CostEstimate(flops=10**8, bytes_accessed=56 * 2**20, transcendentals=0),
-    )(total, down_weight, up_weight, out_weight, query_key_value, *[g[None] for g in gains])
-
-
-def normed_rows(x, gain):
-    out, normed, inverse = layer_norm(x.astype(F32), gain)
-    return out.astype(BF16), normed, inverse
-
-
-def layer_back(upstream, normed, inverse, gain):
-    scaled = upstream * gain
-    return inverse * (
-        scaled
-        - jnp.mean(scaled, axis=-1, keepdims=True)
-        - normed * jnp.mean(scaled * normed, axis=-1, keepdims=True)
+        cost_estimate=pl.CostEstimate(
+            flops=2 * 10**9, bytes_accessed=56 * 2**20, transcendentals=0
+        ),
+    )(
+        slots,
+        total,
+        down_weight,
+        up_weight,
+        out_weight,
+        query_key_value,
+        gains,
+        *rows,
     )
 
 
@@ -1147,84 +1438,50 @@
     feed_gain,
     hidden_gain,
 ):
-    place = lax.axis_index("seq")
     long_first = segment_ids[0, -1] == 0
     x_long = jnp.where(long_first, tokens[0], tokens[1])
-    x_pack = jnp.where(long_first, tokens[1], tokens[0])
-    dy_long = jnp.where(long_first, cotangent[0], cotangent[1])
-    dy_pack = jnp.where(long_first, cotangent[1], cotangent[0])
     x_blocks = [x_long] + [shifted_by(x_long, shift) for shift in range(1, SEQ)]
-    wide = lambda gain: jnp.broadcast_to(gain[:, None], (gain.shape[0], 128))
-    gains = (wide(inner_gain), wide(feed_gain), wide(hidden_gain))
-    weights = (out_weight, up_weight, down_weight, up_weight)
-    a_pack, pack_normed, pack_inverse = normed_rows(x_pack, attend_gain)
-    qkv_pack = lax.dot_general(
-        query_key_value, a_pack, (((0,), (1,)), ((), ())), preferred_element_type=F32
-    )
-    qkv_pack = qkv_pack.astype(BF16).reshape(3, D, BLOCK)
-    o_pack, lse_pack = attend_forward(qkv_pack, HEADS)
-    out_pack, dh_pack, do_pack, gd_pack, gu_pack, go_pack = feed_both(
-        o_pack, x_pack, dy_pack, gains, weights
+    long_slot = jnp.where(long_first, 0, 1).astype(jnp.int32)
+    slots = jnp.stack([long_slot, 1 - long_slot])
+    gains = jnp.concatenate([attend_gain, inner_gain, feed_gain, hidden_gain])[None]
+    weights = (out_weight, up_weight, down_weight)
+    a_pack, qkv_pack, o_pack, lse_pack, x_pack = pack_forward(
+        slots[1:], tokens, query_key_value, gains
+    )
+    out_pack, dh_pack, do_pack, go_pack, gd_pack, gu_pack = feed_both(
+        slots[1:], o_pack, tokens, cotangent, gains, weights
     )
     *x_blocks, do_pack = lax.optimization_barrier((*x_blocks, do_pack))
-    own_rows = HEADS_OWN * HEAD_DIM
-    w_own = lax.dynamic_slice_in_dim(
-        query_key_value.reshape(D, 3, D), place * own_rows, own_rows, 2
-    ).reshape(D, 3 * own_rows)
-    x_all = by_block(jnp.stack(x_blocks), place).reshape(SEQ * BLOCK, D)
-    a_all, _, _ = normed_rows(x_all, attend_gain)
-    qkv_long = lax.dot_general(w_own, a_all, (((0,), (1,)), ((), ())), preferred_element_type=F32)
-    qkv_long = qkv_long.astype(BF16).reshape(3, own_rows, SEQ * BLOCK)
-    o_long, lse_long = attend_forward(qkv_long, HEADS_OWN)
-    o_low = o_long.astype(BF16)
-    o_parts = []
-    for shift in range(SEQ):
-        leaving = lax.dynamic_slice_in_dim(o_low, ((place + shift) % SEQ) * BLOCK, BLOCK, 1)
-        o_parts.append(shifted_by(leaving, shift) if shift else leaving)
-    do_pack, _ = lax.optimization_barrier((do_pack, o_low))
-    dqkv_pack = attend_backward(qkv_pack, o_pack, lse_pack, do_pack, HEADS).reshape(3 * D, BLOCK)
-    gq_pack = matmul(dqkv_pack, a_pack).astype(BF16)
-    dxa_pack = layer_back(
-        left_t(dqkv_pack, query_key_value.T), pack_normed, pack_inverse, attend_gain
-    )
-    dx_pack = (dh_pack + dxa_pack).astype(BF16)
-    *o_parts, gq_pack, dx_pack = lax.optimization_barrier((*o_parts, gq_pack, dx_pack))
-    o_mine = by_block(jnp.stack(o_parts), place).reshape(D, BLOCK)
-    out_long, dh_long, do_long, gd, gu, go = feed_both(
-        o_mine, x_long, dy_long, gains, weights, (gd_pack, gu_pack, go_pack)
+    a_all, qkv_long, o_long, lse_long, o_mine, gq_pack, dx_pack = long_forward(
+        x_blocks,
+        query_key_value,
+        gains,
+        (qkv_pack, o_pack, lse_pack, do_pack, a_pack, x_pack, dh_pack),
+        1,
+    )
+    out_long, dh_long, do_long, go, gd, gu = feed_both(
+        slots[:1], o_mine, tokens, cotangent, gains, weights, (gd_pack, gu_pack, go_pack)
     )
     total, dqkv_long = summed_everywhere(
         gd,
         gu,
         go,
         gq_pack,
-        do_long.reshape(SEQ, own_rows, BLOCK),
+        do_long.reshape(SEQ, HEADS_OWN * HEAD_DIM, BLOCK),
         qkv_long,
         o_long,
-        lse_long.reshape(HEADS_OWN, 8, SEQ * BLOCK),
+        lse_long,
         a_all,
         0,
     )
-    _, long_normed, long_inverse = normed_rows(x_long, attend_gain)
-    dxa_long = layer_back(
-        left_t(dqkv_long.reshape(3 * D, BLOCK), query_key_value.T),
-        long_normed,
-        long_inverse,
-        attend_gain,
-    )
-    dx_long = (dh_long + dxa_long).astype(BF16)
-    down_grad, up_grad, out_grad, qkv_grad, inner_total, feed_total, hidden_total, attend_total = (
-        finished(
-            total,
-            down_weight,
-            up_weight,
-            out_weight,
-            query_key_value,
-            (inner_gain, feed_gain, hidden_gain, attend_gain),
-        )
-    )
-    output = jnp.where(long_first, jnp.stack([out_long, out_pack]), jnp.stack([out_pack, out_long]))
-    tokens_grad = jnp.where(long_first, jnp.stack([dx_long, dx_pack]), jnp.stack([dx_pack, dx_long]))
+    down_grad, up_grad, out_grad, qkv_grad, *sums, output, tokens_grad = finished(
+        slots,
+        total,
+        (down_weight, up_weight, out_weight, query_key_value),
+        gains,
+        (dqkv_long, dh_long, tokens, out_pack, out_long, dx_pack),
+    )
+    inner_total, feed_total, hidden_total, attend_total = sums
     return (
         output,
         tokens_grad,
@@ -1232,10 +1489,10 @@
         out_grad,
         up_grad,
         down_grad,
-        attend_total[0],
-        inner_total[0],
-        feed_total[0],
-        hidden_total[0],
+        attend_total,
+        inner_total,
+        feed_total,
+        hidden_total,
     )
 
 

time: 392 us -> 324 us (0.83)
  other arithmetic: 24.7 us -> 2.06 us
  matrix products: 20.3 us -> 0 us
  local copies, waits for them, and re-layouts: 18.3 us -> 1.93 us
  Pallas kernels: 303 us -> 294 us
  waiting for transfers between devices: 9.36 us -> 15.9 us
    pallas_call x1, Pallas kernels: 163 us -> 140 us  [summed_everywhere(): pl.pallas_call(sum_kernel, out_shape=[jax.ShapeDtypeStruct((n * PIECE, D)...]
    dot_general x5 -> x0, matrix products: 20.3 us -> none  [the longest x2 9.27 us: left_t(): lax.dot_general(left, right, (((0,), (0,)), ((), ())), preferred_element_...]
    pallas_call x4 -> x3, Pallas kernels: 66.2 us -> 85.1 us  [the longest x1 40.8 us: long_forward(): pl.pallas_call(long_kernel, in_specs=[resident] * 4 + [anywhere] + [resid...]
    convert_element_type x4 -> x0, other arithmetic: 7.97 us -> none  [the longest x2 5.92 us: normed_rows(): return (out.astype(BF16), normed, inverse)]
    ppermute x6 -> x3, waiting for transfers between devices: 9.36 us -> 15.9 us  [shifted_by(): lax.ppermute(value, 'seq', [(i, (i + shift) % SEQ) for i in range(SEQ)])]
    unnamed x39 -> x12, local copies, waits for them, and re-layouts: 5.84 us -> 0.03 us
    pallas_call x2, Pallas kernels: 73.6 us -> 68.7 us  [feed_both(): pl.pallas_call(functools.partial(feed_kernel, steps, chunk, sub, has_part...]
    broadcast_in_dim x6 -> x1, local copies, waits for them, and re-layouts: 5.19 us -> 0.62 us  [split_layer(): jnp.concatenate([attend_gain, inner_gain, feed_gain, hidden_gain])[None]]
  transfers between devices with their start and end apart: 6 -> 3, of which waited for: 2 -> 1; matrix products, arithmetic and copies ran while one was open for 7% -> 0% of each run, Pallas kernels for 12% -> 15%
where the time goes in v3:
time: 324 us; the launch traced here: 320 us
  Pallas kernels  294 us (91%)
  waiting for transfers between devices  15.9 us (5%)
  starting transfers between devices  4.72 us (1%)
    pallas_call x1, Pallas kernels, summed_everywhere(): pl.pallas_call(sum_kernel, out_shape=[jax.ShapeDtypeStruct((n * PIECE, D)...  140 us
    pallas_call x2, Pallas kernels, feed_both(): pl.pallas_call(functools.partial(feed_kernel, steps, chunk, sub, has_part...  68.7 us
    pallas_call x1, Pallas kernels, long_forward(): pl.pallas_call(long_kernel, in_specs=[resident] * 4 + [anywhere] + [resid...  40.8 us
    pallas_call x1, Pallas kernels, finished(): pl.pallas_call(finish_kernel, grid_spec=pltpu.PrefetchScalarGridSpec(num_...  30.6 us
    ppermute x3, waiting for transfers between devices, shifted_by(): lax.ppermute(value, 'seq', [(i, (i + shift) % SEQ) for i in range(SEQ)])  15.9 us
    pallas_call x1, Pallas kernels, pack_forward(): pl.pallas_call(pack_kernel, grid_spec=pltpu.PrefetchScalarGridSpec(num_sc...  13.7 us
  transfers between devices with their start and end apart: 3, of which 1 were waited for; matrix products, arithmetic and copies ran while one was open for 0% of the time, Pallas kernels for 15%

profile of v3, /device:TPU:9, one launch (start us, length us, event | category | flops | bytes accessed | tf_op | source)
XLA Modules:
  0.0 320.3 jit_solution(16550611345365124681)
XLA Ops:
  0.6 0.0 copy-start.1
  0.7 0.0 copy-start.2
  0.7 0.0 copy-start.3
  0.7 0.0 copy-start.4
  0.7 1.3 slice.9
  2.6 1.5 select_bitcast_fusion.refs_0_
  4.1 0.0 copy-start
  4.1 0.1 collective-permute-start.2
  4.2 2.5 collective-permute-start.1
  6.6 2.2 collective-permute-start
  8.8 0.0 copy-done.1
  8.8 0.0 copy-done.2
  8.8 0.0 copy-done.3
  8.8 0.6 broadcast_in_dim.3.gain_ref.refs_3_.refs_5_
  9.5 13.7 %shard_map.186 = (bf16[512,768]{1,0:T(8,128)(2,1)}, bf16[3,768,512]{2,1,0:T(8,128)(2,1)}, f32[768,512]{1,0:T(8,128)}, f32[96,512]{1,0:T(8,128)}, bf16[512,768]{1,0:T(8,128)(2,1)}) custom-call(s32[1]{0:T(128)} %bitcast.2.slot_ref.slot, bf16[2,512,768]{2,1,0:T(8,128)(2,1)} %refs_8_.1, bf16[768,2304]{1,0:T(8,128)(2,1)} %refs_4_.7, ...), custom_call_target="tpu_custom_call" | custom-call | flops 8000000000 | bytes 10485760 | tf_op jit(solution)/shard_map/pallas_call | solution.py:427
  23.2 33.9 %shard_map.187 = (bf16[512,768]{1,0:T(8,128)(2,1)}, f32[768,512]{1,0:T(8,128)}, bf16[768,512]{1,0:T(8,128)(2,1)}, bf16[768,768]{1,0:T(8,128)(2,1)}, bf16[3072,76...) custom-call(s32[1]{0:T(128)} %bitcast.2.slot_ref.slot, f32[768,512]{1,0:T(8,128)} %get-tuple-element.51.refs_0_.refs_7_, ...), custom_call_target="tpu_custom_call" | custom-call | flops 16307453952 | bytes 52428800 | tf_op jit(solution)/shard_map/pallas_call | solution.py:704
  57.2 0.6 pad_add_fusion.slots
  57.8 0.0 collective-permute-done.2.refs_3_
  57.8 0.0 collective-permute-done.1.refs_2_
  57.8 15.9 %collective-permute-done.refs_1_ = bf16[512,768]{1,0:T(8,128)(2,1)} collective-permute-done((bf16[512,768]{1,0:T(8,128)(2,1)S(1)}, bf16[512,768]{1,0:T(8,128)(2,1)}, u32[]{:S(2)}, u32[]{:S(2)}) %collective-permute-start) | collective-permute-done | bytes 786464 | tf_op jit(solution)/shard_map/ppermute | solution.py:1286
  73.7 40.8 %shard_map.188 = (bf16[2048,768]{1,0:T(8,128)(2,1)}, bf16[3,192,2048]{2,1,0:T(8,128)(2,1)}, f32[192,2048]{1,0:T(8,128)}, f32[3,8,2048]{2,1,0:T(8,128)}, bf16[768...) custom-call(bf16[512,768]{1,0:T(8,128)(2,1)} %copy-done, ...), custom_call_target="tpu_custom_call" | custom-call | flops 20000000000 | bytes 41943040 | tf_op jit(solution)/shard_map/pallas_call | solution.py:868
  114.5 34.8 %shard_map.189 = (bf16[512,768]{1,0:T(8,128)(2,1)}, f32[768,512]{1,0:T(8,128)}, bf16[768,512]{1,0:T(8,128)(2,1)}, bf16[768,768]{1,0:T(8,128)(2,1)}, bf16[3072,76...) custom-call(s32[1]{0:T(128)} %bitcast.1.slot, bf16[768,512]{1,0:T(8,128)(2,1)} %get-tuple-element.63.refs_0_, ...), custom_call_target="tpu_custom_call" | custom-call | flops 16307453952 | bytes 52428800 | tf_op jit(solution)/shard_map/pallas_call | solution.py:704
  149.3 140.3 %shard_map.190 = (bf16[9216,768]{1,0:T(8,128)(2,1)}, bf16[3,768,512]{2,1,0:T(8,128)(2,1)}) custom-call(bf16[3072,768]{1,0:T(8,128)(2,1)} %get-tuple-element.67.refs_0_, bf16[3072,768]{1,0:T(8,128)(2,1)} %get-tuple-element.68.refs_1_, bf16[768,768]{1,0:T(8,128)(2,1)} %get-tuple-element.69.refs_2_, bf16[2304,768]{1,0:T(8,128)(2,1)} %get-tuple-element.70.refs_3_, ...), custom_call_target="tpu_custom_call" | custom-call | bytes 452984832 | tf_op jit(solution)/shard_map/pallas_call | solution.py:1245
  289.6 30.6 %shard_map.191 = (f32[3072,768]{1,0:T(8,128)}, f32[768,3072]{1,0:T(8,128)}, f32[768,768]{1,0:T(8,128)}, f32[768,2304]{1,0:T(8,128)}, f32[768]{0:T(1024)}, /*inde...) custom-call(s32[2]{0:T(128)} %pad_add_fusion.slots, ...), custom_call_target="tpu_custom_call" | custom-call | flops 2000000000 | bytes 58720256 | tf_op jit(solution)/shard_map/pallas_call | solution.py:1389
  (5 shorter events, 0.0 us)
Async XLA Ops:
  0.6 8.2 %copy-start.1 = (f32[3072]{0:T(1024)S(1)}, f32[3072]{0:T(1024)}, u32[]{:S(2)}) copy-start(f32[3072]{0:T(1024)} %param.21) | copy-start | bytes 36868
  0.7 8.2 %copy-start.2 = (f32[768]{0:T(1024)S(1)}, f32[768]{0:T(1024)}, u32[]{:S(2)}) copy-start(f32[768]{0:T(1024)} %param.20) | copy-start | bytes 9220
  0.7 8.2 %copy-start.3 = (f32[768]{0:T(1024)S(1)}, f32[768]{0:T(1024)}, u32[]{:S(2)}) copy-start(f32[768]{0:T(1024)} %param.19) | copy-start | bytes 9220
  0.7 8.2 %copy-start.4 = (f32[768]{0:T(1024)S(1)}, f32[768]{0:T(1024)}, u32[]{:S(2)}) copy-start(f32[768]{0:T(1024)} %param.18) | copy-start | bytes 9220
  4.1 19.1 %copy-start = (bf16[512,768]{1,0:T(8,128)(2,1)}, bf16[512,768]{1,0:T(8,128)(2,1)S(1)}, u32[]{:S(2)}) copy-start(bf16[512,768]{1,0:T(8,128)(2,1)S(1)} %select_bitcast_fusion.refs_0_) | copy-start | bytes 2359300
  4.1 53.7 %collective-permute-start.2 = (bf16[512,768]{1,0:T(8,128)(2,1)S(1)}, bf16[512,768]{1,0:T(8,128)(2,1)S(1)}, u32[]{:S(2)}, u32[]{:S(2)}) collective-permute-start(bf16[512,768]{1,0:T(8,128)(2,1)S(1)} %select_bitcast_fusion.refs_0_), channel_id=1, source_target_pairs={{0,3},{1,0},{2,1},{3,2},{4,7},{5,4},{6,5},{7,6},{8,11},{9,8},{10,9... | collective-permute-start | bytes 2359304 | tf_op jit(solution)/shard_map/ppermute | solution.py:1286
  4.2 53.6 %collective-permute-start.1 = (bf16[512,768]{1,0:T(8,128)(2,1)S(1)}, bf16[512,768]{1,0:T(8,128)(2,1)}, u32[]{:S(2)}, u32[]{:S(2)}) collective-permute-start(bf16[512,768]{1,0:T(8,128)(2,1)S(1)} %select_bitcast_fusion.refs_0_), channel_id=1, source_target_pairs={{0,2},{1,3},{2,0},{3,1},{4,6},{5,7},{6,4},{7,5},{8,10},{9,11},{10,... | collective-permute-start | bytes 2359304 | tf_op jit(solution)/shard_map/ppermute | solution.py:1286
  6.6 67.1 %collective-permute-start = (bf16[512,768]{1,0:T(8,128)(2,1)S(1)}, bf16[512,768]{1,0:T(8,128)(2,1)}, u32[]{:S(2)}, u32[]{:S(2)}) collective-permute-start(bf16[512,768]{1,0:T(8,128)(2,1)S(1)} %select_bitcast_fusion.refs_0_), channel_id=1, source_target_pairs={{0,1},{1,2},{2,3},{3,0},{4,5},{5,6},{6,7},{7,4},{8,9},{9,10},{10,1... | collective-permute-start | bytes 2359304 | tf_op jit(solution)/shard_map/ppermute | solution.py:1286
  57.8 15.9 %copy-start.5 = (bf16[512,768]{1,0:T(8,128)(2,1)}, bf16[512,768]{1,0:T(8,128)(2,1)S(1)}, u32[]{:S(2)}) copy-start(bf16[512,768]{1,0:T(8,128)(2,1)S(1)} %collective-permute-done.2.refs_3_) | copy-start | bytes 2359300

commit v4 on v3

--- a/solution.py
+++ b/solution.py
@@ -353,6 +353,7 @@
 FF = 3072
 SEQ = 4
 BLOCK = 512
+SPLIT = BLOCK // 2
 HEADS_OWN = HEADS // SEQ
 GROUP = HEADS_OWN * 3 * HEAD_DIM
 MESH = pl.DeviceIdType.MESH
@@ -374,18 +375,36 @@
         peak = jnp.full((1, BLOCK), MASKED, F32)
         total = jnp.zeros((1, BLOCK), F32)
         accum = jnp.zeros((HEAD_DIM, BLOCK), F32)
-        for key_block in range(query_block + 1):
+        for key_block in range(query_block):
             there = slice(key_block * BLOCK, (key_block + 1) * BLOCK)
             logits = matmul(read(1, there).T, queries)
-            if key_block == query_block:
-                logits = jnp.where(causal_mask(0, BLOCK, BLOCK), logits, MASKED)
             new_peak = jnp.maximum(peak, jnp.max(logits, axis=0, keepdims=True))
             weights = jnp.exp(logits - new_peak)
             factor = jnp.exp(peak - new_peak)
             total = total * factor + jnp.sum(weights, axis=0, keepdims=True)
             accum = accum * factor + matmul(read(2, there), weights.astype(BF16))
             peak = new_peak
-        write(query_block, here, accum / total, peak + jnp.log(total))
+        keys = read(1, here).T
+        values = read(2, here)
+        logits = jnp.where(
+            causal_mask(0, SPLIT, BLOCK), matmul(keys[:SPLIT], queries), MASKED
+        )
+        corner = jnp.where(
+            causal_mask(0, SPLIT, SPLIT), matmul(keys[SPLIT:], queries[:, SPLIT:]), MASKED
+        )
+        new_peak = jnp.maximum(peak, jnp.max(logits, axis=0, keepdims=True))
+        late_peak = jnp.maximum(new_peak[:, SPLIT:], jnp.max(corner, axis=0, keepdims=True))
+        new_peak = jnp.concatenate([new_peak[:, :SPLIT], late_peak], axis=1)
+        weights = jnp.exp(logits - new_peak)
+        corner = jnp.exp(corner - late_peak)
+        factor = jnp.exp(peak - new_peak)
+        total = total * factor + jnp.sum(weights, axis=0, keepdims=True)
+        accum = accum * factor + matmul(values[:, :SPLIT], weights.astype(BF16))
+        corner_total = jnp.sum(corner, axis=0, keepdims=True)
+        corner_accum = matmul(values[:, SPLIT:], corner.astype(BF16))
+        total = jnp.concatenate([total[:, :SPLIT], total[:, SPLIT:] + corner_total], axis=1)
+        accum = jnp.concatenate([accum[:, :SPLIT], accum[:, SPLIT:] + corner_accum], axis=1)
+        write(query_block, here, accum / total, new_peak + jnp.log(total))
 
 
 def norm_in(x, gain):
@@ -481,6 +500,8 @@
     take = lambda count: [next(names) for _ in range(count)]
     o_in, x_in, dy_in, gain_ref, wo_in, wu_in, wd_in = take(7)
     part_in = take(3) if has_partial else []
+    if has_partial:
+        take(1)
     out_to, dh_to, do_to, go_to, gd_ref, gu_ref = take(6)
     o_ref, x_ref, dy_ref, wo, wu, wd, out_s, dh_s, do_s, go_s = take(10)
     ig, fg, hg, b_s, h_s, c_s, cn_s, dyt_s, n_s, slope_s, t_s, sum_s, dc_s, st = take(14)
@@ -508,7 +529,7 @@
         )
 
     def save(k):
-        source, target = [(out_s, out_to), (dh_s, dh_to), (do_s, do_to), (go_s, go_to)][k]
+        source, target = [(out_s, out_to.at[slot[0]]), (dh_s, dh_to), (do_s, do_to), (go_s, go_to)][k]
         return pltpu.make_async_copy(source, target, save_sem.at[k])
 
     @pl.when(step == 0)
@@ -662,7 +683,7 @@
             save(k).wait()
 
 
-def feed_both(slot, o_t, tokens, cotangent, gains, weights, partial=None, chunk=1536, sub=256):
+def feed_both(slot, o_t, tokens, cotangent, gains, weights, partial=None, output=None, chunk=1536, sub=256):
     width = BLOCK
     steps = FF // chunk
     has_partial = partial is not None
@@ -698,7 +719,7 @@
     ]
     args = [o_t, tokens, cotangent, gains, *weights]
     if has_partial:
-        args += list(partial)
+        args += [*partial, output]
         scratch += [pltpu.VMEM((steps, chunk, D), BF16), pltpu.VMEM((D, D), BF16)]
     scratch += [dma((5,)), dma((steps,)), dma((steps,)), dma((2, steps)), dma((4,))]
     return pl.pallas_call(
@@ -713,8 +734,9 @@
             + [pl.BlockSpec((chunk, D), second), pl.BlockSpec((chunk, D), third)],
             scratch_shapes=scratch,
         ),
+        input_output_aliases={len(args): 0} if has_partial else {},
         out_shape=[
-            jax.ShapeDtypeStruct((width, D), BF16),
+            jax.ShapeDtypeStruct((2, width, D), BF16),
             jax.ShapeDtypeStruct((D, width), F32),
             jax.ShapeDtypeStruct((D, width), BF16),
             jax.ShapeDtypeStruct((D, D), BF16),
@@ -729,11 +751,11 @@
 
 
 def long_kernel(*refs):
-    x0, x1, x2, x3, w_ref, gain_ref = refs[:6]
-    qkv_ref, o_ref, lse_ref, do_ref, a_ref, x_ref, dh_ref = refs[6:13]
-    a_out, qkv_out, o_out, lse_out, mine_out, gq_out, dx_out = refs[13:20]
-    a_all, qkv, o_own, lse_own, o_low, w, qp, op, lp, dop, ap, xp, dhp, dp, gq, dx = refs[20:36]
-    w_near, w_own, load_sem, save_sem, swap_send, swap_recv = refs[36:]
+    own_x, left, right, left_two, right_two, across, w_ref, gain_ref = refs[:8]
+    qkv_ref, o_ref, lse_ref, do_ref, a_ref, x_ref, dh_ref = refs[8:15]
+    a_out, qkv_out, o_out, lse_out, mine_out, gq_out, dx_out = refs[15:22]
+    a_all, qkv, o_own, lse_own, o_low, w, qp, op, lp, dop, ap, xp, dhp, dp, gq, dx = refs[22:38]
+    x_all, w_near, w_own, load_sem, save_sem, swap_send, swap_recv = refs[38:]
     gain_row = gain_ref[:, 0:D]
     r = lax.axis_index("rows")
     s = lax.axis_index("seq")
@@ -756,6 +778,23 @@
         )
         for part in range(3)
     ]
+    x_from = [
+        [own_x, right, right_two, across],
+        [left, own_x, right, right_two],
+        [left_two, left, own_x, right],
+        [across, left_two, left, own_x],
+    ]
+
+    def x_load(k, j):
+        return pltpu.make_async_copy(x_from[k][j], x_all.at[j], load_sem.at[11 + j])
+
+    for k in range(SEQ):
+
+        @pl.when(s == k)
+        def _():
+            for j in range(SEQ):
+                x_load(k, j).start()
+
     for load in nears + loads:
         load.start()
     saves = [
@@ -792,13 +831,14 @@
         def _():
             w_own[part] = w_near[part, :, 64:256]
 
-    for shift, x in enumerate((x0, x1, x2, x3)):
-        start = pl.multiple_of(((s - shift) % SEQ) * BLOCK, BLOCK)
-        a = norm_in(x[...].astype(F32), gain_row)
-        a_all[pl.ds(start, BLOCK), :] = a
+    for j in range(SEQ):
+        start = j * BLOCK
+        x_load(0, j).wait()
+        a = norm_in(x_all[j].astype(F32), gain_row)
+        a_all[start : start + BLOCK, :] = a
         a_t = a.T
         for part in range(3):
-            qkv[part, :, pl.ds(start, BLOCK)] = left_t(w_own[part], a_t).astype(BF16)
+            qkv[part, :, start : start + BLOCK] = left_t(w_own[part], a_t).astype(BF16)
     saves[0].start()
     saves[1].start()
     for h in range(HEADS_OWN):
@@ -824,13 +864,27 @@
         do_t = dop[rows, :]
         lse = lp[pl.ds(pl.multiple_of(h * 8, 8), 8), :][0:1]
         delta = jnp.sum(do_t.astype(F32) * op[rows, :], axis=0, keepdims=True)
-        probs = jnp.exp(matmul(keys_t.T, queries_t) - lse)
-        probs = jnp.where(causal_mask(0, BLOCK, BLOCK), probs, 0.0)
-        dprobs = matmul(qp[2, rows, :].T, do_t)
+        keys = keys_t.T
+        values = qp[2, rows, :].T
+        queries = queries_t.T
+        do_rows = do_t.T
+        probs = jnp.exp(matmul(keys[:SPLIT], queries_t) - lse)
+        probs = jnp.where(causal_mask(0, SPLIT, BLOCK), probs, 0.0)
+        dprobs = matmul(values[:SPLIT], do_t)
         dlogits = (probs * (dprobs - delta)).astype(BF16)
-        dp[0, rows, :] = (matmul(keys_t, dlogits) * 0.125).astype(BF16)
-        dp[1, rows, :] = matmul(dlogits, queries_t.T).T.astype(BF16)
-        dp[2, rows, :] = matmul(probs.astype(BF16), do_t.T).T.astype(BF16)
+        late = slice(SPLIT, BLOCK)
+        corner = jnp.exp(matmul(keys[SPLIT:], queries_t[:, late]) - lse[:, late])
+        corner = jnp.where(causal_mask(0, SPLIT, SPLIT), corner, 0.0)
+        dcorner = matmul(values[SPLIT:], do_t[:, late])
+        dcorner = (corner * (dcorner - delta[:, late])).astype(BF16)
+        dq = matmul(keys_t[:, :SPLIT], dlogits)
+        dq_late = dq[:, late] + matmul(keys_t[:, late], dcorner)
+        dp[0, rows, :SPLIT] = (dq[:, :SPLIT] * 0.125).astype(BF16)
+        dp[0, rows, late] = (dq_late * 0.125).astype(BF16)
+        dp[1, rows, :SPLIT] = matmul(dlogits, queries).T.astype(BF16)
+        dp[1, rows, late] = matmul(dcorner, queries[late]).T.astype(BF16)
+        dp[2, rows, :SPLIT] = matmul(probs.astype(BF16), do_rows).T.astype(BF16)
+        dp[2, rows, late] = matmul(corner.astype(BF16), do_rows[late]).T.astype(BF16)
         return carry
 
     lax.fori_loop(0, HEADS, back, 0)
@@ -867,7 +921,7 @@
     resident = pl.BlockSpec(memory_space=pltpu.VMEM)
     return pl.pallas_call(
         long_kernel,
-        in_specs=[resident] * 4 + [anywhere] + [resident] + [anywhere] * 7,
+        in_specs=[anywhere] * 7 + [resident] + [anywhere] * 7,
         out_specs=[anywhere] * 7,
         out_shape=[
             jax.ShapeDtypeStruct((length, D), BF16),
@@ -895,9 +949,10 @@
             pltpu.VMEM((3, D, BLOCK), BF16),
             pltpu.VMEM((3 * D, D), BF16),
             pltpu.VMEM((BLOCK, D), BF16),
+            pltpu.VMEM((SEQ, BLOCK, D), BF16),
             pltpu.VMEM((3, D, 256), BF16),
             pltpu.VMEM((3, D, own_rows), BF16),
-            dma((11,)),
+            dma((11 + SEQ,)),
             dma((6 + HEADS_OWN,)),
             dma((HEADS_OWN, SEQ)),
             dma((HEADS_OWN, SEQ)),
@@ -921,12 +976,15 @@
 QKV_TICK = 5
 BACK_TICK = 3
 BACKS = 1
+DX_TICK = 13
 
 
 def sum_kernel(*refs):
-    gd, gu, go, gq, do_ref, qkv_ref, o_ref, lse_ref, a_ref, total_ref, back_ref = refs[:11]
-    own, r0, r1, r2, r3, r4, fin, qkv, o_own, lse_own, a_all, gq_own, do_own, d_own = refs[11:25]
-    dk_acc, dv_acc, own_sem, send_sem, recv_sem, fin_sem, in_sem, swap_send, swap_recv = refs[25:]
+    gd, gu, go, gq, do_ref, qkv_ref, o_ref, lse_ref, a_ref, gain_ref = refs[:10]
+    x_ref, dh_ref, wd_ref, wu_ref, wo_ref, wq_ref, total_ref, dx_ref, sums_ref = refs[10:19]
+    own, r0, r1, r2, r3, r4, fin, qkv, o_own, lse_own, a_all, gq_own, do_own, d_own = refs[19:33]
+    dk_acc, dv_acc, back_ref, x_own, dh_own, wq, dx, grads, factors, sums = refs[33:43]
+    own_sem, send_sem, recv_sem, fin_sem, in_sem, swap_send, swap_recv, gain_sem = refs[43:]
     r = lax.axis_index("rows")
     s = lax.axis_index("seq")
     core, xb, yb = r % 2, (r // 2) % 2, r // 4
@@ -1038,6 +1096,13 @@
         pltpu.make_async_copy(a_ref, a_all, in_sem.at[3]),
         pltpu.make_async_copy(gq, gq_own, in_sem.at[4]),
     ]
+    late = [
+        pltpu.make_async_copy(x_ref, x_own, in_sem.at[6 + HEADS_OWN]),
+        pltpu.make_async_copy(dh_ref, dh_own, in_sem.at[7 + HEADS_OWN]),
+        pltpu.make_async_copy(wq_ref, wq, in_sem.at[8 + HEADS_OWN]),
+    ]
+    dx_save = pltpu.make_async_copy(dx, dx_ref, in_sem.at[9 + HEADS_OWN])
+    sums_save = pltpu.make_async_copy(sums, sums_ref, in_sem.at[10 + HEADS_OWN])
     for shift in range(1, SEQ):
         do_copy(shift).start()
     offset = 0
@@ -1139,8 +1204,57 @@
         after_pair_back,
         after_second_back,
         after_first_back,
-        after_core_back,
     ]
+
+    def square(ref, p):
+        return ref.at[rows_at(p * PIECE, PIECE), :]
+
+    def grad_load(p):
+        return pltpu.make_async_copy(square(total_ref, p), grads.at[p % 2], gain_sem.at[0, p % 2])
+
+    def factor_load(ref, p):
+        return pltpu.make_async_copy(ref, factors.at[p % 2], gain_sem.at[1, p % 2])
+
+    def fetch(p):
+        grad_load(p).start()
+
+        @pl.when(p < 4)
+        def _():
+            factor_load(square(wd_ref, p), p).start()
+
+        @pl.when((p >= 4) & (p < 8))
+        def _():
+            columns = pl.ds(pl.multiple_of((p - 4) * PIECE, PIECE), PIECE)
+            factor_load(wu_ref.at[:, columns], p).start()
+
+        @pl.when(p == 8)
+        def _():
+            factor_load(wo_ref, p).start()
+
+    def row_sums(values):
+        folded = values[:, 0:128]
+        for k in range(1, D // 128):
+            folded = folded + values[:, k * 128 : (k + 1) * 128]
+        return jnp.sum(folded.T, axis=0, keepdims=True)
+
+    def weigh(p):
+        grad_load(p).wait()
+        factor_load(wo_ref, p).wait()
+        grad = grads[p % 2].astype(F32)
+
+        @pl.when(p < 4)
+        def _():
+            place = pl.ds(pl.multiple_of(p * PIECE, PIECE), PIECE)
+            sums[0:1, place] = row_sums(grad * factors[p % 2].astype(F32))
+
+        @pl.when((p >= 4) & (p < 8))
+        def _():
+            term = jnp.sum(grad * factors[p % 2].T.astype(F32), axis=0, keepdims=True)
+            sums[1:2, 0:D] = jnp.where(p == 4, 0.0, sums[1:2, 0:D]) + term
+
+        @pl.when(p == 8)
+        def _():
+            sums[2:3, 0:D] = row_sums(grad * factors[p % 2].astype(F32))
 
     def head_rows(h):
         return rows_at(h * HEAD_DIM, HEAD_DIM)
@@ -1202,6 +1316,8 @@
         def _():
             for load in loads:
                 load.wait()
+            for load in late:
+                load.start()
             for shift in range(SEQ):
                 do_copy(shift).wait()
 
@@ -1227,16 +1343,47 @@
             def _():
                 back_copy(unit // 3, unit % 3 + 1).start()
 
+        for sub in range(2):
+            p = 2 * (t - len(stages) - 1) + sub
+
+            @pl.when((p >= 0) & (p < FEED_PIECES))
+            def _():
+                weigh(p)
+
+        for sub in range(2):
+            p = 2 * (t - len(stages)) + sub
+
+            @pl.when((p >= 0) & (p < FEED_PIECES))
+            def _():
+                after_core_back(p)
+                fetch(p)
+
+            q = p - 2 * QKV_TICK
+
+            @pl.when((q >= 0) & (q < QKV_PIECES))
+            def _():
+                after_core_back(FEED_PIECES + q)
+
+        @pl.when(t == DX_TICK)
+        def _():
+            for load in late:
+                load.wait()
+            for h in range(HEADS_OWN):
+                for shift in range(SEQ):
+                    back_copy(h, shift).wait()
+            dx[...] = first_norm_back(x_own[...], dh_own[...], wq, back_ref, gain_ref[:, 0:D])
+            dx_save.start()
+
         return carry
 
-    last = QKV_TICK + (QKV_PIECES - 1) // 2 + len(stages)
+    last = QKV_TICK + (QKV_PIECES - 1) // 2 + len(stages) + 1
     lax.fori_loop(0, last, tick, 0)
-    for h in range(HEADS_OWN):
-        for shift in range(SEQ):
-            back_copy(h, shift).wait()
-
-
-def summed_everywhere(gd, gu, go, gq, do_pieces, qkv_own, o_own, lse, a_all, collective_id):
+    sums_save.start()
+    dx_save.wait()
+    sums_save.wait()
+
+
+def summed_everywhere(*args, collective_id):
     n = PIECES
     length = SEQ * BLOCK
     own_rows = HEADS_OWN * HEAD_DIM
@@ -1246,10 +1393,11 @@
         sum_kernel,
         out_shape=[
             jax.ShapeDtypeStruct((n * PIECE, D), BF16),
-            jax.ShapeDtypeStruct((3, D, BLOCK), BF16),
+            jax.ShapeDtypeStruct((BLOCK, D), BF16),
+            jax.ShapeDtypeStruct((8, FF), F32),
         ],
-        in_specs=[anywhere] * 9,
-        out_specs=[anywhere] * 2,
+        in_specs=[anywhere] * 9 + [pl.BlockSpec(memory_space=pltpu.VMEM)] + [anywhere] * 6,
+        out_specs=[anywhere] * 3,
         scratch_shapes=[
             pltpu.VMEM((n, HALF, D), BF16),
             pltpu.VMEM((n, HALF, D), BF16),
@@ -1267,162 +1415,124 @@
             pltpu.VMEM((SEQ, 3, own_rows, BLOCK), BF16),
             pltpu.VMEM((length, HEAD_DIM), F32),
             pltpu.VMEM((length, HEAD_DIM), F32),
+            pltpu.VMEM((3, D, BLOCK), BF16),
+            pltpu.VMEM((BLOCK, D), BF16),
+            pltpu.VMEM((D, BLOCK), F32),
+            pltpu.VMEM((D, 3 * D), BF16),
+            pltpu.VMEM((BLOCK, D), BF16),
+            pltpu.VMEM((2, PIECE, D), BF16),
+            pltpu.VMEM((2, PIECE, D), BF16),
+            pltpu.VMEM((8, FF), F32),
             dma((n,)),
             dma((16, n)),
             dma((16, n)),
             dma((2, n)),
-            dma((6 + HEADS_OWN,)),
+            dma((11 + HEADS_OWN,)),
             dma((1 + HEADS_OWN, SEQ)),
             dma((1 + HEADS_OWN, SEQ)),
+            dma((2, 2)),
         ],
         compiler_params=pltpu.CompilerParams(
-            collective_id=collective_id, has_side_effects=True, vmem_limit_bytes=VMEM_LIMIT
+            collective_id=collective_id, has_side_effects=True, vmem_limit_bytes=60 * 2**20
         ),
         cost_estimate=pl.CostEstimate(flops=0, bytes_accessed=n * PIECE * D * 64, transcendentals=0),
-    )(gd, gu, go, gq, do_pieces, qkv_own, o_own, lse, a_all)
-
-
-def shifted_by(value, shift):
-    return lax.ppermute(value, "seq", [(i, (i + shift) % SEQ) for i in range(SEQ)])
-
-
-def finish_kernel(slots, *refs):
-    total, wd, wu, wo, wq, gain_ref = refs[:6]
-    dqkv_ref, dh_ref, tokens, out_pack, out_long, dx_pack = refs[6:12]
-    gd, gu, go, gq, si, sf, sh, sa, output, grad_out = refs[12:22]
-    acc, dqkv, dh_t, x_long, dx, rows, load_sem, copy_sem = refs[22:]
+    )(*args)
+
+
+def sent(value, *pairs):
+    return lax.ppermute(value, "seq", pairs)
+
+
+def finish_kernel(slots, total, wq, gain_ref, sums, dx_long, dx_pack, *refs):
+    gd, gu, go, gq, si, sf, sh, sa, grad_out, acc, dx, load_sem, copy_sem = refs
     step = pl.program_id(0)
-    sources = [dqkv_ref, dh_ref, tokens.at[slots[0]]]
-    targets = [dqkv, dh_t, x_long]
     loads = [
-        pltpu.make_async_copy(source, target, load_sem.at[k])
-        for k, (source, target) in enumerate(zip(sources, targets))
-    ]
-    fetches = [
-        pltpu.make_async_copy(source, rows.at[k], load_sem.at[3 + k])
-        for k, source in enumerate((out_long, out_pack, dx_pack))
+        pltpu.make_async_copy(source, dx.at[k], load_sem.at[k])
+        for k, source in enumerate((dx_long, dx_pack))
     ]
     copies = [
-        pltpu.make_async_copy(rows.at[0], output.at[slots[0]], copy_sem.at[0]),
-        pltpu.make_async_copy(rows.at[1], output.at[slots[1]], copy_sem.at[1]),
-        pltpu.make_async_copy(rows.at[2], grad_out.at[slots[1]], copy_sem.at[2]),
+        pltpu.make_async_copy(dx.at[k], grad_out.at[slots[k]], copy_sem.at[k]) for k in range(2)
     ]
-    last = pltpu.make_async_copy(dx, grad_out.at[slots[0]], copy_sem.at[3])
-
-    def lanes(values):
-        folded = values[:, 0:128]
-        for k in range(1, D // 128):
-            folded = folded + values[:, k * 128 : (k + 1) * 128]
-        return folded
-
-    def as_row(folded, start):
-        gain = gain_ref[:, pl.ds(pl.multiple_of(start, D), D)]
-        return (jnp.sum(folded.T, axis=0, keepdims=True) / gain)[0]
 
     @pl.when(step == 0)
     def _():
-        for copy in loads + fetches:
-            copy.start()
-
-    @pl.when(step == 4)
+        for load in loads:
+            load.start()
+        si[...] = (sums[2:3, 0:D] / gain_ref[:, D : 2 * D])[0]
+        sf[...] = (sums[1:2, 0:D] / gain_ref[:, 2 * D : 3 * D])[0]
+        sh[...] = (sums[0:1, :] / gain_ref[:, 3 * D :])[0]
+
+    @pl.when(step == 2)
     def _():
-        for fetch, copy in zip(fetches, copies):
-            fetch.wait()
+        for load, copy in zip(loads, copies):
+            load.wait()
             copy.start()
 
     @pl.when(step < 4)
     def _():
-        grad = total[...].astype(F32)
-        gd[...] = grad
-        rows_here = pl.ds(pl.multiple_of(step * D, D), D)
-        sh[rows_here] = as_row(lanes(grad * wd[...].astype(F32)), (3 + step) * D)
+        gd[...] = total[...].astype(F32)
 
     @pl.when((step >= 4) & (step < 8))
     def _():
-        grad = total[...].T.astype(F32)
-        gu[...] = grad
-        acc[0] = lanes(grad * wu[...].astype(F32)) + jnp.where(step == 4, 0.0, acc[0])
+        gu[...] = total[...].T.astype(F32)
 
     @pl.when(step == 8)
     def _():
-        sf[...] = as_row(acc[0], 2 * D)
-        grad = total[...].astype(F32)
-        go[...] = grad
-        si[...] = as_row(lanes(grad * wo[...].astype(F32)), D)
-
-    @pl.when(step == 6)
-    def _():
-        for load in loads:
-            load.wait()
-        dx[...] = first_norm_back(x_long[...], dh_t[...], wq, dqkv, gain_ref[:, 0:D])
-        last.start()
+        go[...] = total[...].astype(F32)
 
     @pl.when(step >= 9)
     def _():
         grad = total[...].T.astype(F32)
         gq[...] = grad
-        columns = pl.ds(pl.multiple_of((step - 9) * D, D), D)
-        acc[1] = lanes(grad * wq[:, columns].astype(F32)) + jnp.where(step == 9, 0.0, acc[1])
+        product = grad * wq[...].astype(F32)
+        folded = product[:, 0:128]
+        for k in range(1, D // 128):
+            folded = folded + product[:, k * 128 : (k + 1) * 128]
+        acc[...] = folded + jnp.where(step == 9, 0.0, acc[...])
 
     @pl.when(step == 11)
     def _():
-        sa[...] = as_row(acc[1], 0)
+        sa[...] = (jnp.sum(acc[...].T, axis=0, keepdims=True) / gain_ref[:, 0:D])[0]
         for copy in copies:
             copy.wait()
-        last.wait()
-
-
-def finished(slots, total, weights, gains, rows):
-    down_weight, up_weight, out_weight, query_key_value = weights
+
+
+def finished(slots, total, weight, gains, sums, dx_long, dx_pack):
     square = lambda index: pl.BlockSpec((D, D), index)
-    row = lambda index: pl.BlockSpec((D,), index)
     at_down = lambda i, slots: (jnp.clip(i, 0, 3), 0)
     at_up = lambda i, slots: (0, jnp.clip(i - 4, 0, 3))
     at_qkv = lambda i, slots: (0, jnp.clip(i - 9, 0, 2))
     still = lambda i, slots: (0, 0)
-    only = lambda i, slots: (0,)
     once = lambda *shape: pl.BlockSpec(shape, still, pipeline_mode=pl.Buffered(1))
+    row = lambda size: pl.BlockSpec((size,), lambda i, slots: (0,))
     anywhere = pl.BlockSpec(memory_space=pl.ANY)
     shapes = [(FF, D), (D, FF), (D, D), (D, 3 * D), (D,), (D,), (FF,), (D,)]
-    pair = jax.ShapeDtypeStruct((2, BLOCK, D), BF16)
     dma = pltpu.SemaphoreType.DMA
     return pl.pallas_call(
         finish_kernel,
         grid_spec=pltpu.PrefetchScalarGridSpec(
             num_scalar_prefetch=1,
             grid=(PIECES,),
-            in_specs=[square(lambda i, slots: (i, 0)), square(at_down), square(at_up)]
-            + [once(D, D), once(D, 3 * D), once(1, 3 * D + FF)]
-            + [anywhere] * 6,
+            in_specs=[square(lambda i, slots: (i, 0)), square(at_qkv)]
+            + [once(1, 3 * D + FF), once(8, FF)]
+            + [anywhere] * 2,
             out_specs=[square(at_down), square(at_up), square(still), square(at_qkv)]
-            + [row(only), row(only), pl.BlockSpec((FF,), only), row(only)]
-            + [anywhere] * 2,
+            + [row(D), row(D), row(FF), row(D)]
+            + [anywhere],
             scratch_shapes=[
-                pltpu.VMEM((2, D, 128), F32),
-                pltpu.VMEM((3, D, BLOCK), BF16),
-                pltpu.VMEM((D, BLOCK), F32),
-                pltpu.VMEM((BLOCK, D), BF16),
-                pltpu.VMEM((BLOCK, D), BF16),
-                pltpu.VMEM((3, BLOCK, D), BF16),
-                dma((6,)),
-                dma((4,)),
+                pltpu.VMEM((D, 128), F32),
+                pltpu.VMEM((2, BLOCK, D), BF16),
+                dma((2,)),
+                dma((2,)),
             ],
         ),
-        out_shape=[jax.ShapeDtypeStruct(shape, F32) for shape in shapes] + [pair, pair],
+        out_shape=[jax.ShapeDtypeStruct(shape, F32) for shape in shapes]
+        + [jax.ShapeDtypeStruct((2, BLOCK, D), BF16)],
         compiler_params=pltpu.CompilerParams(vmem_limit_bytes=VMEM_LIMIT),
         cost_estimate=pl.CostEstimate(
-            flops=2 * 10**9, bytes_accessed=56 * 2**20, transcendentals=0
-        ),
-    )(
-        slots,
-        total,
-        down_weight,
-        up_weight,
-        out_weight,
-        query_key_value,
-        gains,
-        *rows,
-    )
+            flops=2 * 10**7, bytes_accessed=46 * 2**20, transcendentals=0
+        ),
+    )(slots, total, weight, gains, sums, dx_long, dx_pack)
 
 
 def split_layer(
@@ -1440,7 +1550,8 @@
 ):
     long_first = segment_ids[0, -1] == 0
     x_long = jnp.where(long_first, tokens[0], tokens[1])
-    x_blocks = [x_long] + [shifted_by(x_long, shift) for shift in range(1, SEQ)]
+    left = sent(x_long, (0, 1), (1, 2), (2, 3))
+    right = sent(x_long, (1, 0), (2, 1), (3, 2))
     long_slot = jnp.where(long_first, 0, 1).astype(jnp.int32)
     slots = jnp.stack([long_slot, 1 - long_slot])
     gains = jnp.concatenate([attend_gain, inner_gain, feed_gain, hidden_gain])[None]
@@ -1448,21 +1559,32 @@
     a_pack, qkv_pack, o_pack, lse_pack, x_pack = pack_forward(
         slots[1:], tokens, query_key_value, gains
     )
-    out_pack, dh_pack, do_pack, go_pack, gd_pack, gu_pack = feed_both(
+    o_pack, left, right = lax.optimization_barrier((o_pack, left, right))
+    left_two = sent(left, (1, 2), (2, 3))
+    right_two = sent(right, (1, 0), (2, 1))
+    across = sent(jnp.where(lax.axis_index("seq") == 1, left, right), (1, 3), (2, 0))
+    output, dh_pack, do_pack, go_pack, gd_pack, gu_pack = feed_both(
         slots[1:], o_pack, tokens, cotangent, gains, weights
     )
-    *x_blocks, do_pack = lax.optimization_barrier((*x_blocks, do_pack))
+    *x_far, do_pack = lax.optimization_barrier((left_two, right_two, across, do_pack))
     a_all, qkv_long, o_long, lse_long, o_mine, gq_pack, dx_pack = long_forward(
-        x_blocks,
+        (x_long, left, right, *x_far),
         query_key_value,
         gains,
         (qkv_pack, o_pack, lse_pack, do_pack, a_pack, x_pack, dh_pack),
         1,
     )
-    out_long, dh_long, do_long, go, gd, gu = feed_both(
-        slots[:1], o_mine, tokens, cotangent, gains, weights, (gd_pack, gu_pack, go_pack)
-    )
-    total, dqkv_long = summed_everywhere(
+    output, dh_long, do_long, go, gd, gu = feed_both(
+        slots[:1],
+        o_mine,
+        tokens,
+        cotangent,
+        gains,
+        weights,
+        (gd_pack, gu_pack, go_pack),
+        output,
+    )
+    total, dx_long, sums = summed_everywhere(
         gd,
         gu,
         go,
@@ -1472,14 +1594,17 @@
         o_long,
         lse_long,
         a_all,
-        0,
-    )
-    down_grad, up_grad, out_grad, qkv_grad, *sums, output, tokens_grad = finished(
-        slots,
-        total,
-        (down_weight, up_weight, out_weight, query_key_value),
         gains,
-        (dqkv_long, dh_long, tokens, out_pack, out_long, dx_pack),
+        x_long,
+        dh_long,
+        down_weight,
+        up_weight,
+        out_weight,
+        query_key_value,
+        collective_id=0,
+    )
+    down_grad, up_grad, out_grad, qkv_grad, *sums, tokens_grad = finished(
+        slots, total, query_key_value, gains, sums, dx_long, dx_pack
     )
     inner_total, feed_total, hidden_total, attend_total = sums
     return (

time: 324 us -> 320 us (0.988); the launches traced: 320 us -> 321 us
  waiting for transfers between devices: 15.9 us -> 2.09 us
  starting transfers between devices: 4.72 us -> 13.3 us
  Pallas kernels: 294 us -> 299 us
    ppermute x3 -> x5, waiting for transfers between devices: 15.9 us -> 2.09 us  [sent(): return lax.ppermute(value, 'seq', pairs)]
    pallas_call x2, Pallas kernels: 68.7 us -> 81.4 us  [feed_both(): pl.pallas_call(functools.partial(feed_kernel, steps, chunk, sub, has_part...]
    ppermute x3 -> x5, starting transfers between devices: 4.72 us -> 13.3 us  [sent(): return lax.ppermute(value, 'seq', pairs)]
    pallas_call x1, Pallas kernels: 30.6 us -> 22.1 us  [finished(): pl.pallas_call(finish_kernel, grid_spec=pltpu.PrefetchScalarGridSpec(num_...]
    pallas_call x1, Pallas kernels: 140 us -> 144 us  [summed_everywhere(): pl.pallas_call(sum_kernel, out_shape=[jax.ShapeDtypeStruct((n * PIECE, D)...]
  transfers between devices with their start and end apart: 3 -> 5, of which waited for: 1 -> 2; matrix products, arithmetic and copies ran while one was open for 0% -> 1% of each run, Pallas kernels for 15% -> 19%
where the time goes in v4:
time: 320 us; the launch traced here: 321 us
  Pallas kernels  299 us (93%)
  starting transfers between devices  13.3 us (4%)
  other arithmetic  3.28 us (1%)
    pallas_call x1, Pallas kernels, summed_everywhere(): pl.pallas_call(sum_kernel, out_shape=[jax.ShapeDtypeStruct((n * PIECE, D)...  144 us
    pallas_call x2, Pallas kernels, feed_both(): pl.pallas_call(functools.partial(feed_kernel, steps, chunk, sub, has_part...  81.4 us
    pallas_call x1, Pallas kernels, long_forward(): pl.pallas_call(long_kernel, in_specs=[anywhere] * 7 + [resident] + [anywh...  37.7 us
    pallas_call x1, Pallas kernels, finished(): pl.pallas_call(finish_kernel, grid_spec=pltpu.PrefetchScalarGridSpec(num_...  22.1 us
    pallas_call x1, Pallas kernels, pack_forward(): pl.pallas_call(pack_kernel, grid_spec=pltpu.PrefetchScalarGridSpec(num_sc...  13.7 us
    ppermute x5, starting transfers between devices, sent(): return lax.ppermute(value, 'seq', pairs)  13.3 us
  transfers between devices with their start and end apart: 5, of which 2 were waited for; matrix products, arithmetic and copies ran while one was open for 1% of the time, Pallas kernels for 19%

profile of v4, /device:TPU:9, one launch (start us, length us, event | category | flops | bytes accessed | tf_op | source)
XLA Modules:
  0.0 321.5 jit_solution(4401661384580158788)
XLA Ops:
  0.7 1.3 slice.9
  2.6 1.5 select_bitcast_fusion.refs_0_.refs_10_
  4.1 1.9 collective-permute-start.1
  6.0 3.4 %collective-permute-start = (bf16[512,768]{1,0:T(8,128)(2,1)S(1)}, bf16[512,768]{1,0:T(8,128)(2,1)}, u32[]{:S(2)}, u32[]{:S(2)}) collective-permute-start(bf16[512,768]{1,0:T(8,128)(2,1)S(1)} %select_bitcast_fusion.refs_0_.refs_10_), channel_id=1, source_target_pairs={{0,1},{1,2},{2,3},{4,5},{5,6},{6,7},{8,9},{9,10},{10,11},{12,13},{... | collective-permute-start | bytes 2359304 | tf_op jit(solution)/shard_map/ppermute | solution.py:1443
  9.4 0.0 copy-done.2
  9.4 0.0 copy-done.3
  9.4 0.0 copy-done.4
  9.5 0.6 pad_add_fusion.slots
  10.0 0.6 broadcast_in_dim.3.gain_ref.refs_3_.refs_7_.refs_9_
  10.7 13.7 %shard_map.186 = (bf16[512,768]{1,0:T(8,128)(2,1)}, bf16[3,768,512]{2,1,0:T(8,128)(2,1)}, f32[768,512]{1,0:T(8,128)}, f32[96,512]{1,0:T(8,128)}, bf16[512,768]{1,0:T(8,128)(2,1)}) custom-call(s32[1]{0:T(128)} %bitcast.3.slot_ref.slot, bf16[2,512,768]{2,1,0:T(8,128)(2,1)} %refs_1_.3, bf16[768,2304]{1,0:T(8,128)(2,1)} %wq.1, ...), custom_call_target="tpu_custom_call" | custom-call | flops 8000000000 | bytes 10485760 | tf_op jit(solution)/shard_map/pallas_call | solution.py:446
  24.3 0.2 collective-permute-done.1.refs_2_
  24.5 1.9 collective-permute-done.refs_1_
  26.4 3.9 %collective-permute-start.2 = (bf16[512,768]{1,0:T(8,128)(2,1)}, bf16[512,768]{1,0:T(8,128)(2,1)}, u32[]{:S(2)}, u32[]{:S(2)}) collective-permute-start(bf16[512,768]{1,0:T(8,128)(2,1)} %collective-permute-done.refs_1_), channel_id=1, source_target_pairs={{1,2},{2,3},{5,6},{6,7},{9,10},{10,11},{13,14},{14,15},{17,18},{18... | collective-permute-start | bytes 2359304 | tf_op jit(solution)/shard_map/ppermute | solution.py:1443
  30.3 1.9 collective-permute-start.3
  32.3 1.2 broadcast_select_fusion
  33.5 2.2 collective-permute-start.4
  35.7 46.7 %shard_map.187 = (bf16[2,512,768]{2,1,0:T(8,128)(2,1)}, f32[768,512]{1,0:T(8,128)}, bf16[768,512]{1,0:T(8,128)(2,1)}, bf16[768,768]{1,0:T(8,128)(2,1)}, bf16[307...) custom-call(s32[1]{0:T(128)} %bitcast.3.slot_ref.slot, f32[768,512]{1,0:T(8,128)} %get-tuple-element.56.refs_0_.refs_9_, ...), custom_call_target="tpu_custom_call" | custom-call | flops 16307453952 | bytes 52428800 | tf_op jit(solution)/shard_map/pallas_call | solution.py:725
  82.4 0.0 collective-permute-done.4.refs_5_
  82.4 0.0 collective-permute-done.2.refs_3_
  82.4 0.0 collective-permute-done.3.refs_4_
  82.4 37.7 %shard_map.188 = (bf16[2048,768]{1,0:T(8,128)(2,1)}, bf16[3,192,2048]{2,1,0:T(8,128)(2,1)}, f32[192,2048]{1,0:T(8,128)}, f32[3,8,2048]{2,1,0:T(8,128)}, bf16[768...) custom-call(bf16[512,768]{1,0:T(8,128)(2,1)} %copy-done, ...), custom_call_target="tpu_custom_call" | custom-call | flops 20000000000 | bytes 41943040 | tf_op jit(solution)/shard_map/pallas_call | solution.py:922
  120.2 34.7 %shard_map.189 = (bf16[2,512,768]{2,1,0:T(8,128)(2,1)}, f32[768,512]{1,0:T(8,128)}, bf16[768,512]{1,0:T(8,128)(2,1)}, bf16[768,768]{1,0:T(8,128)(2,1)}, bf16[307...) custom-call(s32[1]{0:T(128)} %bitcast.1.slot, ...), custom_call_target="tpu_custom_call", output_to_operand_aliasing={{0}: (11, {})} | custom-call | flops 16307453952 | bytes 52428800 | tf_op jit(solution)/shard_map/pallas_call | solution.py:725
  154.9 144.3 %shard_map.190 = (bf16[9216,768]{1,0:T(8,128)(2,1)}, bf16[512,768]{1,0:T(8,128)(2,1)}, f32[8,3072]{1,0:T(8,128)}) custom-call(bf16[3072,768]{1,0:T(8,128)(2,1)} %get-tuple-element.73.refs_0_, bf16[3072,768]{1,0:T(8,128)(2,1)} %get-tuple-element.74.refs_1_, bf16[768,768]{1,0:T(8,128)(2,1)} %get-tuple-element.75.refs_2_, ...), custom_call_target="tpu_custom_call" | custom-call | bytes 452984832 | tf_op jit(solution)/shard_map/pallas_call | solution.py:1392
  299.2 22.1 %shard_map.191 = (f32[3072,768]{1,0:T(8,128)}, f32[768,3072]{1,0:T(8,128)}, f32[768,768]{1,0:T(8,128)}, f32[768,2304]{1,0:T(8,128)}, f32[768]{0:T(1024)}, /*inde...) custom-call(s32[2]{0:T(128)} %pad_add_fusion.slots, ...), custom_call_target="tpu_custom_call" | custom-call | flops 20000000 | bytes 48234496 | tf_op jit(solution)/shard_map/pallas_call | solution.py:1511
  (10 shorter events, 0.0 us)
Async XLA Ops:
  0.6 8.8 %copy-start.2 = (f32[3072]{0:T(1024)S(1)}, f32[3072]{0:T(1024)}, u32[]{:S(2)}) copy-start(f32[3072]{0:T(1024)} %param.21) | copy-start | bytes 36868
  0.7 8.8 %copy-start.3 = (f32[768]{0:T(1024)S(1)}, f32[768]{0:T(1024)}, u32[]{:S(2)}) copy-start(f32[768]{0:T(1024)} %param.20) | copy-start | bytes 9220
  0.7 8.8 %copy-start.4 = (f32[768]{0:T(1024)S(1)}, f32[768]{0:T(1024)}, u32[]{:S(2)}) copy-start(f32[768]{0:T(1024)} %param.19) | copy-start | bytes 9220
  0.7 8.8 %copy-start.5 = (f32[768]{0:T(1024)S(1)}, f32[768]{0:T(1024)}, u32[]{:S(2)}) copy-start(f32[768]{0:T(1024)} %param.18) | copy-start | bytes 9220
  4.1 20.3 %copy-start = (bf16[512,768]{1,0:T(8,128)(2,1)}, bf16[512,768]{1,0:T(8,128)(2,1)S(1)}, u32[]{:S(2)}) copy-start(bf16[512,768]{1,0:T(8,128)(2,1)S(1)} %select_bitcast_fusion.refs_0_.refs_10_) | copy-start | bytes 2359300
  4.1 20.4 %collective-permute-start.1 = (bf16[512,768]{1,0:T(8,128)(2,1)S(1)}, bf16[512,768]{1,0:T(8,128)(2,1)S(1)}, u32[]{:S(2)}, u32[]{:S(2)}) collective-permute-start(bf16[512,768]{1,0:T(8,128)(2,1)S(1)} %select_bitcast_fusion.refs_0_.refs_10_), channel_id=1, source_target_pairs={{1,0},{2,1},{3,2},{5,4},{6,5},{7,6},{9,8},{10,9},{11,10},{13,12},{... | collective-permute-start | bytes 2359304 | tf_op jit(solution)/shard_map/ppermute | solution.py:1443
  6.0 20.4 %collective-permute-start = (bf16[512,768]{1,0:T(8,128)(2,1)S(1)}, bf16[512,768]{1,0:T(8,128)(2,1)}, u32[]{:S(2)}, u32[]{:S(2)}) collective-permute-start(bf16[512,768]{1,0:T(8,128)(2,1)S(1)} %select_bitcast_fusion.refs_0_.refs_10_), channel_id=1, source_target_pairs={{0,1},{1,2},{2,3},{4,5},{5,6},{6,7},{8,9},{9,10},{10,11},{12,13},{... | collective-permute-start | bytes 2359304 | tf_op jit(solution)/shard_map/ppermute | solution.py:1443
  24.5 57.9 %copy-start.1 = (bf16[512,768]{1,0:T(8,128)(2,1)}, bf16[512,768]{1,0:T(8,128)(2,1)S(1)}, u32[]{:S(2)}) copy-start(bf16[512,768]{1,0:T(8,128)(2,1)S(1)} %collective-permute-done.1.refs_2_) | copy-start | bytes 2359300
  26.4 56.0 %collective-permute-start.2 = (bf16[512,768]{1,0:T(8,128)(2,1)}, bf16[512,768]{1,0:T(8,128)(2,1)}, u32[]{:S(2)}, u32[]{:S(2)}) collective-permute-start(bf16[512,768]{1,0:T(8,128)(2,1)} %collective-permute-done.refs_1_), channel_id=1, source_target_pairs={{1,2},{2,3},{5,6},{6,7},{9,10},{10,11},{13,14},{14,15},{17,18},{18... | collective-permute-start | bytes 2359304 | tf_op jit(solution)/shard_map/ppermute | solution.py:1443
  30.3 52.1 %collective-permute-start.3 = (bf16[512,768]{1,0:T(8,128)(2,1)S(1)}, bf16[512,768]{1,0:T(8,128)(2,1)}, u32[]{:S(2)}, u32[]{:S(2)}) collective-permute-start(bf16[512,768]{1,0:T(8,128)(2,1)S(1)} %collective-permute-done.1.refs_2_), channel_id=1, source_target_pairs={{1,0},{2,1},{5,4},{6,5},{9,8},{10,9},{13,12},{14,13},{17,16},{18,1... | collective-permute-start | bytes 2359304 | tf_op jit(solution)/shard_map/ppermute | solution.py:1443
  33.5 48.9 %collective-permute-start.4 = (bf16[512,768]{1,0:T(8,128)(2,1)S(1)}, bf16[512,768]{1,0:T(8,128)(2,1)}, u32[]{:S(2)}, u32[]{:S(2)}) collective-permute-start(bf16[512,768]{1,0:T(8,128)(2,1)S(1)} %broadcast_select_fusion), channel_id=1, source_target_pairs={{1,3},{2,0},{5,7},{6,4},{9,11},{10,8},{13,15},{14,12},{17,19},{18,... | collective-permute-start | bytes 2359304 | tf_op jit(solution)/shard_map/ppermute | solution.py:1443

commit v5 on v4

--- a/solution.py
+++ b/solution.py
@@ -354,6 +354,7 @@
 SEQ = 4
 BLOCK = 512
 SPLIT = BLOCK // 2
+TOGETHER = 2
 HEADS_OWN = HEADS // SEQ
 GROUP = HEADS_OWN * 3 * HEAD_DIM
 MESH = pl.DeviceIdType.MESH
@@ -428,13 +429,15 @@
                 columns = slice(part * D + k, part * D + k + 256)
                 qkv_ref[part, k : k + 256, :] = left_t(w_ref[:, columns], at[...]).astype(BF16)
 
-    rows = pl.ds(pl.multiple_of(h * HEAD_DIM, HEAD_DIM), HEAD_DIM)
-
-    def write(query_block, here, o, lse):
-        o_ref[...] = o
-        lse_ref[0:1, :] = lse
-
-    attend_head(lambda part, columns: qkv_ref[part, rows, :], write, 1)
+    for sub in range(TOGETHER):
+        start = (h * TOGETHER + sub) * HEAD_DIM
+        rows = pl.ds(pl.multiple_of(start, HEAD_DIM), HEAD_DIM)
+
+        def write(query_block, here, o, lse):
+            o_ref[sub * HEAD_DIM : (sub + 1) * HEAD_DIM, :] = o
+            lse_ref[8 * sub : 8 * sub + 1, :] = lse
+
+        attend_head(lambda part, columns: qkv_ref[part, rows, :], write, 1)
 
 
 def pack_forward(slot, tokens, weight, gain):
@@ -442,12 +445,12 @@
     once = lambda *shape: pl.BlockSpec(
         shape, lambda h, slot: (0,) * len(shape), pipeline_mode=pl.Buffered(1)
     )
-    by_head = lambda rows: pl.BlockSpec((rows, BLOCK), lambda h, slot: (h, 0))
+    by_head = lambda rows: pl.BlockSpec((TOGETHER * rows, BLOCK), lambda h, slot: (h, 0))
     return pl.pallas_call(
         pack_kernel,
         grid_spec=pltpu.PrefetchScalarGridSpec(
             num_scalar_prefetch=1,
-            grid=(HEADS,),
+            grid=(HEADS // TOGETHER,),
             in_specs=[
                 pl.BlockSpec((1, BLOCK, D), lambda h, slot: (slot[0], 0, 0)),
                 once(D, 3 * D),
@@ -857,7 +860,7 @@
     for load in loads:
         load.wait()
 
-    def back(h, carry):
+    def back_head(h):
         rows = pl.ds(pl.multiple_of(h * HEAD_DIM, HEAD_DIM), HEAD_DIM)
         queries_t = (qp[0, rows, :].astype(F32) * 0.125).astype(BF16)
         keys_t = qp[1, rows, :]
@@ -885,9 +888,13 @@
         dp[1, rows, late] = matmul(dcorner, queries[late]).T.astype(BF16)
         dp[2, rows, :SPLIT] = matmul(probs.astype(BF16), do_rows).T.astype(BF16)
         dp[2, rows, late] = matmul(corner.astype(BF16), do_rows[late]).T.astype(BF16)
+
+    def back(turn, carry):
+        for sub in range(TOGETHER):
+            back_head(turn * TOGETHER + sub)
         return carry
 
-    lax.fori_loop(0, HEADS, back, 0)
+    lax.fori_loop(0, HEADS // TOGETHER, back, 0)
     for part in range(3):
         gq[part * D : (part + 1) * D, :] = matmul(dp[part], ap[...]).astype(BF16)
     saves[4].start()

time: 320 us -> 312 us (0.975); the launches traced: 321 us -> 307 us
  Pallas kernels: 299 us -> 283 us
    pallas_call x2, Pallas kernels: 81.4 us -> 68.4 us  [feed_both(): pl.pallas_call(functools.partial(feed_kernel, steps, chunk, sub, has_part...]
  transfers between devices with their start and end apart: 5 -> 5, of which waited for: 2 -> 2; matrix products, arithmetic and copies ran while one was open for 1% -> 1% of each run, Pallas kernels for 19% -> 15%
where the time goes in v5:
time: 312 us; the launch traced here: 307 us
  Pallas kernels  283 us (91%)
  starting transfers between devices  13.3 us (4%)
  waiting for transfers between devices  4.02 us (1%)
  other arithmetic  3.28 us (1%)
    pallas_call x1, Pallas kernels, summed_everywhere(): pl.pallas_call(sum_kernel, out_shape=[jax.ShapeDtypeStruct((n * PIECE, D)...  144 us
    pallas_call x2, Pallas kernels, feed_both(): pl.pallas_call(functools.partial(feed_kernel, steps, chunk, sub, has_part...  68.4 us
    pallas_call x1, Pallas kernels, long_forward(): pl.pallas_call(long_kernel, in_specs=[anywhere] * 7 + [resident] + [anywh...  36.2 us
    pallas_call x1, Pallas kernels, finished(): pl.pallas_call(finish_kernel, grid_spec=pltpu.PrefetchScalarGridSpec(num_...  22.1 us
    ppermute x5, starting transfers between devices, sent(): return lax.ppermute(value, 'seq', pairs)  13.3 us
    pallas_call x1, Pallas kernels, pack_forward(): pl.pallas_call(pack_kernel, grid_spec=pltpu.PrefetchScalarGridSpec(num_sc...  11.7 us
  transfers between devices with their start and end apart: 5, of which 2 were waited for; matrix products, arithmetic and copies ran while one was open for 1% of the time, Pallas kernels for 15%

profile of v5, /device:TPU:9, one launch (start us, length us, event | category | flops | bytes accessed | tf_op | source)
XLA Modules:
  0.0 307.0 jit_solution(17755613558178418849)
XLA Ops:
  0.6 0.0 copy-start.2
  0.7 0.0 copy-start.3
  0.7 0.0 copy-start.4
  0.7 1.3 slice.9
  2.6 1.5 select_bitcast_fusion.refs_0_.refs_10_
  4.1 1.9 collective-permute-start.1
  6.0 3.4 %collective-permute-start = (bf16[512,768]{1,0:T(8,128)(2,1)S(1)}, bf16[512,768]{1,0:T(8,128)(2,1)}, u32[]{:S(2)}, u32[]{:S(2)}) collective-permute-start(bf16[512,768]{1,0:T(8,128)(2,1)S(1)} %select_bitcast_fusion.refs_0_.refs_10_), channel_id=1, source_target_pairs={{0,1},{1,2},{2,3},{4,5},{5,6},{6,7},{8,9},{9,10},{10,11},{12,13},{... | collective-permute-start | bytes 2359304 | tf_op jit(solution)/shard_map/ppermute | solution.py:1450
  9.5 0.6 pad_add_fusion.slots
  10.0 0.6 broadcast_in_dim.3.gain_ref.refs_3_.refs_7_.refs_9_
  10.7 11.7 %shard_map.186 = (bf16[512,768]{1,0:T(8,128)(2,1)}, bf16[3,768,512]{2,1,0:T(8,128)(2,1)}, f32[768,512]{1,0:T(8,128)}, f32[96,512]{1,0:T(8,128)}, bf16[512,768]{1,0:T(8,128)(2,1)}) custom-call(s32[1]{0:T(128)} %bitcast.3.slot_ref.slot, bf16[2,512,768]{2,1,0:T(8,128)(2,1)} %refs_1_.3, bf16[768,2304]{1,0:T(8,128)(2,1)} %wq.1, ...), custom_call_target="tpu_custom_call" | custom-call | flops 8000000000 | bytes 10485760 | tf_op jit(solution)/shard_map/pallas_call | solution.py:449
  22.4 2.1 collective-permute-done.1.refs_2_
  24.5 1.9 collective-permute-done.refs_1_
  26.4 3.9 %collective-permute-start.2 = (bf16[512,768]{1,0:T(8,128)(2,1)}, bf16[512,768]{1,0:T(8,128)(2,1)}, u32[]{:S(2)}, u32[]{:S(2)}) collective-permute-start(bf16[512,768]{1,0:T(8,128)(2,1)} %collective-permute-done.refs_1_), channel_id=1, source_target_pairs={{1,2},{2,3},{5,6},{6,7},{9,10},{10,11},{13,14},{14,15},{17,18},{18... | collective-permute-start | bytes 2359304 | tf_op jit(solution)/shard_map/ppermute | solution.py:1450
  30.3 1.9 collective-permute-start.3
  32.3 1.2 broadcast_select_fusion
  33.5 2.2 collective-permute-start.4
  35.7 33.7 %shard_map.187 = (bf16[2,512,768]{2,1,0:T(8,128)(2,1)}, f32[768,512]{1,0:T(8,128)}, bf16[768,512]{1,0:T(8,128)(2,1)}, bf16[768,768]{1,0:T(8,128)(2,1)}, bf16[307...) custom-call(s32[1]{0:T(128)} %bitcast.3.slot_ref.slot, f32[768,512]{1,0:T(8,128)} %get-tuple-element.56.refs_0_.refs_9_, ...), custom_call_target="tpu_custom_call" | custom-call | flops 16307453952 | bytes 52428800 | tf_op jit(solution)/shard_map/pallas_call | solution.py:728
  69.5 0.0 collective-permute-done.4.refs_5_
  69.5 0.0 collective-permute-done.2.refs_3_
  69.5 0.0 collective-permute-done.3.refs_4_
  69.5 36.2 %shard_map.188 = (bf16[2048,768]{1,0:T(8,128)(2,1)}, bf16[3,192,2048]{2,1,0:T(8,128)(2,1)}, f32[192,2048]{1,0:T(8,128)}, f32[3,8,2048]{2,1,0:T(8,128)}, bf16[768...) custom-call(bf16[512,768]{1,0:T(8,128)(2,1)} %copy-done, ...), custom_call_target="tpu_custom_call" | custom-call | flops 20000000000 | bytes 41943040 | tf_op jit(solution)/shard_map/pallas_call | solution.py:929
  105.7 34.7 %shard_map.189 = (bf16[2,512,768]{2,1,0:T(8,128)(2,1)}, f32[768,512]{1,0:T(8,128)}, bf16[768,512]{1,0:T(8,128)(2,1)}, bf16[768,768]{1,0:T(8,128)(2,1)}, bf16[307...) custom-call(s32[1]{0:T(128)} %bitcast.1.slot, ...), custom_call_target="tpu_custom_call", output_to_operand_aliasing={{0}: (11, {})} | custom-call | flops 16307453952 | bytes 52428800 | tf_op jit(solution)/shard_map/pallas_call | solution.py:728
  140.5 144.2 %shard_map.190 = (bf16[9216,768]{1,0:T(8,128)(2,1)}, bf16[512,768]{1,0:T(8,128)(2,1)}, f32[8,3072]{1,0:T(8,128)}) custom-call(bf16[3072,768]{1,0:T(8,128)(2,1)} %get-tuple-element.73.refs_0_, bf16[3072,768]{1,0:T(8,128)(2,1)} %get-tuple-element.74.refs_1_, bf16[768,768]{1,0:T(8,128)(2,1)} %get-tuple-element.75.refs_2_, ...), custom_call_target="tpu_custom_call" | custom-call | bytes 452984832 | tf_op jit(solution)/shard_map/pallas_call | solution.py:1399
  284.7 22.1 %shard_map.191 = (f32[3072,768]{1,0:T(8,128)}, f32[768,3072]{1,0:T(8,128)}, f32[768,768]{1,0:T(8,128)}, f32[768,2304]{1,0:T(8,128)}, f32[768]{0:T(1024)}, /*inde...) custom-call(s32[2]{0:T(128)} %pad_add_fusion.slots, ...), custom_call_target="tpu_custom_call" | custom-call | flops 20000000 | bytes 48234496 | tf_op jit(solution)/shard_map/pallas_call | solution.py:1518
  (10 shorter events, 0.0 us)
Async XLA Ops:
  0.6 8.8 %copy-start.2 = (f32[3072]{0:T(1024)S(1)}, f32[3072]{0:T(1024)}, u32[]{:S(2)}) copy-start(f32[3072]{0:T(1024)} %param.21) | copy-start | bytes 36868
  0.7 8.8 %copy-start.3 = (f32[768]{0:T(1024)S(1)}, f32[768]{0:T(1024)}, u32[]{:S(2)}) copy-start(f32[768]{0:T(1024)} %param.20) | copy-start | bytes 9220
  0.7 8.8 %copy-start.4 = (f32[768]{0:T(1024)S(1)}, f32[768]{0:T(1024)}, u32[]{:S(2)}) copy-start(f32[768]{0:T(1024)} %param.19) | copy-start | bytes 9220
  0.7 8.8 %copy-start.5 = (f32[768]{0:T(1024)S(1)}, f32[768]{0:T(1024)}, u32[]{:S(2)}) copy-start(f32[768]{0:T(1024)} %param.18) | copy-start | bytes 9220
  4.1 18.3 %copy-start = (bf16[512,768]{1,0:T(8,128)(2,1)}, bf16[512,768]{1,0:T(8,128)(2,1)S(1)}, u32[]{:S(2)}) copy-start(bf16[512,768]{1,0:T(8,128)(2,1)S(1)} %select_bitcast_fusion.refs_0_.refs_10_) | copy-start | bytes 2359300
  4.1 20.4 %collective-permute-start.1 = (bf16[512,768]{1,0:T(8,128)(2,1)S(1)}, bf16[512,768]{1,0:T(8,128)(2,1)S(1)}, u32[]{:S(2)}, u32[]{:S(2)}) collective-permute-start(bf16[512,768]{1,0:T(8,128)(2,1)S(1)} %select_bitcast_fusion.refs_0_.refs_10_), channel_id=1, source_target_pairs={{1,0},{2,1},{3,2},{5,4},{6,5},{7,6},{9,8},{10,9},{11,10},{13,12},{... | collective-permute-start | bytes 2359304 | tf_op jit(solution)/shard_map/ppermute | solution.py:1450
  6.0 20.4 %collective-permute-start = (bf16[512,768]{1,0:T(8,128)(2,1)S(1)}, bf16[512,768]{1,0:T(8,128)(2,1)}, u32[]{:S(2)}, u32[]{:S(2)}) collective-permute-start(bf16[512,768]{1,0:T(8,128)(2,1)S(1)} %select_bitcast_fusion.refs_0_.refs_10_), channel_id=1, source_target_pairs={{0,1},{1,2},{2,3},{4,5},{5,6},{6,7},{8,9},{9,10},{10,11},{12,13},{... | collective-permute-start | bytes 2359304 | tf_op jit(solution)/shard_map/ppermute | solution.py:1450
  24.5 45.0 %copy-start.1 = (bf16[512,768]{1,0:T(8,128)(2,1)}, bf16[512,768]{1,0:T(8,128)(2,1)S(1)}, u32[]{:S(2)}) copy-start(bf16[512,768]{1,0:T(8,128)(2,1)S(1)} %collective-permute-done.1.refs_2_) | copy-start | bytes 2359300
  26.4 43.0 %collective-permute-start.2 = (bf16[512,768]{1,0:T(8,128)(2,1)}, bf16[512,768]{1,0:T(8,128)(2,1)}, u32[]{:S(2)}, u32[]{:S(2)}) collective-permute-start(bf16[512,768]{1,0:T(8,128)(2,1)} %collective-permute-done.refs_1_), channel_id=1, source_target_pairs={{1,2},{2,3},{5,6},{6,7},{9,10},{10,11},{13,14},{14,15},{17,18},{18... | collective-permute-start | bytes 2359304 | tf_op jit(solution)/shard_map/ppermute | solution.py:1450
  30.3 39.1 %collective-permute-start.3 = (bf16[512,768]{1,0:T(8,128)(2,1)S(1)}, bf16[512,768]{1,0:T(8,128)(2,1)}, u32[]{:S(2)}, u32[]{:S(2)}) collective-permute-start(bf16[512,768]{1,0:T(8,128)(2,1)S(1)} %collective-permute-done.1.refs_2_), channel_id=1, source_target_pairs={{1,0},{2,1},{5,4},{6,5},{9,8},{10,9},{13,12},{14,13},{17,16},{18,1... | collective-permute-start | bytes 2359304 | tf_op jit(solution)/shard_map/ppermute | solution.py:1450
  33.5 36.0 %collective-permute-start.4 = (bf16[512,768]{1,0:T(8,128)(2,1)S(1)}, bf16[512,768]{1,0:T(8,128)(2,1)}, u32[]{:S(2)}, u32[]{:S(2)}) collective-permute-start(bf16[512,768]{1,0:T(8,128)(2,1)S(1)} %broadcast_select_fusion), channel_id=1, source_target_pairs={{1,3},{2,0},{5,7},{6,4},{9,11},{10,8},{13,15},{14,12},{17,19},{18,... | collective-permute-start | bytes 2359304 | tf_op jit(solution)/shard_map/ppermute | solution.py:1450

commit v6 on v5

--- a/solution.py
+++ b/solution.py
@@ -1276,17 +1276,34 @@
         lse = lse_own[h, 0:1, here]
         delta = jnp.sum(do_t.astype(F32) * o_own[rows, here], axis=0, keepdims=True)
         dq = jnp.zeros((HEAD_DIM, BLOCK), F32)
-        for key_block in range(query_block + 1):
+        for key_block in range(query_block):
             there = slice(key_block * BLOCK, (key_block + 1) * BLOCK)
             keys_t = qkv[1, rows, there]
             probs = jnp.exp(matmul(keys_t.T, queries_t) - lse)
-            if key_block == query_block:
-                probs = jnp.where(causal_mask(0, BLOCK, BLOCK), probs, 0.0)
             dprobs = matmul(qkv[2, rows, there].T, do_t)
             dlogits = (probs * (dprobs - delta)).astype(BF16)
             dq = dq + matmul(keys_t, dlogits)
             dv_acc[there, :] += matmul(probs.astype(BF16), do_rows)
             dk_acc[there, :] += matmul(dlogits, queries)
+        early = slice(query_block * BLOCK, query_block * BLOCK + SPLIT)
+        late = slice(query_block * BLOCK + SPLIT, (query_block + 1) * BLOCK)
+        keys_t = qkv[1, rows, here]
+        keys = keys_t.T
+        values = qkv[2, rows, here].T
+        probs = jnp.exp(matmul(keys[:SPLIT], queries_t) - lse)
+        probs = jnp.where(causal_mask(0, SPLIT, BLOCK), probs, 0.0)
+        dlogits = (probs * (matmul(values[:SPLIT], do_t) - delta)).astype(BF16)
+        corner = jnp.exp(matmul(keys[SPLIT:], queries_t[:, SPLIT:]) - lse[:, SPLIT:])
+        corner = jnp.where(causal_mask(0, SPLIT, SPLIT), corner, 0.0)
+        dcorner = matmul(values[SPLIT:], do_t[:, SPLIT:]) - delta[:, SPLIT:]
+        dcorner = (corner * dcorner).astype(BF16)
+        dq = dq + matmul(keys_t[:, :SPLIT], dlogits)
+        dq_late = dq[:, SPLIT:] + matmul(keys_t[:, SPLIT:], dcorner)
+        dq = jnp.concatenate([dq[:, :SPLIT], dq_late], axis=1)
+        dv_acc[early, :] += matmul(probs.astype(BF16), do_rows)
+        dk_acc[early, :] += matmul(dlogits, queries)
+        dv_acc[late, :] += matmul(corner.astype(BF16), do_rows[SPLIT:])
+        dk_acc[late, :] += matmul(dcorner, queries[SPLIT:])
         d_own[query_block, 0, rows, :] = (dq * 0.125).astype(BF16)
 
     def finish_head(h):

time: 312 us -> 311 us (level)
  no operation moved by 1% of the time
where the time goes in v6:
time: 311 us; the launch traced here: 306 us
  Pallas kernels  282 us (91%)
  starting transfers between devices  13.3 us (4%)
  waiting for transfers between devices  4.02 us (1%)
  other arithmetic  3.28 us (1%)
    pallas_call x1, Pallas kernels, summed_everywhere(): pl.pallas_call(sum_kernel, out_shape=[jax.ShapeDtypeStruct((n * PIECE, D)...  143 us
    pallas_call x2, Pallas kernels, feed_both(): pl.pallas_call(functools.partial(feed_kernel, steps, chunk, sub, has_part...  68.4 us
    pallas_call x1, Pallas kernels, long_forward(): pl.pallas_call(long_kernel, in_specs=[anywhere] * 7 + [resident] + [anywh...  36.2 us
    pallas_call x1, Pallas kernels, finished(): pl.pallas_call(finish_kernel, grid_spec=pltpu.PrefetchScalarGridSpec(num_...  22.1 us
    ppermute x5, starting transfers between devices, sent(): return lax.ppermute(value, 'seq', pairs)  13.3 us
    pallas_call x1, Pallas kernels, pack_forward(): pl.pallas_call(pack_kernel, grid_spec=pltpu.PrefetchScalarGridSpec(num_sc...  11.7 us
  transfers between devices with their start and end apart: 5, of which 2 were waited for; matrix products, arithmetic and copies ran while one was open for 1% of the time, Pallas kernels for 15%

profile of v6, /device:TPU:9, one launch (start us, length us, event | category | flops | bytes accessed | tf_op | source)
XLA Modules:
  0.0 306.3 jit_solution(15159379679944558556)
XLA Ops:
  0.6 0.0 copy-start.2
  0.7 0.0 copy-start.3
  0.7 0.0 copy-start.4
  0.7 1.3 slice.9
  2.6 1.5 select_bitcast_fusion.refs_0_.refs_10_
  4.1 1.9 collective-permute-start.1
  6.0 3.4 %collective-permute-start = (bf16[512,768]{1,0:T(8,128)(2,1)S(1)}, bf16[512,768]{1,0:T(8,128)(2,1)}, u32[]{:S(2)}, u32[]{:S(2)}) collective-permute-start(bf16[512,768]{1,0:T(8,128)(2,1)S(1)} %select_bitcast_fusion.refs_0_.refs_10_), channel_id=1, source_target_pairs={{0,1},{1,2},{2,3},{4,5},{5,6},{6,7},{8,9},{9,10},{10,11},{12,13},{... | collective-permute-start | bytes 2359304 | tf_op jit(solution)/shard_map/ppermute | solution.py:1467
  9.5 0.6 pad_add_fusion.slots
  10.0 0.6 broadcast_in_dim.3.gain_ref.refs_3_.refs_7_.refs_9_
  10.7 11.7 %shard_map.186 = (bf16[512,768]{1,0:T(8,128)(2,1)}, bf16[3,768,512]{2,1,0:T(8,128)(2,1)}, f32[768,512]{1,0:T(8,128)}, f32[96,512]{1,0:T(8,128)}, bf16[512,768]{1,0:T(8,128)(2,1)}) custom-call(s32[1]{0:T(128)} %bitcast.3.slot_ref.slot, bf16[2,512,768]{2,1,0:T(8,128)(2,1)} %refs_1_.3, bf16[768,2304]{1,0:T(8,128)(2,1)} %wq.1, ...), custom_call_target="tpu_custom_call" | custom-call | flops 8000000000 | bytes 10485760 | tf_op jit(solution)/shard_map/pallas_call | solution.py:449
  22.4 2.1 collective-permute-done.1.refs_2_
  24.5 1.9 collective-permute-done.refs_1_
  26.4 3.9 %collective-permute-start.2 = (bf16[512,768]{1,0:T(8,128)(2,1)}, bf16[512,768]{1,0:T(8,128)(2,1)}, u32[]{:S(2)}, u32[]{:S(2)}) collective-permute-start(bf16[512,768]{1,0:T(8,128)(2,1)} %collective-permute-done.refs_1_), channel_id=1, source_target_pairs={{1,2},{2,3},{5,6},{6,7},{9,10},{10,11},{13,14},{14,15},{17,18},{18... | collective-permute-start | bytes 2359304 | tf_op jit(solution)/shard_map/ppermute | solution.py:1467
  30.3 1.9 collective-permute-start.3
  32.3 1.2 broadcast_select_fusion
  33.5 2.2 collective-permute-start.4
  35.7 33.7 %shard_map.187 = (bf16[2,512,768]{2,1,0:T(8,128)(2,1)}, f32[768,512]{1,0:T(8,128)}, bf16[768,512]{1,0:T(8,128)(2,1)}, bf16[768,768]{1,0:T(8,128)(2,1)}, bf16[307...) custom-call(s32[1]{0:T(128)} %bitcast.3.slot_ref.slot, f32[768,512]{1,0:T(8,128)} %get-tuple-element.56.refs_0_.refs_9_, ...), custom_call_target="tpu_custom_call" | custom-call | flops 16307453952 | bytes 52428800 | tf_op jit(solution)/shard_map/pallas_call | solution.py:728
  69.5 0.0 collective-permute-done.4.refs_5_
  69.5 0.0 collective-permute-done.2.refs_3_
  69.5 0.0 collective-permute-done.3.refs_4_
  69.5 36.2 %shard_map.188 = (bf16[2048,768]{1,0:T(8,128)(2,1)}, bf16[3,192,2048]{2,1,0:T(8,128)(2,1)}, f32[192,2048]{1,0:T(8,128)}, f32[3,8,2048]{2,1,0:T(8,128)}, bf16[768...) custom-call(bf16[512,768]{1,0:T(8,128)(2,1)} %copy-done, ...), custom_call_target="tpu_custom_call" | custom-call | flops 20000000000 | bytes 41943040 | tf_op jit(solution)/shard_map/pallas_call | solution.py:929
  105.7 34.7 %shard_map.189 = (bf16[2,512,768]{2,1,0:T(8,128)(2,1)}, f32[768,512]{1,0:T(8,128)}, bf16[768,512]{1,0:T(8,128)(2,1)}, bf16[768,768]{1,0:T(8,128)(2,1)}, bf16[307...) custom-call(s32[1]{0:T(128)} %bitcast.1.slot, ...), custom_call_target="tpu_custom_call", output_to_operand_aliasing={{0}: (11, {})} | custom-call | flops 16307453952 | bytes 52428800 | tf_op jit(solution)/shard_map/pallas_call | solution.py:728
  140.5 143.5 %shard_map.190 = (bf16[9216,768]{1,0:T(8,128)(2,1)}, bf16[512,768]{1,0:T(8,128)(2,1)}, f32[8,3072]{1,0:T(8,128)}) custom-call(bf16[3072,768]{1,0:T(8,128)(2,1)} %get-tuple-element.73.refs_0_, bf16[3072,768]{1,0:T(8,128)(2,1)} %get-tuple-element.74.refs_1_, bf16[768,768]{1,0:T(8,128)(2,1)} %get-tuple-element.75.refs_2_, ...), custom_call_target="tpu_custom_call" | custom-call | bytes 452984832 | tf_op jit(solution)/shard_map/pallas_call | solution.py:1416
  283.9 22.1 %shard_map.191 = (f32[3072,768]{1,0:T(8,128)}, f32[768,3072]{1,0:T(8,128)}, f32[768,768]{1,0:T(8,128)}, f32[768,2304]{1,0:T(8,128)}, f32[768]{0:T(1024)}, /*inde...) custom-call(s32[2]{0:T(128)} %pad_add_fusion.slots, ...), custom_call_target="tpu_custom_call" | custom-call | flops 20000000 | bytes 48234496 | tf_op jit(solution)/shard_map/pallas_call | solution.py:1535
  (10 shorter events, 0.0 us)
Async XLA Ops:
  0.6 8.8 %copy-start.2 = (f32[3072]{0:T(1024)S(1)}, f32[3072]{0:T(1024)}, u32[]{:S(2)}) copy-start(f32[3072]{0:T(1024)} %param.21) | copy-start | bytes 36868
  0.7 8.8 %copy-start.3 = (f32[768]{0:T(1024)S(1)}, f32[768]{0:T(1024)}, u32[]{:S(2)}) copy-start(f32[768]{0:T(1024)} %param.20) | copy-start | bytes 9220
  0.7 8.8 %copy-start.4 = (f32[768]{0:T(1024)S(1)}, f32[768]{0:T(1024)}, u32[]{:S(2)}) copy-start(f32[768]{0:T(1024)} %param.19) | copy-start | bytes 9220
  0.7 8.8 %copy-start.5 = (f32[768]{0:T(1024)S(1)}, f32[768]{0:T(1024)}, u32[]{:S(2)}) copy-start(f32[768]{0:T(1024)} %param.18) | copy-start | bytes 9220
  4.1 18.3 %copy-start = (bf16[512,768]{1,0:T(8,128)(2,1)}, bf16[512,768]{1,0:T(8,128)(2,1)S(1)}, u32[]{:S(2)}) copy-start(bf16[512,768]{1,0:T(8,128)(2,1)S(1)} %select_bitcast_fusion.refs_0_.refs_10_) | copy-start | bytes 2359300
  4.1 20.4 %collective-permute-start.1 = (bf16[512,768]{1,0:T(8,128)(2,1)S(1)}, bf16[512,768]{1,0:T(8,128)(2,1)S(1)}, u32[]{:S(2)}, u32[]{:S(2)}) collective-permute-start(bf16[512,768]{1,0:T(8,128)(2,1)S(1)} %select_bitcast_fusion.refs_0_.refs_10_), channel_id=1, source_target_pairs={{1,0},{2,1},{3,2},{5,4},{6,5},{7,6},{9,8},{10,9},{11,10},{13,12},{... | collective-permute-start | bytes 2359304 | tf_op jit(solution)/shard_map/ppermute | solution.py:1467
  6.0 20.4 %collective-permute-start = (bf16[512,768]{1,0:T(8,128)(2,1)S(1)}, bf16[512,768]{1,0:T(8,128)(2,1)}, u32[]{:S(2)}, u32[]{:S(2)}) collective-permute-start(bf16[512,768]{1,0:T(8,128)(2,1)S(1)} %select_bitcast_fusion.refs_0_.refs_10_), channel_id=1, source_target_pairs={{0,1},{1,2},{2,3},{4,5},{5,6},{6,7},{8,9},{9,10},{10,11},{12,13},{... | collective-permute-start | bytes 2359304 | tf_op jit(solution)/shard_map/ppermute | solution.py:1467
  24.5 45.0 %copy-start.1 = (bf16[512,768]{1,0:T(8,128)(2,1)}, bf16[512,768]{1,0:T(8,128)(2,1)S(1)}, u32[]{:S(2)}) copy-start(bf16[512,768]{1,0:T(8,128)(2,1)S(1)} %collective-permute-done.1.refs_2_) | copy-start | bytes 2359300
  26.4 43.0 %collective-permute-start.2 = (bf16[512,768]{1,0:T(8,128)(2,1)}, bf16[512,768]{1,0:T(8,128)(2,1)}, u32[]{:S(2)}, u32[]{:S(2)}) collective-permute-start(bf16[512,768]{1,0:T(8,128)(2,1)} %collective-permute-done.refs_1_), channel_id=1, source_target_pairs={{1,2},{2,3},{5,6},{6,7},{9,10},{10,11},{13,14},{14,15},{17,18},{18... | collective-permute-start | bytes 2359304 | tf_op jit(solution)/shard_map/ppermute | solution.py:1467
  30.3 39.1 %collective-permute-start.3 = (bf16[512,768]{1,0:T(8,128)(2,1)S(1)}, bf16[512,768]{1,0:T(8,128)(2,1)}, u32[]{:S(2)}, u32[]{:S(2)}) collective-permute-start(bf16[512,768]{1,0:T(8,128)(2,1)S(1)} %collective-permute-done.1.refs_2_), channel_id=1, source_target_pairs={{1,0},{2,1},{5,4},{6,5},{9,8},{10,9},{13,12},{14,13},{17,16},{18,1... | collective-permute-start | bytes 2359304 | tf_op jit(solution)/shard_map/ppermute | solution.py:1467
  33.5 36.0 %collective-permute-start.4 = (bf16[512,768]{1,0:T(8,128)(2,1)S(1)}, bf16[512,768]{1,0:T(8,128)(2,1)}, u32[]{:S(2)}, u32[]{:S(2)}) collective-permute-start(bf16[512,768]{1,0:T(8,128)(2,1)S(1)} %broadcast_select_fusion), channel_id=1, source_target_pairs={{1,3},{2,0},{5,7},{6,4},{9,11},{10,8},{13,15},{14,12},{17,19},{18,... | collective-permute-start | bytes 2359304 | tf_op jit(solution)/shard_map/ppermute | solution.py:1467
